TPU v7x, 512 devices: a whole 4x4x16 slice. The times are simulated.
512 devices in a mesh: row: 16 (over x_lo, y, core), col: 32 (over x_hi, z).
Axes of the slice: x: 4 (x_hi: 2, x_lo: 2; x = x_hi * 2 + x_lo), y: 4, z: 16, core: 2. Of those that a mesh axis runs over, the one named last changes fastest.
Arguments:
- eigvecs: bfloat16 [65536, 4096], P('row', 'col'), may hold values from -6 to 6
- reflectors: bfloat16 [65536, 8192], P('row', 'col'), may hold values from -0.0234375 to 0.0234375
- factors: float32 [2, 256, 256], replicated, as said below
- owners: int32 [32], replicated, may hold values from 0 to 31, each once
Outputs:
- result: bfloat16 [65536, 4096], P('row', 'col')
Inputs may be any that keep to these rules, and one draw needn't show every extreme that they name: `factors`: each panel's factor is upper triangular. `owners` is a permutation of 0..31: panel p is stored in slot owners[p] for p < 2, and entries owners[2:] are not used.
All inputs are finite; a program needn't handle non-finite values.
Results may differ from a plain program's by a relative error of at most 0.0034.
Values may be sent and summed in bfloat16 or wider, within the bound.
No kernel may reach another device: no remote copies, remote signals or barrier semaphores. Data moves between devices by JAX's collectives and lax.ppermute only.
A program may use at most 64 MiB of HBM per device.

v0:
```python
import jax
import jax.numpy as jnp
from jax import lax
from jax.sharding import PartitionSpec as P


def from_root(block, axis, owner):
    block = jnp.where(lax.axis_index(axis) == owner, block, jnp.zeros_like(block))
    return lax.psum(block, axis)


def project(left, right):
    return lax.dot_general(
        left, right, (((0,), (0,)), ((), ())), preferred_element_type=jnp.float32
    )


def reduce_block(wlist, glist):
    count = len(wlist)
    summed = lax.psum(tuple(wlist) + tuple(glist), "row")
    return (list(summed[:count]), list(summed[count:]))


def finish(wsum, gsums, factor, coeffs):
    acc = wsum
    for q in range(len(gsums)):
        acc = acc - jnp.dot(
            gsums[q], coeffs[q].astype(jnp.float32), precision=lax.Precision.HIGHEST
        )
    return jnp.dot(factor, acc, precision=lax.Precision.HIGHEST).astype(jnp.bfloat16)


def per_device(eigvecs, reflectors, factors, owners):
    count = factors.shape[0]
    stored = []
    coeffs = []
    for p in range(count):
        panel = from_root(reflectors, "col", owners[p])
        wpart = project(panel, eigvecs)
        gparts = [project(panel, other) for other in stored]
        wsum, gsums = reduce_block([wpart], gparts)
        coeffs.append(finish(wsum[0], gsums, factors[p], coeffs))
        stored.append(panel)
    total = eigvecs.astype(jnp.float32)
    for p in range(count):
        total = total - jnp.dot(stored[p], coeffs[p], preferred_element_type=jnp.float32)
    return total.astype(jnp.bfloat16)


def solution(mesh):
    placed = (P("row", "col"), P("row", "col"), P(), P())
    return jax.shard_map(
        per_device, mesh=mesh, in_specs=placed, out_specs=P("row", "col"), check_vma=False
    )
```

profile of v0, /device:TPU:1, one launch (start us, length us, event | category | flops | bytes accessed | tf_op | source)
XLA Modules:
  0.0 477.3 jit_solution(1804652246866622704)
XLA Ops:
  6.5 0.0 all-reduce.7.cloned.1.call-start
  6.5 1.3 fusion.5
  9.1 3.8 broadcast_select_fusion
  12.9 0.0 copy-start.1
  12.9 0.0 all-reduce.7.cloned.1.call-update
  12.9 0.0 all-reduce.5.cloned.1.call-start
  13.0 300.0 %all-reduce.7.cloned.1.call-done = (bf16[4096,256]{1,0:T(8,128)(2,1)}, bf16[4096,256]{1,0:T(8,128)(2,1)}) async-done(((bf16[4096,256]{1,0:T(8,128)(2,1)}, bf16[4096,256]{1,0:T(8,128)(2,1)}), (bf16[4096,256]{1,0:T(8,128)(2,1)}, bf16[4096,256]{1,0:T(8,128)(2,1)})) %all-reduce.7.cloned.1.call-update) | async-done | bytes 4194320 | tf_op jit(solution)/shard_map/psum | solution.py:9
  313.0 0.0 copy-start.2
  313.0 0.0 copy-done.1
  313.0 3.1 fusion.6
  316.2 0.0 copy-start
  316.2 0.0 copy-done.2
  316.2 1.4 fusion.7
  317.6 0.2 copy-done
  317.7 1.4 fusion.8
  319.2 0.0 all-reduce.5.cloned.1.call-update
  319.2 146.2 %all-reduce.5.cloned.1.call-done = (f32[256,128]{1,0:T(8,128)}, f32[256,128]{1,0:T(8,128)}, f32[256,256]{1,0:T(8,128)}) async-done(((f32[256,128]{1,0:T(8,128)}, f32[256,128]{1,0:T(8,128)}, f32[256,256]{1,0:T(8,128)}), (f32[256,128]{1,0:T(8,128)}, f32[256,128]{1,0:T(8,128)}, f32[256,256]{1,0:T(8,128)})) %all-reduce.5.cloned.1.call-update) | async-done | bytes 524304 | tf_op jit(solution)/shard_map/psum | solution.py:20
  465.4 1.4 convolution_convert_fusion.1
  466.9 0.0 copy-start.5
  466.9 0.0 copy-start.6
  466.9 0.0 copy-start.4
  466.9 0.0 copy-start.3
  466.9 0.7 convolution_subtract_fusion.1
  467.6 0.2 copy-done.5
  467.8 0.0 copy-done.6
  467.9 0.3 convolution_subtract_fusion.2
  468.2 0.0 copy-done.4
  468.2 0.4 convolution_convert_fusion
  468.6 0.2 copy-done.3
  468.8 1.7 fusion
Async XLA Ops:
  6.5 306.5 %all-reduce.7.cloned.1.call-start = ((), (), s32[]{:S(2)}) async-start(), calls=%async_computation.1 | async-start | bytes 8388608 | tf_op jit(solution)/shard_map/psum | solution.py:9
  12.9 300.1 %copy-start.1 = (bf16[4096,128]{1,0:T(8,128)(2,1)S(1)}, bf16[4096,128]{1,0:T(8,128)(2,1)}, u32[]{:S(2)}) copy-start(bf16[4096,128]{1,0:T(8,128)(2,1)} %param.4) | copy-start | bytes 3145732
  12.9 452.5 %all-reduce.5.cloned.1.call-start = ((), (), s32[]{:S(2)}) async-start(), calls=%async_computation | async-start | bytes 1048576 | tf_op jit(solution)/shard_map/psum | solution.py:20
  313.0 3.1 copy-start.2
  316.2 1.6 copy-start
  466.9 1.0 copy-start.5
  466.9 1.0 copy-start.6
  466.9 1.2 copy-start.4
  466.9 1.9 copy-start.3
Sparse Core Ops, SparseCore 0:
  13.1 299.9 all-reduce.6
  319.3 146.0 all-reduce.4
where the time goes:
time: 478 us; the launch traced here: 477 us
  waiting for transfers between devices  446 us (93%)
  between operations  14.7 us (3%)
  matrix products  10.5 us (2%)
    psum x1, waiting for transfers between devices, from_root(): return lax.psum(block, axis)  300 us
    psum x1, waiting for transfers between devices, reduce_block(): summed = lax.psum(tuple(wlist) + tuple(glist), 'row')  146 us
  transfers between devices with their start and end apart: 2, of which 2 were waited for; matrix products, arithmetic and copies ran while one was open for 0% of the time, Pallas kernels for 0%

commit v1 on v0

v1 whole, which is shorter than its diff:
```python
import jax
import jax.numpy as jnp
from jax import lax
from jax.sharding import PartitionSpec as P

RING = 16
HALVES = 2
RINGS = [[half * RING + z for z in range(RING)] for half in range(HALVES)]
ACROSS = [(c, (c + RING) % (HALVES * RING)) for c in range(HALVES * RING)]


def shards(reflectors, owners):
    rows, width = reflectors.shape
    here = lax.axis_index("col") // RING
    sent = lax.all_to_all(
        reflectors.reshape(RING, rows // RING, width), "col", 0, 0, axis_index_groups=RINGS
    )
    mine = [lax.dynamic_index_in_dim(sent, owners[p] % RING, 0, False) for p in range(2)]
    theirs = lax.ppermute(jnp.stack(mine), "col", ACROSS)
    return jnp.concatenate(
        [jnp.where(owners[p] // RING == here, mine[p], theirs[p]) for p in range(2)], axis=1
    )


def contract(left, right, dims):
    return lax.dot_general(left, right, (dims, ((), ())), preferred_element_type=jnp.float32)


def sum_over_rows(part):
    count = lax.axis_size("row")
    cut = part.reshape((count, part.shape[0] // count) + part.shape[1:])
    share = jnp.sum(lax.all_to_all(cut, "row", 0, 0), axis=0)
    spread = jnp.broadcast_to(share[None], (count,) + share.shape)
    return lax.all_to_all(spread, "row", 0, 0).reshape(part.shape)


def exact(left, right):
    return lax.dot_general(
        left, right, (((1,), (1,)), ((), ())), precision=lax.Precision.HIGHEST,
        preferred_element_type=jnp.float32,
    )


def per_device(eigvecs, reflectors, factors, owners):
    width = reflectors.shape[1]
    columns = eigvecs.shape[1]
    panels = lax.all_gather(
        shards(reflectors, owners), "col", tiled=True, axis_index_groups=RINGS
    )
    proj = contract(eigvecs, panels, ((0,), (0,)))
    cross = contract(panels[:, width:], panels[:, :width], ((0,), (0,)))
    packed = jnp.concatenate([proj[:, :width], proj[:, width:], cross], axis=0)
    summed = sum_over_rows(packed)
    first, second = summed[:columns], summed[columns : 2 * columns]
    cross = summed[2 * columns :]
    lead = exact(first, factors[0]).astype(jnp.bfloat16)
    rest = second - exact(lead.astype(jnp.float32), cross)
    tail = exact(rest, factors[1]).astype(jnp.bfloat16)
    coeffs = jnp.concatenate([lead, tail], axis=1)
    update = contract(panels, coeffs, ((1,), (1,)))
    return (eigvecs.astype(jnp.float32) - update).astype(jnp.bfloat16)


def solution(mesh):
    placed = (P("row", "col"), P("row", "col"), P(), P())
    return jax.shard_map(
        per_device, mesh=mesh, in_specs=placed, out_specs=P("row", "col"), check_vma=False
    )
```

time: 478 us -> 252 us (0.53)
  waiting for transfers between devices: 446 us -> 164 us
  blocking collectives: 0 us -> 38 us
  starting transfers between devices: 0.04 us -> 20.6 us
    psum x2 -> x0, waiting for transfers between devices: 446 us -> none  [the longest x1 300 us: from_root(): return lax.psum(block, axis)]
    all_to_all x0 -> x1, waiting for transfers between devices: none -> 87.3 us  [shards(): lax.all_to_all(reflectors.reshape(RING, rows // RING, width), 'col', 0, 0...]
    all_gather x0 -> x1, waiting for transfers between devices: none -> 73.6 us  [per_device(): lax.all_gather(shards(reflectors, owners), 'col', tiled=True, axis_index_...]
    all_to_all x0 -> x2, blocking collectives: none -> 38 us  [the longest x1 24.5 us: sum_over_rows(): share = jnp.sum(lax.all_to_all(cut, 'row', 0, 0), axis=0)]
    all_to_all x0 -> x1, starting transfers between devices: none -> 15.9 us  [shards(): lax.all_to_all(reflectors.reshape(RING, rows // RING, width), 'col', 0, 0...]
    dot_general x8 -> x6, matrix products: 10.5 us -> 9.38 us  [the longest x3 8.28 us: contract(): lax.dot_general(left, right, (dims, ((), ())), preferred_element_type=jnp...]
  transfers between devices with their start and end apart: 2 -> 3, of which waited for: 2 -> 3; matrix products, arithmetic and copies ran while one was open for 0% -> 0% of each run, Pallas kernels for 0% -> 0%
where the time goes in v1:
time: 252 us
  waiting for transfers between devices  164 us (65%)
  blocking collectives  38 us (15%)
  starting transfers between devices  20.6 us (8%)
  between operations  18.7 us (7%)
  matrix products  9.38 us (4%)
    all_to_all x1, waiting for transfers between devices, shards(): lax.all_to_all(reflectors.reshape(RING, rows // RING, width), 'col', 0, 0...  87.3 us
    all_gather x1, waiting for transfers between devices, per_device(): lax.all_gather(shards(reflectors, owners), 'col', tiled=True, axis_index_...  73.6 us
    all_to_all x1, blocking collectives, sum_over_rows(): share = jnp.sum(lax.all_to_all(cut, 'row', 0, 0), axis=0)  24.5 us
    all_to_all x1, starting transfers between devices, shards(): lax.all_to_all(reflectors.reshape(RING, rows // RING, width), 'col', 0, 0...  15.9 us
    all_to_all x1, blocking collectives, sum_over_rows(): return lax.all_to_all(spread, 'row', 0, 0).reshape(part.shape)  13.5 us
    dot_general x3, matrix products, contract(): lax.dot_general(left, right, (dims, ((), ())), preferred_element_type=jnp...  8.28 us
  transfers between devices with their start and end apart: 3, of which 3 were waited for; matrix products, arithmetic and copies ran while one was open for 0% of the time, Pallas kernels for 0%

profile of v1, /device:TPU:1, one launch (start us, length us, event | category | flops | bytes accessed | tf_op | source)
XLA Modules:
  0.0 252.1 jit_solution(18215345077934941937)
XLA Ops:
  6.5 0.0 copy-start.3
  6.5 0.0 copy-start.1
  6.5 15.9 %all-to-all-start = ((bf16[16,256,256]{2,1,0:T(8,128)(2,1)}), bf16[16,256,256]{2,1,0:T(8,128)(2,1)S(1)}, u32[]{:S(2)}, u32[]{:S(2)}) async-start(bf16[16,256,256]{2,1,0:T(8,128)(2,1)} %bitcast.26), calls=%async_computation | async-start | bytes 4194304 | tf_op jit(solution)/shard_map/all_to_all | solution.py:15
  22.4 0.0 all-gather.2.cloned.1.call-start
  22.5 0.0 copy-done.3
  22.5 0.6 fusion.16
  27.0 87.3 %all-to-all-done = bf16[16,256,256]{2,1,0:T(8,128)(2,1)S(1)} async-done(((bf16[16,256,256]{2,1,0:T(8,128)(2,1)}), bf16[16,256,256]{2,1,0:T(8,128)(2,1)S(1)}, u32[]{:S(2)}, u32[]{:S(2)}) %all-to-all-start) | async-done | bytes 2097184 | tf_op jit(solution)/shard_map/all_to_all | solution.py:15
  114.3 4.7 %collective-permute-start = (bf16[2,256,256]{2,1,0:T(8,128)(2,1)S(1)}, bf16[2,256,256]{2,1,0:T(8,128)(2,1)S(1)}, u32[]{:S(2)}, u32[]{:S(2)}) collective-permute-start(bf16[2,256,256]{2,1,0:T(8,128)(2,1)S(1)} %pad_maximum_fusion.1), channel_id=1, source_target_pairs={{0,16},{1,17},{2,18},{3,19},{4,20},{5,21},{6,22},{7,23},{8,24},{9,... | collective-permute-start | bytes 786440 | tf_op jit(solution)/shard_map/ppermute | solution.py:19
  120.3 2.6 %collective-permute-done = bf16[2,256,256]{2,1,0:T(8,128)(2,1)S(1)} collective-permute-done((bf16[2,256,256]{2,1,0:T(8,128)(2,1)S(1)}, bf16[2,256,256]{2,1,0:T(8,128)(2,1)S(1)}, u32[]{:S(2)}, u32[]{:S(2)}) %collective-permute-start) | collective-permute-done | bytes 262176 | tf_op jit(solution)/shard_map/ppermute | solution.py:19
  123.0 0.7 pad_maximum_fusion.2
  123.7 0.0 all-gather.2.cloned.1.call-update
  123.7 73.6 %all-gather.2.cloned.1.call-done = bf16[4096,512]{1,0:T(8,128)(2,1)} async-done(((bf16[256,512]{1,0:T(8,128)(2,1)}), bf16[4096,512]{1,0:T(8,128)(2,1)}) %all-gather.2.cloned.1.call-update) | async-done | bytes 4194320 | tf_op jit(solution)/shard_map/all_gather | solution.py:47
  197.3 0.0 copy-done.1
  197.3 0.0 copy-start
  197.3 3.1 %convolution_bitcast_fusion = f32[128,512]{1,0:T(8,128)S(1)} fusion(bf16[4096,512]{1,0:T(8,128)(2,1)} %all-gather.2.cloned.1.call-done, bf16[4096,128]{1,0:T(8,128)(2,1)S(1)} %copy-done.1), kind=kOutput, calls=%fused_computation.5 | convolution fusion | flops 536870912 | bytes 5505024 | tf_op jit(solution)/shard_map/dot_general | solution.py:26
  200.5 0.3 copy-done
  200.8 0.7 fusion.1
  201.5 0.0 copy-start.2
  201.6 24.5 %all_to_all.15 = f32[16,32,256]{2,1,0:T(8,128)S(1)} all-to-all(f32[16,32,256]{2,1,0:T(8,128)S(1)} %bitcast.27), channel_id=1, replica_groups=mesh['row'=16,'col'=32] {'row'}, dimensions={0} | all-to-all | bytes 1048576 | tf_op jit(solution)/shard_map/all_to_all | solution.py:32
  226.2 13.5 %all_to_all.16 = f32[16,32,256]{2,1,0:T(8,128)S(1)} all-to-all(f32[16,32,256]{2,1,0:T(8,128)S(1)} %broadcast_in_dim.2), channel_id=1, replica_groups=mesh['row'=16,'col'=32] {'row'}, dimensions={0} | all-to-all | bytes 1048576 | tf_op jit(solution)/shard_map/all_to_all | solution.py:34
  239.7 0.0 copy-done.2
  239.7 0.4 convolution_convert_fusion.1
  240.1 0.3 convolution_subtract_fusion.1
  240.4 0.4 convolution_convert_fusion
  240.8 4.4 %fusion = bf16[4096,128]{1,0:T(8,128)(2,1)} fusion(bf16[4096,512]{1,0:T(8,128)(2,1)} %all-gather.2.cloned.1.call-done, bf16[4096,128]{1,0:T(8,128)(2,1)S(1)} %copy-done.1, bf16[128,256]{1,0:T(8,128)(2,1)S(1)} %convolution_convert_fusion, bf16[128,256]{1,0:T(8,128)(2,1)S(1)} %convolution_convert_fusion.1), kind=kOutput, calls=%fused_computation.1 | convolution fusion | flops 538705920 | bytes 6422528 | tf_op jit(solution)/shard_map/dot_general | solution.py:26
  (9 shorter events, 0.2 us)
Async XLA Ops:
  6.5 15.9 %copy-start.3 = (s32[32]{0:T(128)S(1)}, s32[32]{0:T(128)}, u32[]{:S(2)}) copy-start(s32[32]{0:T(128)} %param.7) | copy-start | bytes 388
  6.5 190.8 %copy-start.1 = (bf16[4096,128]{1,0:T(8,128)(2,1)S(1)}, bf16[4096,128]{1,0:T(8,128)(2,1)}, u32[]{:S(2)}) copy-start(bf16[4096,128]{1,0:T(8,128)(2,1)} %param.4) | copy-start | bytes 3145732
  6.5 107.7 %all-to-all-start = ((bf16[16,256,256]{2,1,0:T(8,128)(2,1)}), bf16[16,256,256]{2,1,0:T(8,128)(2,1)S(1)}, u32[]{:S(2)}, u32[]{:S(2)}) async-start(bf16[16,256,256]{2,1,0:T(8,128)(2,1)} %bitcast.26), calls=%async_computation | async-start | bytes 4194304 | tf_op jit(solution)/shard_map/all_to_all | solution.py:15
  22.4 174.9 %all-gather.2.cloned.1.call-start = ((), (), s32[]{:S(2)}) async-start(), calls=%async_computation.3 | async-start | bytes 4456448 | tf_op jit(solution)/shard_map/all_gather | solution.py:47
  114.3 8.6 %collective-permute-start = (bf16[2,256,256]{2,1,0:T(8,128)(2,1)S(1)}, bf16[2,256,256]{2,1,0:T(8,128)(2,1)S(1)}, u32[]{:S(2)}, u32[]{:S(2)}) collective-permute-start(bf16[2,256,256]{2,1,0:T(8,128)(2,1)S(1)} %pad_maximum_fusion.1), channel_id=1, source_target_pairs={{0,16},{1,17},{2,18},{3,19},{4,20},{5,21},{6,22},{7,23},{8,24},{9,... | collective-permute-start | bytes 786440 | tf_op jit(solution)/shard_map/ppermute | solution.py:19
  197.3 3.4 %copy-start = (bf16[4096,512]{1,0:T(8,128)(2,1)S(1)}, bf16[4096,512]{1,0:T(8,128)(2,1)}, u32[]{:S(2)}) copy-start(bf16[4096,512]{1,0:T(8,128)(2,1)} %all-gather.2.cloned.1.call-done) | copy-start | bytes 12582916
  201.5 38.1 %copy-start.2 = (f32[2,256,256]{2,1,0:T(8,128)S(1)}, f32[2,256,256]{2,1,0:T(8,128)}, u32[]{:S(2)}) copy-start(f32[2,256,256]{2,1,0:T(8,128)} %param.6) | copy-start | bytes 1572868
Sparse Core Ops, SparseCore 0:
  123.8 73.4 all-gather.1

commit v2 on v1

v2 whole, which is shorter than its diff:
```python
import jax
import jax.numpy as jnp
from jax import lax
from jax.sharding import PartitionSpec as P

RING = 16
HALVES = 2
RINGS = [[half * RING + z for z in range(RING)] for half in range(HALVES)]
PAIRS = [[z, z + RING] for z in range(RING)]
SCALE = 2.0**21


def gather_panels(reflectors, owners):
    z = lax.axis_index("col") % RING
    block = (reflectors.astype(jnp.float32) * SCALE).astype(jnp.float16)
    both = lax.all_gather(block, "col", axis_index_groups=PAIRS)
    sent = []
    for p in range(2):
        tile = lax.dynamic_index_in_dim(both, owners[p] // RING, 0, False)
        sent.append(jnp.where(owners[p] % RING == z, tile, jnp.zeros_like(tile)))
    whole = lax.psum(jnp.concatenate(sent, axis=1), "col", axis_index_groups=RINGS)
    return whole.astype(jnp.bfloat16)


def contract(left, right, dims):
    return lax.dot_general(left, right, (dims, ((), ())), preferred_element_type=jnp.float32)


def sum_over_rows(part):
    count = lax.axis_size("row")
    cut = part.reshape((count, part.shape[0] // count) + part.shape[1:])
    share = jnp.sum(lax.all_to_all(cut, "row", 0, 0), axis=0)
    spread = jnp.broadcast_to(share[None], (count,) + share.shape)
    return lax.all_to_all(spread, "row", 0, 0).reshape(part.shape)


def exact(left, right):
    return lax.dot_general(
        left, right, (((1,), (1,)), ((), ())), precision=lax.Precision.HIGHEST,
        preferred_element_type=jnp.float32,
    )


def per_device(eigvecs, reflectors, factors, owners):
    width = reflectors.shape[1]
    columns = eigvecs.shape[1]
    panels = gather_panels(reflectors, owners)
    proj = contract(eigvecs, panels, ((0,), (0,)))
    cross = contract(panels[:, width:], panels[:, :width], ((0,), (0,)))
    packed = jnp.concatenate([proj[:, :width], proj[:, width:], cross], axis=0)
    summed = sum_over_rows(packed)
    first = summed[:columns] * (1 / SCALE)
    second = summed[columns : 2 * columns] * (1 / SCALE)
    cross = summed[2 * columns :] * (1 / SCALE**2)
    lead = exact(first, factors[0]).astype(jnp.bfloat16)
    rest = second - exact(lead.astype(jnp.float32), cross)
    tail = exact(rest, factors[1]).astype(jnp.bfloat16)
    coeffs = jnp.concatenate([lead, tail], axis=1)
    update = contract(panels, coeffs, ((1,), (1,)))
    return (eigvecs.astype(jnp.float32) - update * (1 / SCALE)).astype(jnp.bfloat16)


def solution(mesh):
    placed = (P("row", "col"), P("row", "col"), P(), P())
    return jax.shard_map(
        per_device, mesh=mesh, in_specs=placed, out_specs=P("row", "col"), check_vma=False
    )
```

time: 252 us -> 211 us (0.84)
  waiting for transfers between devices: 164 us -> 0 us
  blocking collectives: 38 us -> 184 us
  starting transfers between devices: 20.6 us -> 0 us
  between operations: 18.7 us -> 5.53 us
  other arithmetic: 0.85 us -> 11.2 us
    psum x0 -> x1, blocking collectives: none -> 104 us  [gather_panels(): lax.psum(jnp.concatenate(sent, axis=1), 'col', axis_index_groups=RINGS)]
    all_to_all x1 -> x0, waiting for transfers between devices: 87.3 us -> none  [shards(): lax.all_to_all(reflectors.reshape(RING, rows // RING, width), 'col', 0, 0...]
    all_gather x1 -> x0, waiting for transfers between devices: 73.6 us -> none  [per_device(): lax.all_gather(shards(reflectors, owners), 'col', tiled=True, axis_index_...]
    all_gather x0 -> x1, blocking collectives: none -> 46.2 us  [gather_panels(): both = lax.all_gather(block, 'col', axis_index_groups=PAIRS)]
    all_to_all x1 -> x0, starting transfers between devices: 15.9 us -> none  [shards(): lax.all_to_all(reflectors.reshape(RING, rows // RING, width), 'col', 0, 0...]
    convert_element_type x0 -> x2, other arithmetic: none -> 4.96 us  [the longest x1 2.86 us: gather_panels(): return whole.astype(jnp.bfloat16)]
    all_to_all x1, blocking collectives: 24.5 us -> 19.7 us  [sum_over_rows(): share = jnp.sum(lax.all_to_all(cut, 'row', 0, 0), axis=0)]
    ppermute x1 -> x0, starting transfers between devices: 4.65 us -> none  [shards(): theirs = lax.ppermute(jnp.stack(mine), 'col', ACROSS)]
  transfers between devices with their start and end apart: 3 -> 0, of which waited for: 3 -> 0; matrix products, arithmetic and copies ran while one was open for 0% -> 0% of each run, Pallas kernels for 0% -> 0%
where the time goes in v2:
time: 211 us
  blocking collectives  184 us (87%)
  other arithmetic  11.2 us (5%)
  matrix products  7.12 us (3%)
  between operations  5.53 us (3%)
  local copies, waits for them, and re-layouts  3.18 us (2%)
    psum x1, blocking collectives, gather_panels(): lax.psum(jnp.concatenate(sent, axis=1), 'col', axis_index_groups=RINGS)  104 us
    all_gather x1, blocking collectives, gather_panels(): both = lax.all_gather(block, 'col', axis_index_groups=PAIRS)  46.2 us
    all_to_all x1, blocking collectives, sum_over_rows(): share = jnp.sum(lax.all_to_all(cut, 'row', 0, 0), axis=0)  19.7 us
    all_to_all x1, blocking collectives, sum_over_rows(): return lax.all_to_all(spread, 'row', 0, 0).reshape(part.shape)  13.5 us
    dot_general x3, matrix products, contract(): lax.dot_general(left, right, (dims, ((), ())), preferred_element_type=jnp...  6.03 us

profile of v2, /device:TPU:1, one launch (start us, length us, event | category | flops | bytes accessed | tf_op | source)
XLA Modules:
  0.0 210.8 jit_solution(243454694891082118)
XLA Ops:
  0.0 1.4 fusion.16
  6.8 2.1 multiply_convert_fusion
  8.9 46.2 %all-gather.2 = f16[8192,256]{1,0:T(8,128)(2,1)} all-gather(f16[4096,256]{1,0:T(8,128)(2,1)S(1)} %multiply_convert_fusion), channel_id=2, replica_groups={{0,16},{1,17},{2,18},{3,19},{4,20},{5,21},{6,22},{7,23},{8,24},{9,25},{..., dimensions={0}, use_global_device_ids=true | all-gather | bytes 6291456 | tf_op jit(solution)/shard_map/all_gather | solution.py:16
  55.1 3.3 %select_bitcast_fusion.1 = (f16[4096,256]{1,0:T(8,128)(2,1)S(1)}, f16[4096,256]{1,0:T(8,128)(2,1)S(1)}) fusion(f16[2,4096,256]{2,1,0:T(8,128)(2,1)} %bitcast.29, s32[]{:T(128)S(6)} %select_n.53, pred[]{:T(512)S(6)} %eq.10, s32[]{:T(128)S(6)} %select_n.59, pred[]{:T(512)S(6)} %eq.11), kind=kLoop, calls=%fused_computation.9 | loop fusion | flops 2097152 | bytes 8388618 | tf_op jit(solution)/shard_map/jit(_where)/select_n | solution.py:20
  58.4 2.9 %pad_maximum_fusion = f16[4096,512]{1,0:T(8,128)(2,1)} fusion(f16[4096,256]{1,0:T(8,128)(2,1)S(1)} %get-tuple-element.6, f16[4096,256]{1,0:T(8,128)(2,1)S(1)} %get-tuple-element.5), kind=kLoop, calls=%fused_computation.3 | loop fusion | flops 2097152 | bytes 8388608 | tf_op jit(solution)/shard_map/concatenate | solution.py:21
  61.3 104.4 %all-reduce.1 = u32[4,262144]{1,0:T(4,128)} all-reduce(u32[4,262144]{1,0:T(4,128)} %bitcast.30), channel_id=1, replica_groups={{0,1,2,3,4,5,6,7,8,9,10,11,12,13,14,15},{16,17,18,19,20,21,22,23,24,25,..., use_global_device_ids=true, to_apply=%region_0.1.clone | all-reduce | flops 1048576 | bytes 8388608 | tf_op jit(solution)/shard_map/psum | solution.py:21
  165.6 2.9 %convert_element_type.25 = bf16[4096,512]{1,0:T(8,128)(2,1)S(1)} convert(f16[4096,512]{1,0:T(8,128)(2,1)} %bitcast.26) | non-fusion elementwise | flops 2097152 | bytes 8388608 | tf_op jit(solution)/shard_map/convert_element_type | solution.py:22
  168.5 0.0 copy-start
  168.5 0.0 copy-start.1
  168.5 0.7 fusion.2
  169.3 1.4 copy-done
  170.7 0.3 copy-done.1
  171.0 0.9 convolution_bitcast_fusion
  171.9 0.0 copy-start.2
  172.0 19.7 %all_to_all.10 = f32[16,32,256]{2,1,0:T(8,128)S(1)} all-to-all(f32[16,32,256]{2,1,0:T(8,128)S(1)} %bitcast.31), channel_id=1, replica_groups=mesh['row'=16,'col'=32] {'row'}, dimensions={0} | all-to-all | bytes 1048576 | tf_op jit(solution)/shard_map/all_to_all | solution.py:32
  191.7 13.5 %all_to_all.11 = f32[16,32,256]{2,1,0:T(8,128)S(1)} all-to-all(f32[16,32,256]{2,1,0:T(8,128)S(1)} %broadcast_in_dim.2), channel_id=1, replica_groups=mesh['row'=16,'col'=32] {'row'}, dimensions={0} | all-to-all | bytes 1048576 | tf_op jit(solution)/shard_map/all_to_all | solution.py:34
  205.2 0.0 copy-done.2
  205.2 0.4 convolution_convert_fusion.1
  205.7 0.3 convolution_subtract_fusion
  206.0 0.4 convolution_convert_fusion
  206.4 4.4 %fusion.1 = bf16[4096,128]{1,0:T(8,128)(2,1)} fusion(bf16[4096,128]{1,0:T(8,128)(2,1)S(1)} %copy-done.1, bf16[128,256]{1,0:T(8,128)(2,1)S(1)} %convolution_convert_fusion, bf16[128,256]{1,0:T(8,128)(2,1)S(1)} %convolution_convert_fusion.1, f16[4096,512]{1,0:T(8,128)(2,1)} %bitcast.27), kind=kOutput, calls=%fused_computation.2 | convolution fusion | flops 541327360 | bytes 6422528 | tf_op jit(solution)/shard_map/dot_general | solution.py:26
  (6 shorter events, 0.2 us)
Async XLA Ops:
  168.5 2.2 %copy-start = (u32[4,262144]{1,0:T(4,128)S(1)}, u32[4,262144]{1,0:T(4,128)}, u32[]{:S(2)}) copy-start(u32[4,262144]{1,0:T(4,128)} %all-reduce.1) | copy-start | bytes 12582916
  168.5 2.5 %copy-start.1 = (bf16[4096,128]{1,0:T(8,128)(2,1)S(1)}, bf16[4096,128]{1,0:T(8,128)(2,1)}, u32[]{:S(2)}) copy-start(bf16[4096,128]{1,0:T(8,128)(2,1)} %param.4) | copy-start | bytes 3145732
  171.9 33.3 %copy-start.2 = (f32[2,256,256]{2,1,0:T(8,128)S(1)}, f32[2,256,256]{2,1,0:T(8,128)}, u32[]{:S(2)}) copy-start(f32[2,256,256]{2,1,0:T(8,128)} %param.6) | copy-start | bytes 1572868

commit v3 on v2

v3 whole, which is shorter than its diff:
```python
import jax
import jax.numpy as jnp
from jax import lax
from jax.sharding import Mesh, PartitionSpec as P

RING = 16
HALVES = 2
SUMMED = ("row", "half")
SCALE = 2.0**21


def gather_panels(reflectors, owners):
    z = lax.axis_index("z")
    rows, width = reflectors.shape
    block = (reflectors.astype(jnp.float32) * SCALE).astype(jnp.float16)
    both = lax.all_to_all(block.reshape(HALVES, rows // HALVES, width), "half", 0, 0)
    sent = []
    for p in range(2):
        tile = lax.dynamic_index_in_dim(both, owners[p] // RING, 0, False)
        sent.append(jnp.where(owners[p] % RING == z, tile, jnp.zeros_like(tile)))
    whole = lax.psum(jnp.concatenate(sent, axis=1), "z")
    return whole.astype(jnp.bfloat16)


def contract(left, right, dims):
    return lax.dot_general(left, right, (dims, ((), ())), preferred_element_type=jnp.float32)


def sum_over(part, axes):
    count = lax.axis_size(axes)
    cut = part.reshape((count, part.shape[0] // count) + part.shape[1:])
    share = jnp.sum(lax.all_to_all(cut, axes, 0, 0), axis=0)
    spread = jnp.broadcast_to(share[None], (count,) + share.shape)
    return lax.all_to_all(spread, axes, 0, 0).reshape(part.shape)


def exact(left, right):
    return lax.dot_general(
        left, right, (((1,), (1,)), ((), ())), precision=lax.Precision.HIGHEST,
        preferred_element_type=jnp.float32,
    )


def swap(block):
    return lax.ppermute(block, "half", [(0, 1), (1, 0)])


def per_device(eigvecs, reflectors, factors, owners):
    rows, columns = eigvecs.shape
    width = reflectors.shape[1]
    half = lax.axis_index("half")
    tiles = eigvecs.reshape(HALVES, rows // HALVES, columns)
    mine = lax.dynamic_index_in_dim(tiles, half, 0, False)
    theirs = swap(lax.dynamic_index_in_dim(tiles, 1 - half, 0, False))
    panels = gather_panels(reflectors, owners)

    def projected(tile):
        return contract(tile, panels, ((0,), (0,)))

    here, there = projected(mine), projected(theirs)
    cross = contract(panels[:, width:], panels[:, :width], ((0,), (0,)))
    lower = jnp.where(half == 0, here, there)
    upper = jnp.where(half == 0, there, here)
    packed = jnp.concatenate(
        [lower[:, :width], upper[:, :width], lower[:, width:], upper[:, width:], cross], axis=0
    )
    summed = sum_over(packed, SUMMED)
    count = HALVES * columns
    first = summed[:count] * (1 / SCALE)
    second = summed[count : 2 * count] * (1 / SCALE)
    cross = summed[2 * count :] * (1 / SCALE**2)
    lead = exact(first, factors[0]).astype(jnp.bfloat16)
    rest = second - exact(lead.astype(jnp.float32), cross)
    tail = exact(rest, factors[1]).astype(jnp.bfloat16)
    coeffs = jnp.concatenate([lead, tail], axis=1).reshape(HALVES, columns, 2 * width)

    def updated(tile, which):
        part = lax.dynamic_index_in_dim(coeffs, which, 0, False)
        update = contract(panels, part, ((1,), (1,)))
        return (tile.astype(jnp.float32) - update * (1 / SCALE)).astype(jnp.bfloat16)

    got = swap(updated(theirs, 1 - half))
    kept = updated(mine, half)
    first_rows = jnp.where(half == 0, kept, got)
    last_rows = jnp.where(half == 0, got, kept)
    return jnp.concatenate([first_rows, last_rows], axis=0)


def solution(mesh):
    fine = Mesh(mesh.devices.reshape(-1, HALVES, RING), ("row", "half", "z"))
    tiled = P("row", ("half", "z"))
    return jax.shard_map(
        per_device, mesh=fine, in_specs=(tiled, tiled, P(), P()), out_specs=tiled, check_vma=False
    )
```

time: 211 us -> 184 us (0.87)
  blocking collectives: 184 us -> 127 us
  waiting for transfers between devices: 0 us -> 22.1 us
  starting transfers between devices: 0 us -> 12.3 us
  other arithmetic: 11.2 us -> 8.14 us
    all_gather x1 -> x0, blocking collectives: 46.2 us -> none  [gather_panels(): both = lax.all_gather(block, 'col', axis_index_groups=PAIRS)]
    psum x1, blocking collectives: 104 us -> 75 us  [gather_panels(): whole = lax.psum(jnp.concatenate(sent, axis=1), 'z')]
    all_to_all x2, blocking collectives: 33.1 us -> 51.7 us  [the longest x1 33.7 us: sum_over(): share = jnp.sum(lax.all_to_all(cut, axes, 0, 0), axis=0)]
    ppermute x0 -> x2, waiting for transfers between devices: none -> 13 us  [swap(): return lax.ppermute(block, 'half', [(0, 1), (1, 0)])]
    all_to_all x0 -> x1, waiting for transfers between devices: none -> 9.14 us  [gather_panels(): lax.all_to_all(block.reshape(HALVES, rows // HALVES, width), 'half', 0, 0)]
    ppermute x0 -> x2, starting transfers between devices: none -> 7.29 us  [swap(): return lax.ppermute(block, 'half', [(0, 1), (1, 0)])]
    all_to_all x0 -> x1, starting transfers between devices: none -> 4.97 us  [gather_panels(): lax.all_to_all(block.reshape(HALVES, rows // HALVES, width), 'half', 0, 0)]
    select_n x1, other arithmetic: 3.29 us -> 0.53 us  [gather_panels(): sent.append(jnp.where(owners[p] % RING == z, tile, jnp.zeros_like(tile)))]
  transfers between devices with their start and end apart: 0 -> 3, of which waited for: 0 -> 2; matrix products, arithmetic and copies ran while one was open for 0% -> 3% of each run, Pallas kernels for 0% -> 0%
where the time goes in v3:
time: 184 us; the launch traced here: 183 us
  blocking collectives  127 us (69%)
  waiting for transfers between devices  22.1 us (12%)
  starting transfers between devices  12.3 us (7%)
  other arithmetic  8.14 us (4%)
  matrix products  6.11 us (3%)
  between operations  5.25 us (3%)
  local copies, waits for them, and re-layouts  2.68 us (1%)
    psum x1, blocking collectives, gather_panels(): whole = lax.psum(jnp.concatenate(sent, axis=1), 'z')  75 us
    all_to_all x1, blocking collectives, sum_over(): share = jnp.sum(lax.all_to_all(cut, axes, 0, 0), axis=0)  33.7 us
    all_to_all x1, blocking collectives, sum_over(): return lax.all_to_all(spread, axes, 0, 0).reshape(part.shape)  18 us
    ppermute x2, waiting for transfers between devices, swap(): return lax.ppermute(block, 'half', [(0, 1), (1, 0)])  13 us
    all_to_all x1, waiting for transfers between devices, gather_panels(): lax.all_to_all(block.reshape(HALVES, rows // HALVES, width), 'half', 0, 0)  9.14 us
    ppermute x2, starting transfers between devices, swap(): return lax.ppermute(block, 'half', [(0, 1), (1, 0)])  7.29 us
    all_to_all x1, starting transfers between devices, gather_panels(): lax.all_to_all(block.reshape(HALVES, rows // HALVES, width), 'half', 0, 0)  4.97 us
    dot_general x5, matrix products, contract(): lax.dot_general(left, right, (dims, ((), ())), preferred_element_type=jnp...  4.96 us
  transfers between devices with their start and end apart: 3, of which 2 were waited for; matrix products, arithmetic and copies ran while one was open for 3% of the time, Pallas kernels for 0%

profile of v3, /device:TPU:1, one launch (start us, length us, event | category | flops | bytes accessed | tf_op | source)
XLA Modules:
  0.0 183.2 jit_solution(11816817635296613770)
XLA Ops:
  0.0 3.5 %multiply_convert_fusion = f16[4096,256]{1,0:T(8,128)(2,1)} fusion(bf16[4096,256]{1,0:T(8,128)(2,1)} %param.5), kind=kLoop, calls=%fused_computation | loop fusion | flops 3145728 | bytes 4194304 | tf_op jit(solution)/shard_map/convert_element_type | solution.py:15
  3.5 0.0 copy-start
  3.5 0.0 copy-start.3
  3.5 5.0 %all-to-all-start = ((f16[2,2048,256]{2,1,0:T(8,128)(2,1)}), f16[2,2048,256]{2,1,0:T(8,128)(2,1)S(1)}, u32[]{:S(2)}, u32[]{:S(2)}) async-start(f16[2,2048,256]{2,1,0:T(8,128)(2,1)} %bitcast.39), calls=%async_computation | async-start | bytes 4194304 | tf_op jit(solution)/shard_map/all_to_all | solution.py:16
  8.4 0.0 copy-done
  8.4 0.8 dynamic-slice_bitcast_fusion
  9.3 4.9 %collective-permute-start = (bf16[2048,128]{1,0:T(8,128)(2,1)}, bf16[2048,128]{1,0:T(8,128)(2,1)}, u32[]{:S(2)}, u32[]{:S(2)}) collective-permute-start(bf16[2048,128]{1,0:T(8,128)(2,1)} %dynamic-slice_bitcast_fusion), channel_id=1, source_target_pairs={{0,16},{16,0},{1,17},{17,1},{2,18},{18,2},{3,19},{19,3},{4,20},{20... | collective-permute-start | bytes 1572872 | tf_op jit(solution)/shard_map/ppermute | solution.py:45
  14.1 0.0 copy-done.3
  14.2 0.6 fusion.27
  19.9 9.1 %all-to-all-done = f16[2,2048,256]{2,1,0:T(8,128)(2,1)S(1)} async-done(((f16[2,2048,256]{2,1,0:T(8,128)(2,1)}), f16[2,2048,256]{2,1,0:T(8,128)(2,1)S(1)}, u32[]{:S(2)}, u32[]{:S(2)}) %all-to-all-start) | async-done | bytes 2097184 | tf_op jit(solution)/shard_map/all_to_all | solution.py:16
  29.0 0.5 select_bitcast_fusion.1
  29.5 1.9 %pad_maximum_fusion = f16[2048,512]{1,0:T(8,128)(2,1)} fusion(f16[2048,256]{1,0:T(8,128)(2,1)S(1)} %get-tuple-element.6, f16[2048,256]{1,0:T(8,128)(2,1)S(1)} %get-tuple-element.5), kind=kLoop, calls=%fused_computation.5 | loop fusion | flops 1048576 | bytes 4194304 | tf_op jit(solution)/shard_map/concatenate | solution.py:21
  31.5 75.0 %all-reduce.1 = u32[4,131072]{1,0:T(4,128)S(1)} all-reduce(u32[4,131072]{1,0:T(4,128)} %bitcast.40), channel_id=1, replica_groups=mesh['row'=16,'half'=2,'z'=16] {'z'}, use_global_device_ids=true, to_apply=%region_0.1.clone | all-reduce | flops 524288 | bytes 4194304 | tf_op jit(solution)/shard_map/psum | solution.py:21
  106.5 0.3 convert_element_type.31
  106.8 0.5 fusion.4
  107.3 0.0 collective-permute-done
  107.3 1.5 broadcast_select_fusion.2
  108.9 0.5 convolution_dynamic-update-slice_fusion
  109.4 0.0 copy-start.2
  109.4 33.7 %all_to_all.15 = f32[32,24,256]{2,1,0:T(8,128)S(1)} all-to-all(f32[32,24,256]{2,1,0:T(8,128)S(1)} %bitcast.46), channel_id=1, replica_groups=mesh['row'=16,'half'=2,'z'=16] {'row','half'}, dimensions={0} | all-to-all | bytes 1572864 | tf_op jit(solution)/shard_map/all_to_all | solution.py:32
  143.1 0.1 reduce_sum.9
  143.2 0.1 broadcast_in_dim.2
  143.2 18.0 %all_to_all.16 = f32[32,24,256]{2,1,0:T(8,128)S(1)} all-to-all(f32[32,24,256]{2,1,0:T(8,128)S(1)} %broadcast_in_dim.2), channel_id=1, replica_groups=mesh['row'=16,'half'=2,'z'=16] {'row','half'}, dimensions={0} | all-to-all | bytes 1572864 | tf_op jit(solution)/shard_map/all_to_all | solution.py:34
  161.2 0.0 copy-done.2
  161.2 0.4 convolution_convert_fusion.1
  161.6 0.3 convolution_subtract_fusion
  162.0 0.4 convolution_convert_fusion
  162.4 0.0 copy-start.1
  162.4 0.7 pad_maximum_fusion.2
  163.1 1.1 copy.7
  164.2 1.8 subtract_convert_fusion
  166.0 2.4 %collective-permute-start.1 = (bf16[2048,128]{1,0:T(8,128)(2,1)S(1)}, bf16[2048,128]{1,0:T(8,128)(2,1)S(1)}, u32[]{:S(2)}, u32[]{:S(2)}) collective-permute-start(bf16[2048,128]{1,0:T(8,128)(2,1)S(1)} %subtract_convert_fusion), channel_id=1, source_target_pairs={{0,16},{16,0},{1,17},{17,1},{2,18},{18,2},{3,19},{19,3},{4,20},{20... | collective-permute-start | bytes 1572872 | tf_op jit(solution)/shard_map/ppermute | solution.py:45
  168.4 0.0 copy-done.1
  168.4 0.7 fusion.1
  169.1 13.0 %collective-permute-done.1 = bf16[2048,128]{1,0:T(8,128)(2,1)S(1)} collective-permute-done((bf16[2048,128]{1,0:T(8,128)(2,1)S(1)}, bf16[2048,128]{1,0:T(8,128)(2,1)S(1)}, u32[]{:S(2)}, u32[]{:S(2)}) %collective-permute-start.1) | collective-permute-done | bytes 524320 | tf_op jit(solution)/shard_map/ppermute | solution.py:45
  182.1 0.1 broadcast_select_fusion.1
  182.2 1.0 pad_maximum_fusion.1
  (4 shorter events, 0.0 us)
Async XLA Ops:
  3.5 5.0 %copy-start = (bf16[4096,128]{1,0:T(8,128)(2,1)S(1)}, bf16[4096,128]{1,0:T(8,128)(2,1)}, u32[]{:S(2)}) copy-start(bf16[4096,128]{1,0:T(8,128)(2,1)} %param.4) | copy-start | bytes 3145732
  3.5 10.7 %copy-start.3 = (s32[32]{0:T(128)S(1)}, s32[32]{0:T(128)}, u32[]{:S(2)}) copy-start(s32[32]{0:T(128)} %param.7) | copy-start | bytes 388
  3.5 25.5 %all-to-all-start = ((f16[2,2048,256]{2,1,0:T(8,128)(2,1)}), f16[2,2048,256]{2,1,0:T(8,128)(2,1)S(1)}, u32[]{:S(2)}, u32[]{:S(2)}) async-start(f16[2,2048,256]{2,1,0:T(8,128)(2,1)} %bitcast.39), calls=%async_computation | async-start | bytes 4194304 | tf_op jit(solution)/shard_map/all_to_all | solution.py:16
  9.3 98.1 %collective-permute-start = (bf16[2048,128]{1,0:T(8,128)(2,1)}, bf16[2048,128]{1,0:T(8,128)(2,1)}, u32[]{:S(2)}, u32[]{:S(2)}) collective-permute-start(bf16[2048,128]{1,0:T(8,128)(2,1)} %dynamic-slice_bitcast_fusion), channel_id=1, source_target_pairs={{0,16},{16,0},{1,17},{17,1},{2,18},{18,2},{3,19},{19,3},{4,20},{20... | collective-permute-start | bytes 1572872 | tf_op jit(solution)/shard_map/ppermute | solution.py:45
  109.4 51.8 %copy-start.2 = (f32[2,256,256]{2,1,0:T(8,128)S(1)}, f32[2,256,256]{2,1,0:T(8,128)}, u32[]{:S(2)}) copy-start(f32[2,256,256]{2,1,0:T(8,128)} %param.6) | copy-start | bytes 1572868
  162.4 6.0 %copy-start.1 = (bf16[4096,128]{1,0:T(8,128)(2,1)S(1)}, bf16[4096,128]{1,0:T(8,128)(2,1)}, u32[]{:S(2)}) copy-start(bf16[4096,128]{1,0:T(8,128)(2,1)} %param.4) | copy-start | bytes 3145732
  166.0 16.1 %collective-permute-start.1 = (bf16[2048,128]{1,0:T(8,128)(2,1)S(1)}, bf16[2048,128]{1,0:T(8,128)(2,1)S(1)}, u32[]{:S(2)}, u32[]{:S(2)}) collective-permute-start(bf16[2048,128]{1,0:T(8,128)(2,1)S(1)} %subtract_convert_fusion), channel_id=1, source_target_pairs={{0,16},{16,0},{1,17},{17,1},{2,18},{18,2},{3,19},{19,3},{4,20},{20... | collective-permute-start | bytes 1572872 | tf_op jit(solution)/shard_map/ppermute | solution.py:45

commit v4 on v3

v4 whole, which is shorter than its diff:
```python
import jax
import jax.numpy as jnp
from jax import lax
from jax.sharding import Mesh, PartitionSpec as P

RING = 16
HALVES = 2
SUMMED = ("row", "half")
SCALE = 2.0**21


def swap(block):
    return lax.ppermute(block, "half", [(0, 1), (1, 0)])


def parts_of(tile, half):
    rows = tile.shape[0] // HALVES
    halves = tile.reshape(HALVES, rows, tile.shape[1])
    return (
        lax.dynamic_index_in_dim(halves, half, 0, False),
        lax.dynamic_index_in_dim(halves, 1 - half, 0, False),
    )


def spread_panels(own, other, owners, half):
    slot = owners[:2].reshape(2, 1, 1)
    level = jnp.where(slot % RING == lax.axis_index("z"), SCALE, 0.0)
    from_own = jnp.where(slot // RING == half, level, 0.0)
    from_other = jnp.where(slot // RING == half, 0.0, level)
    sent = own.astype(jnp.float32) * from_own + other.astype(jnp.float32) * from_other
    return lax.psum(sent.astype(jnp.float16), "z").astype(jnp.bfloat16)


def contract(left, right, dims):
    return lax.dot_general(left, right, (dims, ((), ())), preferred_element_type=jnp.float32)


def sum_over(part, axes):
    count = lax.axis_size(axes)
    cut = part.reshape((count, part.shape[0] // count) + part.shape[1:])
    share = jnp.sum(lax.all_to_all(cut, axes, 0, 0), axis=0)
    spread = jnp.broadcast_to(share[None], (count,) + share.shape)
    return lax.all_to_all(spread, axes, 0, 0).reshape(part.shape)


def exact(left, right):
    return lax.dot_general(
        left, right, (((1,), (1,)), ((), ())), precision=lax.Precision.HIGHEST,
        preferred_element_type=jnp.float32,
    )


def per_device(eigvecs, reflectors, factors, owners):
    columns = eigvecs.shape[1]
    half = lax.axis_index("half")
    own, away = parts_of(reflectors, half)
    other = swap(away)
    mine, guest = parts_of(eigvecs, half)
    other, guest = lax.optimization_barrier((other, guest))
    theirs = swap(guest)
    panels = spread_panels(own, other, owners, half)

    blocks = []
    for p in range(2):
        here = contract(mine, panels[p], ((0,), (0,)))
        there = contract(theirs, panels[p], ((0,), (0,)))
        blocks += [jnp.where(half == 0, here, there), jnp.where(half == 0, there, here)]
    cross = contract(panels[1], panels[0], ((0,), (0,)))
    summed = sum_over(jnp.concatenate(blocks + [cross], axis=0), SUMMED)
    count = HALVES * columns
    first = summed[:count] * (1 / SCALE)
    second = summed[count : 2 * count] * (1 / SCALE)
    cross = summed[2 * count :] * (1 / SCALE**2)
    lead = exact(first, factors[0]).astype(jnp.bfloat16)
    rest = second - exact(lead.astype(jnp.float32), cross)
    tail = exact(rest, factors[1]).astype(jnp.bfloat16)
    coeffs = [part.reshape(HALVES, columns, part.shape[1]) for part in (lead, tail)]

    def updated(tile, which):
        total = tile.astype(jnp.float32)
        for p in range(2):
            part = lax.dynamic_index_in_dim(coeffs[p], which, 0, False)
            total = total - contract(panels[p], part, ((1,), (1,))) * (1 / SCALE)
        return total.astype(jnp.bfloat16)

    got = swap(updated(theirs, 1 - half))
    kept = updated(mine, half)
    first_rows = jnp.where(half == 0, kept, got)
    last_rows = jnp.where(half == 0, got, kept)
    return jnp.concatenate([first_rows, last_rows], axis=0)


def solution(mesh):
    fine = Mesh(mesh.devices.reshape(-1, HALVES, RING), ("row", "half", "z"))
    tiled = P("row", ("half", "z"))
    return jax.shard_map(
        per_device, mesh=fine, in_specs=(tiled, tiled, P(), P()), out_specs=tiled, check_vma=False
    )
```

time: 184 us -> 186 us (1.011)
  waiting for transfers between devices: 22.1 us -> 31.6 us
  between operations: 5.25 us -> 0.23 us
  blocking collectives: 127 us -> 125 us
    ppermute x2 -> x3, waiting for transfers between devices: 13 us -> 31.6 us  [swap(): return lax.ppermute(block, 'half', [(0, 1), (1, 0)])]
    all_to_all x1 -> x0, waiting for transfers between devices: 9.14 us -> none  [gather_panels(): lax.all_to_all(block.reshape(HALVES, rows // HALVES, width), 'half', 0, 0)]
    ppermute x2 -> x3, starting transfers between devices: 7.29 us -> 13.5 us  [swap(): return lax.ppermute(block, 'half', [(0, 1), (1, 0)])]
    all_to_all x1 -> x0, starting transfers between devices: 4.97 us -> none  [gather_panels(): lax.all_to_all(block.reshape(HALVES, rows // HALVES, width), 'half', 0, 0)]
    mul x0 -> x1, other arithmetic: none -> 2.82 us  [spread_panels(): own.astype(jnp.float32) * from_own + other.astype(jnp.float32) * from_other]
    concatenate x2 -> x0, other arithmetic: 2.65 us -> none  [the longest x1 1.93 us: gather_panels(): whole = lax.psum(jnp.concatenate(sent, axis=1), 'z')]
    psum x1, blocking collectives: 75 us -> 73 us  [spread_panels(): return lax.psum(sent.astype(jnp.float16), 'z').astype(jnp.bfloat16)]
    convert_element_type x2 -> x3, other arithmetic: 3.79 us -> 5.6 us  [the longest x2 4.21 us: spread_panels(): return lax.psum(sent.astype(jnp.float16), 'z').astype(jnp.bfloat16)]
  transfers between devices with their start and end apart: 3 -> 3, of which waited for: 2 -> 2; matrix products, arithmetic and copies ran while one was open for 3% -> 4% of each run, Pallas kernels for 0% -> 0%
where the time goes in v4:
time: 186 us; the launch traced here: 185 us
  blocking collectives  125 us (67%)
  waiting for transfers between devices  31.6 us (17%)
  starting transfers between devices  13.5 us (7%)
  other arithmetic  9.64 us (5%)
  matrix products  4.85 us (3%)
    psum x1, blocking collectives, spread_panels(): return lax.psum(sent.astype(jnp.float16), 'z').astype(jnp.bfloat16)  73 us
    all_to_all x1, blocking collectives, sum_over(): share = jnp.sum(lax.all_to_all(cut, axes, 0, 0), axis=0)  33.4 us
    ppermute x3, waiting for transfers between devices, swap(): return lax.ppermute(block, 'half', [(0, 1), (1, 0)])  31.6 us
    all_to_all x1, blocking collectives, sum_over(): return lax.all_to_all(spread, axes, 0, 0).reshape(part.shape)  18.1 us
    ppermute x3, starting transfers between devices, swap(): return lax.ppermute(block, 'half', [(0, 1), (1, 0)])  13.5 us
    convert_element_type x2, other arithmetic, spread_panels(): return lax.psum(sent.astype(jnp.float16), 'z').astype(jnp.bfloat16)  4.21 us
  transfers between devices with their start and end apart: 3, of which 2 were waited for; matrix products, arithmetic and copies ran while one was open for 4% of the time, Pallas kernels for 0%

profile of v4, /device:TPU:1, one launch (start us, length us, event | category | flops | bytes accessed | tf_op | source)
XLA Modules:
  0.0 185.3 jit_solution(17875663867101681635)
XLA Ops:
  0.0 0.0 copy-start.4
  0.0 0.0 copy-start
  0.0 2.8 %bitcast_convert_fusion = (f32[2048,256]{1,0:T(8,128)S(1)}, bf16[2048,256]{1,0:T(8,128)(2,1)}) fusion(bf16[2,2048,256]{2,1,0:T(8,128)(2,1)} %bitcast.75, s32[]{:T(128)S(6)} %select_n.78, s32[]{:T(128)S(6)} %select_n.83), kind=kLoop, calls=%fused_computation.15 | loop fusion | flops 524288 | bytes 5242888 | tf_op jit(solution)/shard_map/mul | solution.py:30
  2.8 5.5 %collective-permute-start = (bf16[2048,256]{1,0:T(8,128)(2,1)}, bf16[2048,256]{1,0:T(8,128)(2,1)}, u32[]{:S(2)}, u32[]{:S(2)}) collective-permute-start(bf16[2048,256]{1,0:T(8,128)(2,1)} %get-tuple-element.13), channel_id=1, source_target_pairs={{0,16},{16,0},{1,17},{17,1},{2,18},{18,2},{3,19},{19,3},{4,20},{20... | collective-permute-start | bytes 3145736 | tf_op jit(solution)/shard_map/ppermute | solution.py:13
  8.3 0.0 copy-done.4
  8.4 0.0 copy-done
  8.4 0.8 dynamic-slice_bitcast_fusion.1
  9.2 18.8 %collective-permute-done = bf16[2048,256]{1,0:T(8,128)(2,1)} collective-permute-done((bf16[2048,256]{1,0:T(8,128)(2,1)}, bf16[2048,256]{1,0:T(8,128)(2,1)}, u32[]{:S(2)}, u32[]{:S(2)}) %collective-permute-start) | collective-permute-done | bytes 1048608 | tf_op jit(solution)/shard_map/ppermute | solution.py:13
  28.0 5.6 %collective-permute-start.1 = (bf16[2048,128]{1,0:T(8,128)(2,1)}, bf16[2048,128]{1,0:T(8,128)(2,1)S(1)}, u32[]{:S(2)}, u32[]{:S(2)}) collective-permute-start(bf16[2048,128]{1,0:T(8,128)(2,1)} %dynamic-slice_bitcast_fusion.1), channel_id=1, source_target_pairs={{0,16},{16,0},{1,17},{17,1},{2,18},{18,2},{3,19},{19,3},{4,20},{20... | collective-permute-start | bytes 1572872 | tf_op jit(solution)/shard_map/ppermute | solution.py:13
  33.6 1.4 convert_element_type.31
  35.0 2.2 %add_convert_fusion = f16[2,2048,256]{2,1,0:T(8,128)(2,1)} fusion(f32[2]{0:T(128)S(1)} %compare_select_fusion.4, f32[2048,256]{1,0:T(8,128)S(1)} %convert_element_type.31, f32[2]{0:T(128)S(1)} %get-tuple-element.9, f32[2048,256]{1,0:T(8,128)S(1)} %get-tuple-element.12), kind=kLoop, calls=%fused_computation | loop fusion | flops 4194304 | bytes 6291472 | tf_op jit(solution)/shard_map/convert_element_type | solution.py:31
  37.2 73.0 %all-reduce.1 = u32[2,4,65536]{2,1,0:T(4,128)} all-reduce(u32[2,4,65536]{2,1,0:T(4,128)} %bitcast.67), channel_id=1, replica_groups=mesh['row'=16,'half'=2,'z'=16] {'z'}, use_global_device_ids=true, to_apply=%region_0.1.clone | all-reduce | flops 524288 | bytes 4194304 | tf_op jit(solution)/shard_map/psum | solution.py:31
  110.2 0.0 copy-start.1
  110.2 2.0 %convert_element_type.33 = bf16[2,2048,256]{2,1,0:T(8,128)(2,1)S(1)} convert(f16[2,2048,256]{2,1,0:T(8,128)(2,1)} %bitcast.68) | non-fusion elementwise | flops 1048576 | bytes 4194304 | tf_op jit(solution)/shard_map/convert_element_type | solution.py:31
  112.3 0.0 collective-permute-done.1
  112.3 0.3 fusion.3
  112.6 0.0 copy-done.1
  112.6 0.4 select_dynamic-update-slice_fusion.3
  113.0 0.3 fusion.5
  113.4 0.4 select_dynamic-update-slice_fusion.1
  113.8 0.5 convolution_dynamic-update-slice_fusion
  114.3 33.4 %all_to_all.10 = f32[32,24,256]{2,1,0:T(8,128)S(1)} all-to-all(f32[32,24,256]{2,1,0:T(8,128)S(1)} %bitcast.78), channel_id=1, replica_groups=mesh['row'=16,'half'=2,'z'=16] {'row','half'}, dimensions={0} | all-to-all | bytes 1572864 | tf_op jit(solution)/shard_map/all_to_all | solution.py:41
  147.7 0.1 reduce_sum.9
  147.8 0.0 copy-start.3
  147.8 0.1 broadcast_in_dim.22
  147.8 18.1 %all_to_all.11 = f32[32,24,256]{2,1,0:T(8,128)S(1)} all-to-all(f32[32,24,256]{2,1,0:T(8,128)S(1)} %broadcast_in_dim.22), channel_id=1, replica_groups=mesh['row'=16,'half'=2,'z'=16] {'row','half'}, dimensions={0} | all-to-all | bytes 1572864 | tf_op jit(solution)/shard_map/all_to_all | solution.py:43
  165.9 0.0 copy-done.3
  165.9 0.4 convolution_convert_fusion.1
  166.4 0.3 convolution_subtract_fusion
  166.7 0.4 convolution_convert_fusion
  167.1 0.4 convolution_multiply_fusion
  167.6 0.0 copy-start.2
  167.6 0.4 subtract_convert_fusion
  168.0 2.4 %collective-permute-start.2 = (bf16[2048,128]{1,0:T(8,128)(2,1)S(1)}, bf16[2048,128]{1,0:T(8,128)(2,1)S(1)}, u32[]{:S(2)}, u32[]{:S(2)}) collective-permute-start(bf16[2048,128]{1,0:T(8,128)(2,1)S(1)} %subtract_convert_fusion), channel_id=1, source_target_pairs={{0,16},{16,0},{1,17},{17,1},{2,18},{18,2},{3,19},{19,3},{4,20},{20... | collective-permute-start | bytes 1572872 | tf_op jit(solution)/shard_map/ppermute | solution.py:13
  170.5 0.0 copy-done.2
  170.5 0.4 fusion.1
  170.9 0.4 fusion.2
  171.4 12.8 %collective-permute-done.2 = bf16[2048,128]{1,0:T(8,128)(2,1)S(1)} collective-permute-done((bf16[2048,128]{1,0:T(8,128)(2,1)S(1)}, bf16[2048,128]{1,0:T(8,128)(2,1)S(1)}, u32[]{:S(2)}, u32[]{:S(2)}) %collective-permute-start.2) | collective-permute-done | bytes 524320 | tf_op jit(solution)/shard_map/ppermute | solution.py:13
  184.2 0.1 broadcast_select_fusion.1
  184.2 1.0 pad_maximum_fusion
  (4 shorter events, 0.1 us)
Async XLA Ops:
  0.0 8.3 %copy-start.4 = (s32[32]{0:T(128)S(1)}, s32[32]{0:T(128)}, u32[]{:S(2)}) copy-start(s32[32]{0:T(128)} %param.7) | copy-start | bytes 388
  0.0 8.4 %copy-start = (bf16[4096,128]{1,0:T(8,128)(2,1)S(1)}, bf16[4096,128]{1,0:T(8,128)(2,1)}, u32[]{:S(2)}) copy-start(bf16[4096,128]{1,0:T(8,128)(2,1)} %param.4) | copy-start | bytes 3145732
  2.8 25.2 %collective-permute-start = (bf16[2048,256]{1,0:T(8,128)(2,1)}, bf16[2048,256]{1,0:T(8,128)(2,1)}, u32[]{:S(2)}, u32[]{:S(2)}) collective-permute-start(bf16[2048,256]{1,0:T(8,128)(2,1)} %get-tuple-element.13), channel_id=1, source_target_pairs={{0,16},{16,0},{1,17},{17,1},{2,18},{18,2},{3,19},{19,3},{4,20},{20... | collective-permute-start | bytes 3145736 | tf_op jit(solution)/shard_map/ppermute | solution.py:13
  28.0 84.2 %collective-permute-start.1 = (bf16[2048,128]{1,0:T(8,128)(2,1)}, bf16[2048,128]{1,0:T(8,128)(2,1)S(1)}, u32[]{:S(2)}, u32[]{:S(2)}) collective-permute-start(bf16[2048,128]{1,0:T(8,128)(2,1)} %dynamic-slice_bitcast_fusion.1), channel_id=1, source_target_pairs={{0,16},{16,0},{1,17},{17,1},{2,18},{18,2},{3,19},{19,3},{4,20},{20... | collective-permute-start | bytes 1572872 | tf_op jit(solution)/shard_map/ppermute | solution.py:13
  110.2 2.4 %copy-start.1 = (bf16[4096,128]{1,0:T(8,128)(2,1)S(1)}, bf16[4096,128]{1,0:T(8,128)(2,1)}, u32[]{:S(2)}) copy-start(bf16[4096,128]{1,0:T(8,128)(2,1)} %param.4) | copy-start | bytes 3145732
  147.8 18.2 %copy-start.3 = (f32[2,256,256]{2,1,0:T(8,128)S(1)}, f32[2,256,256]{2,1,0:T(8,128)}, u32[]{:S(2)}) copy-start(f32[2,256,256]{2,1,0:T(8,128)} %param.6) | copy-start | bytes 1572868
  167.6 2.9 %copy-start.2 = (bf16[4096,128]{1,0:T(8,128)(2,1)S(1)}, bf16[4096,128]{1,0:T(8,128)(2,1)}, u32[]{:S(2)}) copy-start(bf16[4096,128]{1,0:T(8,128)(2,1)} %param.4) | copy-start | bytes 3145732
  168.0 16.1 %collective-permute-start.2 = (bf16[2048,128]{1,0:T(8,128)(2,1)S(1)}, bf16[2048,128]{1,0:T(8,128)(2,1)S(1)}, u32[]{:S(2)}, u32[]{:S(2)}) collective-permute-start(bf16[2048,128]{1,0:T(8,128)(2,1)S(1)} %subtract_convert_fusion), channel_id=1, source_target_pairs={{0,16},{16,0},{1,17},{17,1},{2,18},{18,2},{3,19},{19,3},{4,20},{20... | collective-permute-start | bytes 1572872 | tf_op jit(solution)/shard_map/ppermute | solution.py:13

commit v5 on v4

--- a/solution.py
+++ b/solution.py
@@ -5,12 +5,11 @@
 
 RING = 16
 HALVES = 2
-SUMMED = ("row", "half")
 SCALE = 2.0**21
 
 
-def swap(block):
-    return lax.ppermute(block, "half", [(0, 1), (1, 0)])
+def swap(block, axis="half"):
+    return lax.ppermute(block, axis, [(0, 1), (1, 0)])
 
 
 def parts_of(tile, half):
@@ -24,11 +23,10 @@
 
 def spread_panels(own, other, owners, half):
     slot = owners[:2].reshape(2, 1, 1)
-    level = jnp.where(slot % RING == lax.axis_index("z"), SCALE, 0.0)
-    from_own = jnp.where(slot // RING == half, level, 0.0)
-    from_other = jnp.where(slot // RING == half, 0.0, level)
-    sent = own.astype(jnp.float32) * from_own + other.astype(jnp.float32) * from_other
-    return lax.psum(sent.astype(jnp.float16), "z").astype(jnp.bfloat16)
+    block = jnp.where(slot // RING == half, own[None], other[None])
+    sent = jnp.where(slot % RING == lax.axis_index("z"), block, jnp.zeros_like(block))
+    scaled = (sent.astype(jnp.float32) * SCALE).astype(jnp.float16)
+    return lax.psum(scaled, "z")
 
 
 def contract(left, right, dims):
@@ -41,6 +39,16 @@
     share = jnp.sum(lax.all_to_all(cut, axes, 0, 0), axis=0)
     spread = jnp.broadcast_to(share[None], (count,) + share.shape)
     return lax.all_to_all(spread, axes, 0, 0).reshape(part.shape)
+
+
+def sum_over_rows(part):
+    core = lax.axis_index("core")
+    keep, give = parts_of(part, core)
+    kept = sum_over(keep + swap(give, "core"), ("chip", "half"))
+    rest = swap(kept, "core")
+    return jnp.concatenate(
+        [jnp.where(core == 0, kept, rest), jnp.where(core == 0, rest, kept)], axis=0
+    )
 
 
 def exact(left, right):
@@ -56,9 +64,9 @@
     own, away = parts_of(reflectors, half)
     other = swap(away)
     mine, guest = parts_of(eigvecs, half)
-    other, guest = lax.optimization_barrier((other, guest))
     theirs = swap(guest)
-    panels = spread_panels(own, other, owners, half)
+    whole = spread_panels(own, other, owners, half)
+    panels = [whole[p].astype(jnp.bfloat16) for p in range(2)]
 
     blocks = []
     for p in range(2):
@@ -66,7 +74,7 @@
         there = contract(theirs, panels[p], ((0,), (0,)))
         blocks += [jnp.where(half == 0, here, there), jnp.where(half == 0, there, here)]
     cross = contract(panels[1], panels[0], ((0,), (0,)))
-    summed = sum_over(jnp.concatenate(blocks + [cross], axis=0), SUMMED)
+    summed = sum_over_rows(jnp.concatenate(blocks + [cross], axis=0))
     count = HALVES * columns
     first = summed[:count] * (1 / SCALE)
     second = summed[count : 2 * count] * (1 / SCALE)
@@ -91,8 +99,8 @@
 
 
 def solution(mesh):
-    fine = Mesh(mesh.devices.reshape(-1, HALVES, RING), ("row", "half", "z"))
-    tiled = P("row", ("half", "z"))
+    fine = Mesh(mesh.devices.reshape(-1, 2, HALVES, RING), ("chip", "core", "half", "z"))
+    tiled = P(("chip", "core"), ("half", "z"))
     return jax.shard_map(
         per_device, mesh=fine, in_specs=(tiled, tiled, P(), P()), out_specs=tiled, check_vma=False
     )

time: 186 us -> 182 us (0.978)
  blocking collectives: 125 us -> 100 us
  starting transfers between devices: 13.5 us -> 30.2 us
  other arithmetic: 9.64 us -> 6.14 us
  local copies, waits for them, and re-layouts: 0.91 us -> 4.35 us
  waiting for transfers between devices: 31.6 us -> 33.8 us
    all_to_all x1, blocking collectives: 33.4 us -> 15.2 us  [sum_over(): share = jnp.sum(lax.all_to_all(cut, axes, 0, 0), axis=0)]
    ppermute x3 -> x5, starting transfers between devices: 13.5 us -> 30.2 us  [swap(): return lax.ppermute(block, axis, [(0, 1), (1, 0)])]
    all_to_all x1, blocking collectives: 18.1 us -> 11.7 us  [sum_over(): return lax.all_to_all(spread, axes, 0, 0).reshape(part.shape)]
    convert_element_type x3 -> x1, other arithmetic: 5.6 us -> 2.32 us  [spread_panels(): scaled = (sent.astype(jnp.float32) * SCALE).astype(jnp.float16)]
    mul x1 -> x0, other arithmetic: 2.82 us -> none  [spread_panels(): own.astype(jnp.float32) * from_own + other.astype(jnp.float32) * from_other]
    broadcast_in_dim x0 -> x1, local copies, waits for them, and re-layouts: none -> 2.73 us  [spread_panels(): block = jnp.where(slot // RING == half, own[None], other[None])]
    ppermute x3 -> x5, waiting for transfers between devices: 31.6 us -> 33.8 us  [swap(): return lax.ppermute(block, axis, [(0, 1), (1, 0)])]
  transfers between devices with their start and end apart: 3 -> 5, of which waited for: 2 -> 4; matrix products, arithmetic and copies ran while one was open for 4% -> 2% of each run, Pallas kernels for 0% -> 0%
where the time goes in v5:
time: 182 us; the launch traced here: 181 us
  blocking collectives  100 us (55%)
  waiting for transfers between devices  33.8 us (19%)
  starting transfers between devices  30.2 us (17%)
  other arithmetic  6.14 us (3%)
  matrix products  5.96 us (3%)
  local copies, waits for them, and re-layouts  4.35 us (2%)
    psum x1, blocking collectives, spread_panels(): return lax.psum(scaled, 'z')  73.4 us
    ppermute x5, waiting for transfers between devices, swap(): return lax.ppermute(block, axis, [(0, 1), (1, 0)])  33.8 us
    ppermute x5, starting transfers between devices, swap(): return lax.ppermute(block, axis, [(0, 1), (1, 0)])  30.2 us
    all_to_all x1, blocking collectives, sum_over(): share = jnp.sum(lax.all_to_all(cut, axes, 0, 0), axis=0)  15.2 us
    all_to_all x1, blocking collectives, sum_over(): return lax.all_to_all(spread, axes, 0, 0).reshape(part.shape)  11.7 us
    dot_general x9, matrix products, contract(): lax.dot_general(left, right, (dims, ((), ())), preferred_element_type=jnp...  4.82 us
  transfers between devices with their start and end apart: 5, of which 4 were waited for; matrix products, arithmetic and copies ran while one was open for 2% of the time, Pallas kernels for 0%

profile of v5, /device:TPU:1, one launch (start us, length us, event | category | flops | bytes accessed | tf_op | source)
XLA Modules:
  0.0 181.2 jit_solution(6333684179865581466)
XLA Ops:
  0.0 0.0 copy-start
  0.0 0.0 copy-start.4
  0.0 2.7 %dynamic-slice_bitcast_fusion.1 = (bf16[2048,256]{1,0:T(8,128)(2,1)S(1)}, bf16[2048,256]{1,0:T(8,128)(2,1)}) fusion(bf16[2,2048,256]{2,1,0:T(8,128)(2,1)} %bitcast.90, s32[]{:T(128)S(6)} %select_n.89, s32[]{:T(128)S(6)} %select_n.92), kind=kLoop, calls=%fused_computation.18 | loop fusion | bytes 4194312 | tf_op jit(solution)/shard_map/jit(_where)/broadcast_in_dim | solution.py:26
  2.7 5.5 %collective-permute-start = (bf16[2048,256]{1,0:T(8,128)(2,1)}, bf16[2048,256]{1,0:T(8,128)(2,1)S(1)}, u32[]{:S(2)}, u32[]{:S(2)}) collective-permute-start(bf16[2048,256]{1,0:T(8,128)(2,1)} %get-tuple-element.6), channel_id=1, source_target_pairs={{0,16},{16,0},{1,17},{17,1},{2,18},{18,2},{3,19},{19,3},{4,20},{20... | collective-permute-start | bytes 3145736 | tf_op jit(solution)/shard_map/ppermute | solution.py:12
  8.2 0.0 copy-done
  8.3 1.9 %collective-permute-start.1 = (bf16[2048,128]{1,0:T(8,128)(2,1)S(1)}, bf16[2048,128]{1,0:T(8,128)(2,1)S(1)}, u32[]{:S(2)}, u32[]{:S(2)}) collective-permute-start(bf16[2048,128]{1,0:T(8,128)(2,1)S(1)} %dynamic-slice_bitcast_fusion.2), channel_id=1, source_target_pairs={{0,16},{16,0},{1,17},{17,1},{2,18},{18,2},{3,19},{19,3},{4,20},{20... | collective-permute-start | bytes 1572872 | tf_op jit(solution)/shard_map/ppermute | solution.py:12
  10.2 0.0 copy-done.4
  10.2 17.7 %collective-permute-done = bf16[2048,256]{1,0:T(8,128)(2,1)S(1)} collective-permute-done((bf16[2048,256]{1,0:T(8,128)(2,1)}, bf16[2048,256]{1,0:T(8,128)(2,1)S(1)}, u32[]{:S(2)}, u32[]{:S(2)}) %collective-permute-start) | collective-permute-done | bytes 1048608 | tf_op jit(solution)/shard_map/ppermute | solution.py:12
  27.9 2.3 %multiply_convert_fusion = f16[2,2048,256]{2,1,0:T(8,128)(2,1)} fusion(pred[2]{0:T(512)(128)(4,1)S(1)} %get-tuple-element.12, pred[2]{0:T(512)(128)(4,1)S(1)} %get-tuple-element.11, bf16[2048,256]{1,0:T(8,128)(2,1)S(1)} %collective-permute-done, bf16[2048,256]{1,0:T(8,128)(2,1)S(1)} %get-tuple-element.5), kind=kLoop, calls=%fused_computation | loop fusion | flops 5242880 | bytes 4194308 | tf_op jit(solution)/shard_map/convert_element_type | solution.py:28
  30.2 73.4 %all-reduce.1 = u32[2,4,65536]{2,1,0:T(4,128)S(1)} all-reduce(u32[2,4,65536]{2,1,0:T(4,128)} %bitcast.85), channel_id=1, replica_groups=mesh['chip'=8,'core'=2,'half'=2,'z'=16] {'z'}, use_global_device_ids=true, to_apply=%region_0.1.clone | all-reduce | flops 524288 | bytes 4194304 | tf_op jit(solution)/shard_map/psum | solution.py:29
  103.7 0.0 collective-permute-done.1
  103.7 0.3 fusion.8
  104.0 0.0 copy-start.1
  104.0 1.5 select_dynamic-update-slice_fusion.3
  105.5 0.3 fusion.17
  105.9 0.0 copy-done.1
  105.9 0.4 select_dynamic-update-slice_fusion.1
  106.3 0.5 convolution_dynamic-update-slice_fusion
  106.8 0.8 dynamic-slice_bitcast_fusion.3
  107.6 14.9 %collective-permute-start.2 = (f32[384,256]{1,0:T(8,128)}, f32[384,256]{1,0:T(8,128)}, u32[]{:S(2)}, u32[]{:S(2)}) collective-permute-start(f32[384,256]{1,0:T(8,128)} %dynamic-slice_bitcast_fusion.3), channel_id=1, source_target_pairs={{0,32},{32,0},{1,33},{33,1},{2,34},{34,2},{3,35},{35,3},{4,36},{36... | collective-permute-start | bytes 1179656 | tf_op jit(solution)/shard_map/ppermute | solution.py:12
  122.5 1.7 collective-permute-done.2
  124.2 1.0 bitcast_add_fusion
  125.2 0.0 copy-start.3
  125.2 15.2 %all_to_all.10 = f32[16,24,256]{2,1,0:T(8,128)S(1)} all-to-all(f32[16,24,256]{2,1,0:T(8,128)S(1)} %bitcast.92), channel_id=1, replica_groups=mesh['chip'=8,'core'=2,'half'=2,'z'=16] {'chip','half'}, dimensions={0} | all-to-all | bytes 786432 | tf_op jit(solution)/shard_map/all_to_all | solution.py:39
  140.4 0.6 reduce_sum.9
  141.1 0.8 broadcast_in_dim.51
  141.8 11.7 %all_to_all.11 = f32[16,24,256]{2,1,0:T(8,128)S(1)} all-to-all(f32[16,24,256]{2,1,0:T(8,128)S(1)} %broadcast_in_dim.51), channel_id=1, replica_groups=mesh['chip'=8,'core'=2,'half'=2,'z'=16] {'chip','half'}, dimensions={0} | all-to-all | bytes 786432 | tf_op jit(solution)/shard_map/all_to_all | solution.py:41
  153.6 4.9 %collective-permute-start.3 = (f32[384,256]{1,0:T(8,128)S(1)}, f32[384,256]{1,0:T(8,128)}, u32[]{:S(2)}, u32[]{:S(2)}) collective-permute-start(f32[384,256]{1,0:T(8,128)S(1)} %bitcast.91), channel_id=1, source_target_pairs={{0,32},{32,0},{1,33},{33,1},{2,34},{34,2},{3,35},{35,3},{4,36},{36... | collective-permute-start | bytes 1179656 | tf_op jit(solution)/shard_map/ppermute | solution.py:12
  158.5 1.5 collective-permute-done.3
  159.9 1.0 broadcast_select_fusion.2
  161.0 0.0 copy-done.3
  161.0 0.4 convolution_convert_fusion.1
  161.4 0.3 fusion.25
  161.7 0.4 convolution_convert_fusion
  162.1 0.4 convolution_multiply_fusion
  162.6 0.0 copy-start.2
  162.6 0.4 subtract_convert_fusion
  163.1 3.0 %collective-permute-start.4 = (bf16[2048,128]{1,0:T(8,128)(2,1)S(1)}, bf16[2048,128]{1,0:T(8,128)(2,1)S(1)}, u32[]{:S(2)}, u32[]{:S(2)}) collective-permute-start(bf16[2048,128]{1,0:T(8,128)(2,1)S(1)} %subtract_convert_fusion), channel_id=1, source_target_pairs={{0,16},{16,0},{1,17},{17,1},{2,18},{18,2},{3,19},{19,3},{4,20},{20... | collective-permute-start | bytes 1572872 | tf_op jit(solution)/shard_map/ppermute | solution.py:12
  166.1 0.0 copy-done.2
  166.1 0.4 fusion.1
  166.5 13.0 %collective-permute-done.4 = bf16[2048,128]{1,0:T(8,128)(2,1)S(1)} collective-permute-done((bf16[2048,128]{1,0:T(8,128)(2,1)S(1)}, bf16[2048,128]{1,0:T(8,128)(2,1)S(1)}, u32[]{:S(2)}, u32[]{:S(2)}) %collective-permute-start.4) | collective-permute-done | bytes 524320 | tf_op jit(solution)/shard_map/ppermute | solution.py:12
  179.6 0.5 broadcast_select_fusion.1
  180.1 1.0 pad_maximum_fusion
  (4 shorter events, 0.1 us)
Async XLA Ops:
  0.0 8.2 %copy-start = (bf16[4096,128]{1,0:T(8,128)(2,1)S(1)}, bf16[4096,128]{1,0:T(8,128)(2,1)}, u32[]{:S(2)}) copy-start(bf16[4096,128]{1,0:T(8,128)(2,1)} %param.4) | copy-start | bytes 3145732
  0.0 10.2 %copy-start.4 = (s32[32]{0:T(128)S(1)}, s32[32]{0:T(128)}, u32[]{:S(2)}) copy-start(s32[32]{0:T(128)} %param.7) | copy-start | bytes 388
  2.7 25.2 %collective-permute-start = (bf16[2048,256]{1,0:T(8,128)(2,1)}, bf16[2048,256]{1,0:T(8,128)(2,1)S(1)}, u32[]{:S(2)}, u32[]{:S(2)}) collective-permute-start(bf16[2048,256]{1,0:T(8,128)(2,1)} %get-tuple-element.6), channel_id=1, source_target_pairs={{0,16},{16,0},{1,17},{17,1},{2,18},{18,2},{3,19},{19,3},{4,20},{20... | collective-permute-start | bytes 3145736 | tf_op jit(solution)/shard_map/ppermute | solution.py:12
  8.3 95.4 %collective-permute-start.1 = (bf16[2048,128]{1,0:T(8,128)(2,1)S(1)}, bf16[2048,128]{1,0:T(8,128)(2,1)S(1)}, u32[]{:S(2)}, u32[]{:S(2)}) collective-permute-start(bf16[2048,128]{1,0:T(8,128)(2,1)S(1)} %dynamic-slice_bitcast_fusion.2), channel_id=1, source_target_pairs={{0,16},{16,0},{1,17},{17,1},{2,18},{18,2},{3,19},{19,3},{4,20},{20... | collective-permute-start | bytes 1572872 | tf_op jit(solution)/shard_map/ppermute | solution.py:12
  104.0 1.9 %copy-start.1 = (bf16[4096,128]{1,0:T(8,128)(2,1)S(1)}, bf16[4096,128]{1,0:T(8,128)(2,1)}, u32[]{:S(2)}) copy-start(bf16[4096,128]{1,0:T(8,128)(2,1)} %param.4) | copy-start | bytes 3145732
  107.6 16.6 %collective-permute-start.2 = (f32[384,256]{1,0:T(8,128)}, f32[384,256]{1,0:T(8,128)}, u32[]{:S(2)}, u32[]{:S(2)}) collective-permute-start(f32[384,256]{1,0:T(8,128)} %dynamic-slice_bitcast_fusion.3), channel_id=1, source_target_pairs={{0,32},{32,0},{1,33},{33,1},{2,34},{34,2},{3,35},{35,3},{4,36},{36... | collective-permute-start | bytes 1179656 | tf_op jit(solution)/shard_map/ppermute | solution.py:12
  125.2 35.8 %copy-start.3 = (f32[2,256,256]{2,1,0:T(8,128)S(1)}, f32[2,256,256]{2,1,0:T(8,128)}, u32[]{:S(2)}) copy-start(f32[2,256,256]{2,1,0:T(8,128)} %param.6) | copy-start | bytes 1572868
  153.6 6.3 %collective-permute-start.3 = (f32[384,256]{1,0:T(8,128)S(1)}, f32[384,256]{1,0:T(8,128)}, u32[]{:S(2)}, u32[]{:S(2)}) collective-permute-start(f32[384,256]{1,0:T(8,128)S(1)} %bitcast.91), channel_id=1, source_target_pairs={{0,32},{32,0},{1,33},{33,1},{2,34},{34,2},{3,35},{35,3},{4,36},{36... | collective-permute-start | bytes 1179656 | tf_op jit(solution)/shard_map/ppermute | solution.py:12
  162.6 3.5 %copy-start.2 = (bf16[4096,128]{1,0:T(8,128)(2,1)S(1)}, bf16[4096,128]{1,0:T(8,128)(2,1)}, u32[]{:S(2)}) copy-start(bf16[4096,128]{1,0:T(8,128)(2,1)} %param.4) | copy-start | bytes 3145732
  163.1 16.5 %collective-permute-start.4 = (bf16[2048,128]{1,0:T(8,128)(2,1)S(1)}, bf16[2048,128]{1,0:T(8,128)(2,1)S(1)}, u32[]{:S(2)}, u32[]{:S(2)}) collective-permute-start(bf16[2048,128]{1,0:T(8,128)(2,1)S(1)} %subtract_convert_fusion), channel_id=1, source_target_pairs={{0,16},{16,0},{1,17},{17,1},{2,18},{18,2},{3,19},{19,3},{4,20},{20... | collective-permute-start | bytes 1572872 | tf_op jit(solution)/shard_map/ppermute | solution.py:12

commit v6 on v4

--- a/solution.py
+++ b/solution.py
@@ -5,7 +5,6 @@
 
 RING = 16
 HALVES = 2
-SUMMED = ("row", "half")
 SCALE = 2.0**21
 
 
@@ -24,11 +23,10 @@
 
 def spread_panels(own, other, owners, half):
     slot = owners[:2].reshape(2, 1, 1)
-    level = jnp.where(slot % RING == lax.axis_index("z"), SCALE, 0.0)
-    from_own = jnp.where(slot // RING == half, level, 0.0)
-    from_other = jnp.where(slot // RING == half, 0.0, level)
-    sent = own.astype(jnp.float32) * from_own + other.astype(jnp.float32) * from_other
-    return lax.psum(sent.astype(jnp.float16), "z").astype(jnp.bfloat16)
+    block = jnp.where(slot // RING == half, own[None], other[None])
+    sent = jnp.where(slot % RING == lax.axis_index("z"), block, jnp.zeros_like(block))
+    scaled = (sent.astype(jnp.float32) * SCALE).astype(jnp.float16)
+    return lax.psum(scaled, "z")
 
 
 def contract(left, right, dims):
@@ -56,9 +54,9 @@
     own, away = parts_of(reflectors, half)
     other = swap(away)
     mine, guest = parts_of(eigvecs, half)
-    other, guest = lax.optimization_barrier((other, guest))
     theirs = swap(guest)
-    panels = spread_panels(own, other, owners, half)
+    whole = spread_panels(own, other, owners, half)
+    panels = [whole[p].astype(jnp.bfloat16) for p in range(2)]
 
     blocks = []
     for p in range(2):
@@ -66,7 +64,9 @@
         there = contract(theirs, panels[p], ((0,), (0,)))
         blocks += [jnp.where(half == 0, here, there), jnp.where(half == 0, there, here)]
     cross = contract(panels[1], panels[0], ((0,), (0,)))
-    summed = sum_over(jnp.concatenate(blocks + [cross], axis=0), SUMMED)
+    packed = jnp.concatenate(blocks + [cross], axis=0)
+    far = swap(whole)
+    summed = sum_over(packed, ("row", "half"))
     count = HALVES * columns
     first = summed[:count] * (1 / SCALE)
     second = summed[count : 2 * count] * (1 / SCALE)
@@ -74,20 +74,22 @@
     lead = exact(first, factors[0]).astype(jnp.bfloat16)
     rest = second - exact(lead.astype(jnp.float32), cross)
     tail = exact(rest, factors[1]).astype(jnp.bfloat16)
-    coeffs = [part.reshape(HALVES, columns, part.shape[1]) for part in (lead, tail)]
+    coeffs = [
+        lax.dynamic_index_in_dim(part.reshape(HALVES, columns, part.shape[1]), half, 0, False)
+        for part in (lead, tail)
+    ]
 
-    def updated(tile, which):
+    def updated(tile, side):
         total = tile.astype(jnp.float32)
         for p in range(2):
-            part = lax.dynamic_index_in_dim(coeffs[p], which, 0, False)
-            total = total - contract(panels[p], part, ((1,), (1,))) * (1 / SCALE)
+            update = contract(side[p].astype(jnp.bfloat16), coeffs[p], ((1,), (1,)))
+            total = total - update * (1 / SCALE)
         return total.astype(jnp.bfloat16)
 
-    got = swap(updated(theirs, 1 - half))
-    kept = updated(mine, half)
-    first_rows = jnp.where(half == 0, kept, got)
-    last_rows = jnp.where(half == 0, got, kept)
-    return jnp.concatenate([first_rows, last_rows], axis=0)
+    near = updated(mine, whole)
+    rest = updated(guest, far)
+    result = jnp.stack([jnp.where(half == 0, near, rest), jnp.where(half == 0, rest, near)])
+    return result.reshape(eigvecs.shape)
 
 
 def solution(mesh):

time: 186 us -> 205 us (1.10)
  starting transfers between devices: 13.5 us -> 33 us
  other arithmetic: 9.64 us -> 4.63 us
  waiting for transfers between devices: 31.6 us -> 26.6 us
  matrix products: 4.85 us -> 9.51 us
  local copies, waits for them, and re-layouts: 0.91 us -> 4.53 us
    all_to_all x1, blocking collectives: 18.1 us -> 52.3 us  [sum_over(): return lax.all_to_all(spread, axes, 0, 0).reshape(part.shape)]
    all_to_all x1 -> x0, blocking collectives: 33.4 us -> none  [sum_over(): share = jnp.sum(lax.all_to_all(cut, axes, 0, 0), axis=0)]
    all_to_all x0 -> x1, starting transfers between devices: none -> 20.9 us  [sum_over(): share = jnp.sum(lax.all_to_all(cut, axes, 0, 0), axis=0)]
    ppermute x3, waiting for transfers between devices: 31.6 us -> 16.9 us  [swap(): return lax.ppermute(block, 'half', [(0, 1), (1, 0)])]
    all_to_all x0 -> x1, waiting for transfers between devices: none -> 9.68 us  [sum_over(): share = jnp.sum(lax.all_to_all(cut, axes, 0, 0), axis=0)]
    dot_general x9, matrix products: 3.7 us -> 8.36 us  [contract(): lax.dot_general(left, right, (dims, ((), ())), preferred_element_type=jnp...]
    convert_element_type x3 -> x1, other arithmetic: 5.6 us -> 2.32 us  [spread_panels(): scaled = (sent.astype(jnp.float32) * SCALE).astype(jnp.float16)]
    mul x1 -> x0, other arithmetic: 2.82 us -> none  [spread_panels(): own.astype(jnp.float32) * from_own + other.astype(jnp.float32) * from_other]
  transfers between devices with their start and end apart: 3 -> 4, of which waited for: 2 -> 2; matrix products, arithmetic and copies ran while one was open for 4% -> 3% of each run, Pallas kernels for 0% -> 0%
where the time goes in v6:
time: 205 us; the launch traced here: 204 us
  blocking collectives  126 us (61%)
  starting transfers between devices  33 us (16%)
  waiting for transfers between devices  26.6 us (13%)
  matrix products  9.51 us (5%)
  other arithmetic  4.63 us (2%)
  local copies, waits for them, and re-layouts  4.53 us (2%)
    psum x1, blocking collectives, spread_panels(): return lax.psum(scaled, 'z')  73.6 us
    all_to_all x1, blocking collectives, sum_over(): return lax.all_to_all(spread, axes, 0, 0).reshape(part.shape)  52.3 us
    all_to_all x1, starting transfers between devices, sum_over(): share = jnp.sum(lax.all_to_all(cut, axes, 0, 0), axis=0)  20.9 us
    ppermute x3, waiting for transfers between devices, swap(): return lax.ppermute(block, 'half', [(0, 1), (1, 0)])  16.9 us
    ppermute x3, starting transfers between devices, swap(): return lax.ppermute(block, 'half', [(0, 1), (1, 0)])  12.2 us
    all_to_all x1, waiting for transfers between devices, sum_over(): share = jnp.sum(lax.all_to_all(cut, axes, 0, 0), axis=0)  9.68 us
    dot_general x9, matrix products, contract(): lax.dot_general(left, right, (dims, ((), ())), preferred_element_type=jnp...  8.36 us
  transfers between devices with their start and end apart: 4, of which 2 were waited for; matrix products, arithmetic and copies ran while one was open for 3% of the time, Pallas kernels for 0%

profile of v6, /device:TPU:1, one launch (start us, length us, event | category | flops | bytes accessed | tf_op | source)
XLA Modules:
  0.0 204.4 jit_solution(14565687108301207635)
XLA Ops:
  0.0 0.0 copy-start
  0.0 0.0 copy-start.3
  0.0 2.7 %dynamic-slice_bitcast_fusion.1 = (bf16[2048,256]{1,0:T(8,128)(2,1)S(1)}, bf16[2048,256]{1,0:T(8,128)(2,1)}) fusion(bf16[2,2048,256]{2,1,0:T(8,128)(2,1)} %bitcast.90, s32[]{:T(128)S(6)} %select_n.68, s32[]{:T(128)S(6)} %select_n.71), kind=kLoop, calls=%fused_computation.25 | loop fusion | bytes 4194312 | tf_op jit(solution)/shard_map/jit(_where)/broadcast_in_dim | solution.py:26
  2.7 5.5 %collective-permute-start = (bf16[2048,256]{1,0:T(8,128)(2,1)}, bf16[2048,256]{1,0:T(8,128)(2,1)S(1)}, u32[]{:S(2)}, u32[]{:S(2)}) collective-permute-start(bf16[2048,256]{1,0:T(8,128)(2,1)} %get-tuple-element.6), channel_id=1, source_target_pairs={{0,16},{16,0},{1,17},{17,1},{2,18},{18,2},{3,19},{19,3},{4,20},{20... | collective-permute-start | bytes 3145736 | tf_op jit(solution)/shard_map/ppermute | solution.py:12
  8.2 0.0 copy-done
  8.2 0.9 dynamic-slice_bitcast_fusion.2
  9.1 1.9 collective-permute-start.1
  11.0 0.0 copy-done.3
  11.0 16.9 %collective-permute-done = bf16[2048,256]{1,0:T(8,128)(2,1)S(1)} collective-permute-done((bf16[2048,256]{1,0:T(8,128)(2,1)}, bf16[2048,256]{1,0:T(8,128)(2,1)S(1)}, u32[]{:S(2)}, u32[]{:S(2)}) %collective-permute-start) | collective-permute-done | bytes 1048608 | tf_op jit(solution)/shard_map/ppermute | solution.py:12
  27.9 2.3 %multiply_convert_fusion = f16[2,2048,256]{2,1,0:T(8,128)(2,1)} fusion(pred[2]{0:T(512)(128)(4,1)S(1)} %get-tuple-element.10, pred[2]{0:T(512)(128)(4,1)S(1)} %get-tuple-element.9, bf16[2048,256]{1,0:T(8,128)(2,1)S(1)} %collective-permute-done, bf16[2048,256]{1,0:T(8,128)(2,1)S(1)} %get-tuple-element.5), kind=kLoop, calls=%fused_computation | loop fusion | flops 5242880 | bytes 4194308 | tf_op jit(solution)/shard_map/convert_element_type | solution.py:28
  30.2 73.6 %all-reduce.1 = u32[2,4,65536]{2,1,0:T(4,128)S(1)} all-reduce(u32[2,4,65536]{2,1,0:T(4,128)} %bitcast.83), channel_id=1, replica_groups=mesh['row'=16,'half'=2,'z'=16] {'z'}, use_global_device_ids=true, to_apply=%region_0.1.clone | all-reduce | flops 524288 | bytes 4194304 | tf_op jit(solution)/shard_map/psum | solution.py:29
  103.9 0.0 collective-permute-done.1
  103.9 1.4 fusion.14
  105.3 0.3 select_dynamic-update-slice_fusion.3
  105.6 1.4 fusion.20
  107.0 0.4 select_dynamic-update-slice_fusion.1
  107.4 0.5 convolution_dynamic-update-slice_fusion
  107.9 0.0 copy-start.1
  107.9 0.9 copy-done.1
  108.8 20.9 %all-to-all-start = ((f32[32,24,256]{2,1,0:T(8,128)}), f32[32,24,256]{2,1,0:T(8,128)}, u32[]{:S(2)}, u32[]{:S(2)}) async-start(f32[32,24,256]{2,1,0:T(8,128)} %bitcast.93), calls=%async_computation | async-start | bytes 1572864 | tf_op jit(solution)/shard_map/all_to_all | solution.py:39
  129.7 4.8 %collective-permute-start.2 = (f16[2,2048,256]{2,1,0:T(8,128)(2,1)S(1)}, f16[2,2048,256]{2,1,0:T(8,128)(2,1)}, u32[]{:S(2)}, u32[]{:S(2)}) collective-permute-start(f16[2,2048,256]{2,1,0:T(8,128)(2,1)S(1)} %bitcast.80), channel_id=1, source_target_pairs={{0,16},{16,0},{1,17},{17,1},{2,18},{18,2},{3,19},{19,3},{4,20},{20... | collective-permute-start | bytes 6291464 | tf_op jit(solution)/shard_map/ppermute | solution.py:12
  134.5 9.7 %all-to-all-done = f32[32,24,256]{2,1,0:T(8,128)} async-done(((f32[32,24,256]{2,1,0:T(8,128)}), f32[32,24,256]{2,1,0:T(8,128)}, u32[]{:S(2)}, u32[]{:S(2)}) %all-to-all-start) | async-done | bytes 786464 | tf_op jit(solution)/shard_map/all_to_all | solution.py:39
  144.1 1.2 reduce_sum.9
  145.3 0.0 copy-start.2
  145.3 0.1 broadcast_in_dim.51
  145.4 52.3 %all_to_all.10 = f32[32,24,256]{2,1,0:T(8,128)S(1)} all-to-all(f32[32,24,256]{2,1,0:T(8,128)S(1)} %broadcast_in_dim.51), channel_id=1, replica_groups=mesh['row'=16,'half'=2,'z'=16] {'row','half'}, dimensions={0} | all-to-all | bytes 1572864 | tf_op jit(solution)/shard_map/all_to_all | solution.py:41
  197.7 0.0 copy-done.2
  197.7 0.4 convolution_convert_fusion.1
  198.2 0.3 convolution_subtract_fusion
  198.5 0.4 convolution_convert_fusion
  198.9 0.4 fusion.3
  199.4 0.0 collective-permute-done.2
  199.4 1.8 fusion.1
  201.2 1.7 fusion.5
  202.8 0.5 select_bitcast_fusion.1
  203.4 1.1 pad_maximum_fusion
  (3 shorter events, 0.1 us)
Async XLA Ops:
  0.0 8.2 %copy-start = (bf16[4096,128]{1,0:T(8,128)(2,1)S(1)}, bf16[4096,128]{1,0:T(8,128)(2,1)}, u32[]{:S(2)}) copy-start(bf16[4096,128]{1,0:T(8,128)(2,1)} %param.4) | copy-start | bytes 3145732
  0.0 11.0 %copy-start.3 = (s32[32]{0:T(128)S(1)}, s32[32]{0:T(128)}, u32[]{:S(2)}) copy-start(s32[32]{0:T(128)} %param.7) | copy-start | bytes 388
  2.7 25.2 %collective-permute-start = (bf16[2048,256]{1,0:T(8,128)(2,1)}, bf16[2048,256]{1,0:T(8,128)(2,1)S(1)}, u32[]{:S(2)}, u32[]{:S(2)}) collective-permute-start(bf16[2048,256]{1,0:T(8,128)(2,1)} %get-tuple-element.6), channel_id=1, source_target_pairs={{0,16},{16,0},{1,17},{17,1},{2,18},{18,2},{3,19},{19,3},{4,20},{20... | collective-permute-start | bytes 3145736 | tf_op jit(solution)/shard_map/ppermute | solution.py:12
  9.1 94.8 %collective-permute-start.1 = (bf16[2048,128]{1,0:T(8,128)(2,1)}, bf16[2048,128]{1,0:T(8,128)(2,1)}, u32[]{:S(2)}, u32[]{:S(2)}) collective-permute-start(bf16[2048,128]{1,0:T(8,128)(2,1)} %dynamic-slice_bitcast_fusion.2), channel_id=1, source_target_pairs={{0,16},{16,0},{1,17},{17,1},{2,18},{18,2},{3,19},{19,3},{4,20},{20... | collective-permute-start | bytes 1572872 | tf_op jit(solution)/shard_map/ppermute | solution.py:12
  107.9 0.9 copy-start.1
  108.8 35.4 %all-to-all-start = ((f32[32,24,256]{2,1,0:T(8,128)}), f32[32,24,256]{2,1,0:T(8,128)}, u32[]{:S(2)}, u32[]{:S(2)}) async-start(f32[32,24,256]{2,1,0:T(8,128)} %bitcast.93), calls=%async_computation | async-start | bytes 1572864 | tf_op jit(solution)/shard_map/all_to_all | solution.py:39
  129.7 69.7 %collective-permute-start.2 = (f16[2,2048,256]{2,1,0:T(8,128)(2,1)S(1)}, f16[2,2048,256]{2,1,0:T(8,128)(2,1)}, u32[]{:S(2)}, u32[]{:S(2)}) collective-permute-start(f16[2,2048,256]{2,1,0:T(8,128)(2,1)S(1)} %bitcast.80), channel_id=1, source_target_pairs={{0,16},{16,0},{1,17},{17,1},{2,18},{18,2},{3,19},{19,3},{4,20},{20... | collective-permute-start | bytes 6291464 | tf_op jit(solution)/shard_map/ppermute | solution.py:12
  145.3 52.4 %copy-start.2 = (f32[2,256,256]{2,1,0:T(8,128)S(1)}, f32[2,256,256]{2,1,0:T(8,128)}, u32[]{:S(2)}) copy-start(f32[2,256,256]{2,1,0:T(8,128)} %param.6) | copy-start | bytes 1572868

commit v7 on v4

--- a/solution.py
+++ b/solution.py
@@ -5,7 +5,6 @@
 
 RING = 16
 HALVES = 2
-SUMMED = ("row", "half")
 SCALE = 2.0**21
 
 
@@ -13,22 +12,22 @@
     return lax.ppermute(block, "half", [(0, 1), (1, 0)])
 
 
-def parts_of(tile, half):
+def part_of(tile, half):
     rows = tile.shape[0] // HALVES
-    halves = tile.reshape(HALVES, rows, tile.shape[1])
-    return (
-        lax.dynamic_index_in_dim(halves, half, 0, False),
-        lax.dynamic_index_in_dim(halves, 1 - half, 0, False),
-    )
+    return lax.dynamic_index_in_dim(tile.reshape(HALVES, rows, tile.shape[1]), half, 0, False)
+
+
+def by_half(first, second, half):
+    place = jnp.arange(HALVES).reshape((HALVES,) + (1,) * first.ndim)
+    return jnp.where(place == half, first[None], second[None])
 
 
 def spread_panels(own, other, owners, half):
     slot = owners[:2].reshape(2, 1, 1)
-    level = jnp.where(slot % RING == lax.axis_index("z"), SCALE, 0.0)
-    from_own = jnp.where(slot // RING == half, level, 0.0)
-    from_other = jnp.where(slot // RING == half, 0.0, level)
-    sent = own.astype(jnp.float32) * from_own + other.astype(jnp.float32) * from_other
-    return lax.psum(sent.astype(jnp.float16), "z").astype(jnp.bfloat16)
+    block = jnp.where(slot // RING == half, own[None], other[None])
+    sent = jnp.where(slot % RING == lax.axis_index("z"), block, jnp.zeros_like(block))
+    scaled = (sent.astype(jnp.float32) * SCALE).astype(jnp.float16)
+    return lax.psum(scaled, "z")
 
 
 def contract(left, right, dims):
@@ -51,22 +50,23 @@
 
 
 def per_device(eigvecs, reflectors, factors, owners):
-    columns = eigvecs.shape[1]
+    columns, width = eigvecs.shape[1], reflectors.shape[1]
     half = lax.axis_index("half")
-    own, away = parts_of(reflectors, half)
-    other = swap(away)
-    mine, guest = parts_of(eigvecs, half)
-    other, guest = lax.optimization_barrier((other, guest))
-    theirs = swap(guest)
-    panels = spread_panels(own, other, owners, half)
+    other = swap(part_of(reflectors, 1 - half))
+    theirs = swap(part_of(eigvecs, 1 - half))
+    reflectors, other = lax.optimization_barrier((reflectors, other))
+    own = part_of(reflectors, half)
+    mine = part_of(eigvecs, half)
+    whole = spread_panels(own, other, owners, half)
+    panels = [whole[p].astype(jnp.bfloat16) for p in range(2)]
 
     blocks = []
     for p in range(2):
         here = contract(mine, panels[p], ((0,), (0,)))
         there = contract(theirs, panels[p], ((0,), (0,)))
-        blocks += [jnp.where(half == 0, here, there), jnp.where(half == 0, there, here)]
+        blocks.append(by_half(here, there, half).reshape(HALVES * columns, width))
     cross = contract(panels[1], panels[0], ((0,), (0,)))
-    summed = sum_over(jnp.concatenate(blocks + [cross], axis=0), SUMMED)
+    summed = sum_over(jnp.concatenate(blocks + [cross], axis=0), ("row", "half"))
     count = HALVES * columns
     first = summed[:count] * (1 / SCALE)
     second = summed[count : 2 * count] * (1 / SCALE)
@@ -85,9 +85,7 @@
 
     got = swap(updated(theirs, 1 - half))
     kept = updated(mine, half)
-    first_rows = jnp.where(half == 0, kept, got)
-    last_rows = jnp.where(half == 0, got, kept)
-    return jnp.concatenate([first_rows, last_rows], axis=0)
+    return by_half(kept, got, half).reshape(eigvecs.shape)
 
 
 def solution(mesh):

time: 186 us -> 188 us (1.011)
  blocking collectives: 125 us -> 108 us
  waiting for transfers between devices: 31.6 us -> 43.8 us
  matrix products: 4.85 us -> 10.9 us
  other arithmetic: 9.64 us -> 5.29 us
  local copies, waits for them, and re-layouts: 0.91 us -> 4.65 us
    all_to_all x1 -> x0, blocking collectives: 18.1 us -> none  [sum_over(): return lax.all_to_all(spread, axes, 0, 0).reshape(part.shape)]
    all_to_all x0 -> x1, waiting for transfers between devices: none -> 14.2 us  [sum_over(): return lax.all_to_all(spread, axes, 0, 0).reshape(part.shape)]
    all_to_all x0 -> x1, starting transfers between devices: none -> 4.3 us  [sum_over(): return lax.all_to_all(spread, axes, 0, 0).reshape(part.shape)]
    dot_general x9, matrix products: 3.7 us -> 7.74 us  [contract(): lax.dot_general(left, right, (dims, ((), ())), preferred_element_type=jnp...]
    ppermute x3, starting transfers between devices: 13.5 us -> 9.81 us  [swap(): return lax.ppermute(block, 'half', [(0, 1), (1, 0)])]
    mul x1 -> x0, other arithmetic: 2.82 us -> none  [spread_panels(): own.astype(jnp.float32) * from_own + other.astype(jnp.float32) * from_other]
    convert_element_type x3 -> x1, other arithmetic: 5.6 us -> 3.54 us  [spread_panels(): scaled = (sent.astype(jnp.float32) * SCALE).astype(jnp.float16)]
    dot_general x3, matrix products: 1.15 us -> 3.2 us  [exact(): lax.dot_general(left, right, (((1,), (1,)), ((), ())), precision=lax.Prec...]
  transfers between devices with their start and end apart: 3 -> 4, of which waited for: 2 -> 3; matrix products, arithmetic and copies ran while one was open for 4% -> 5% of each run, Pallas kernels for 0% -> 0%
where the time goes in v7:
time: 188 us; the launch traced here: 187 us
  blocking collectives  108 us (57%)
  waiting for transfers between devices  43.8 us (23%)
  starting transfers between devices  14.1 us (8%)
  matrix products  10.9 us (6%)
  other arithmetic  5.29 us (3%)
  local copies, waits for them, and re-layouts  4.65 us (2%)
    psum x1, blocking collectives, spread_panels(): return lax.psum(scaled, 'z')  74.1 us
    all_to_all x1, blocking collectives, sum_over(): share = jnp.sum(lax.all_to_all(cut, axes, 0, 0), axis=0)  34.2 us
    ppermute x3, waiting for transfers between devices, swap(): return lax.ppermute(block, 'half', [(0, 1), (1, 0)])  29.6 us
    all_to_all x1, waiting for transfers between devices, sum_over(): return lax.all_to_all(spread, axes, 0, 0).reshape(part.shape)  14.2 us
    ppermute x3, starting transfers between devices, swap(): return lax.ppermute(block, 'half', [(0, 1), (1, 0)])  9.81 us
    dot_general x9, matrix products, contract(): lax.dot_general(left, right, (dims, ((), ())), preferred_element_type=jnp...  7.74 us
    all_to_all x1, starting transfers between devices, sum_over(): return lax.all_to_all(spread, axes, 0, 0).reshape(part.shape)  4.3 us
  transfers between devices with their start and end apart: 4, of which 3 were waited for; matrix products, arithmetic and copies ran while one was open for 5% of the time, Pallas kernels for 0%

profile of v7, /device:TPU:1, one launch (start us, length us, event | category | flops | bytes accessed | tf_op | source)
XLA Modules:
  0.0 187.2 jit_solution(3842136663398155000)
XLA Ops:
  0.0 0.0 copy-start
  0.0 0.0 copy-start.3
  0.0 0.0 copy-start.5
  0.0 1.6 copy-done
  1.6 1.0 dynamic-slice_bitcast_fusion.1
  2.6 5.5 %collective-permute-start = (bf16[2048,256]{1,0:T(8,128)(2,1)}, bf16[2048,256]{1,0:T(8,128)(2,1)}, u32[]{:S(2)}, u32[]{:S(2)}) collective-permute-start(bf16[2048,256]{1,0:T(8,128)(2,1)} %dynamic-slice_bitcast_fusion.1), channel_id=1, source_target_pairs={{0,16},{16,0},{1,17},{17,1},{2,18},{18,2},{3,19},{19,3},{4,20},{20... | collective-permute-start | bytes 3145736 | tf_op jit(solution)/shard_map/ppermute | solution.py:12
  8.1 0.0 copy-done.3
  8.1 0.8 dynamic-slice_bitcast_fusion.2
  9.0 1.9 %collective-permute-start.1 = (bf16[2048,128]{1,0:T(8,128)(2,1)}, bf16[2048,128]{1,0:T(8,128)(2,1)S(1)}, u32[]{:S(2)}, u32[]{:S(2)}) collective-permute-start(bf16[2048,128]{1,0:T(8,128)(2,1)} %dynamic-slice_bitcast_fusion.2), channel_id=1, source_target_pairs={{0,16},{16,0},{1,17},{17,1},{2,18},{18,2},{3,19},{19,3},{4,20},{20... | collective-permute-start | bytes 1572872 | tf_op jit(solution)/shard_map/ppermute | solution.py:12
  10.9 0.1 broadcast_bitcast_fusion
  11.0 0.0 copy-done.5
  11.0 16.8 %collective-permute-done = bf16[2048,256]{1,0:T(8,128)(2,1)} collective-permute-done((bf16[2048,256]{1,0:T(8,128)(2,1)}, bf16[2048,256]{1,0:T(8,128)(2,1)}, u32[]{:S(2)}, u32[]{:S(2)}) %collective-permute-start) | collective-permute-done | bytes 1048608 | tf_op jit(solution)/shard_map/ppermute | solution.py:12
  27.8 0.1 dynamic-slice_bitcast_fusion
  27.9 3.5 %multiply_convert_fusion = f16[2,2048,256]{2,1,0:T(8,128)(2,1)} fusion(pred[2]{0:T(512)(128)(4,1)S(1)} %get-tuple-element.12, pred[2]{0:T(512)(128)(4,1)S(1)} %get-tuple-element.11, bf16[2048,256]{1,0:T(8,128)(2,1)} %collective-permute-done, bf16[2048,256]{1,0:T(8,128)(2,1)S(1)} %dynamic-slice_bitcast_fusion), kind=kLoop, calls=%fused_computation | loop fusion | flops 5242880 | bytes 4194308 | tf_op jit(solution)/shard_map/convert_element_type | solution.py:29
  31.4 74.1 %all-reduce.1 = u32[2,4,65536]{2,1,0:T(4,128)} all-reduce(u32[2,4,65536]{2,1,0:T(4,128)} %bitcast.84), channel_id=1, replica_groups=mesh['row'=16,'half'=2,'z'=16] {'z'}, use_global_device_ids=true, to_apply=%region_0.1.clone | all-reduce | flops 524288 | bytes 4194304 | tf_op jit(solution)/shard_map/psum | solution.py:30
  105.5 0.0 copy-start.1
  105.5 1.9 fusion.11
  107.4 1.7 fusion.20
  109.1 0.0 copy-done.1
  109.1 0.5 fusion.7
  109.6 0.0 collective-permute-done.1
  109.6 0.3 fusion.9
  110.0 0.3 fusion.18
  110.3 0.1 bitcast_select_fusion.2
  110.5 0.1 pad_maximum_fusion
  110.5 34.2 %all_to_all.10 = f32[32,24,256]{2,1,0:T(8,128)S(1)} all-to-all(f32[32,24,256]{2,1,0:T(8,128)S(1)} %bitcast.89), channel_id=1, replica_groups=mesh['row'=16,'half'=2,'z'=16] {'row','half'}, dimensions={0} | all-to-all | bytes 1572864 | tf_op jit(solution)/shard_map/all_to_all | solution.py:40
  144.7 0.1 reduce_sum.9
  144.8 0.9 broadcast_in_dim.152
  145.7 4.3 %all-to-all-start.1 = ((f32[32,24,256]{2,1,0:T(8,128)}), f32[32,24,256]{2,1,0:T(8,128)S(1)}, u32[]{:S(2)}, u32[]{:S(2)}) async-start(f32[32,24,256]{2,1,0:T(8,128)} %broadcast_in_dim.152), calls=%async_computation.1 | async-start | bytes 1572864 | tf_op jit(solution)/shard_map/all_to_all | solution.py:42
  150.0 0.1 broadcast_in_dim.132
  150.1 14.2 %all-to-all-done.1 = f32[32,24,256]{2,1,0:T(8,128)S(1)} async-done(((f32[32,24,256]{2,1,0:T(8,128)}), f32[32,24,256]{2,1,0:T(8,128)S(1)}, u32[]{:S(2)}, u32[]{:S(2)}) %all-to-all-start.1) | async-done | bytes 786464 | tf_op jit(solution)/shard_map/all_to_all | solution.py:42
  164.3 0.0 copy-start.2
  164.3 1.5 convolution_convert_fusion.1
  165.8 0.3 convolution_subtract_fusion
  166.1 1.4 convolution_convert_fusion
  167.5 1.7 convolution_multiply_fusion
  169.2 0.0 copy-start.4
  169.2 0.0 copy-done.2
  169.2 0.5 subtract_convert_fusion
  169.7 2.4 %collective-permute-start.2 = (bf16[2048,128]{1,0:T(8,128)(2,1)S(1)}, bf16[2048,128]{1,0:T(8,128)(2,1)S(1)}, u32[]{:S(2)}, u32[]{:S(2)}) collective-permute-start(bf16[2048,128]{1,0:T(8,128)(2,1)S(1)} %subtract_convert_fusion), channel_id=1, source_target_pairs={{0,16},{16,0},{1,17},{17,1},{2,18},{18,2},{3,19},{19,3},{4,20},{20... | collective-permute-start | bytes 1572872 | tf_op jit(solution)/shard_map/ppermute | solution.py:12
  172.1 0.0 copy-done.4
  172.1 0.4 fusion.1
  172.5 0.4 fusion.2
  173.0 12.8 %collective-permute-done.2 = bf16[2048,128]{1,0:T(8,128)(2,1)S(1)} collective-permute-done((bf16[2048,128]{1,0:T(8,128)(2,1)S(1)}, bf16[2048,128]{1,0:T(8,128)(2,1)S(1)}, u32[]{:S(2)}, u32[]{:S(2)}) %collective-permute-start.2) | collective-permute-done | bytes 524320 | tf_op jit(solution)/shard_map/ppermute | solution.py:12
  185.7 1.5 bitcast_select_fusion
  (3 shorter events, 0.0 us)
Async XLA Ops:
  0.0 1.6 copy-start
  0.0 8.1 %copy-start.3 = (bf16[4096,128]{1,0:T(8,128)(2,1)S(1)}, bf16[4096,128]{1,0:T(8,128)(2,1)}, u32[]{:S(2)}) copy-start(bf16[4096,128]{1,0:T(8,128)(2,1)} %param.4) | copy-start | bytes 3145732
  0.0 11.0 %copy-start.5 = (s32[32]{0:T(128)S(1)}, s32[32]{0:T(128)}, u32[]{:S(2)}) copy-start(s32[32]{0:T(128)} %param.7) | copy-start | bytes 388
  2.6 25.2 %collective-permute-start = (bf16[2048,256]{1,0:T(8,128)(2,1)}, bf16[2048,256]{1,0:T(8,128)(2,1)}, u32[]{:S(2)}, u32[]{:S(2)}) collective-permute-start(bf16[2048,256]{1,0:T(8,128)(2,1)} %dynamic-slice_bitcast_fusion.1), channel_id=1, source_target_pairs={{0,16},{16,0},{1,17},{17,1},{2,18},{18,2},{3,19},{19,3},{4,20},{20... | collective-permute-start | bytes 3145736 | tf_op jit(solution)/shard_map/ppermute | solution.py:12
  9.0 100.7 %collective-permute-start.1 = (bf16[2048,128]{1,0:T(8,128)(2,1)}, bf16[2048,128]{1,0:T(8,128)(2,1)S(1)}, u32[]{:S(2)}, u32[]{:S(2)}) collective-permute-start(bf16[2048,128]{1,0:T(8,128)(2,1)} %dynamic-slice_bitcast_fusion.2), channel_id=1, source_target_pairs={{0,16},{16,0},{1,17},{17,1},{2,18},{18,2},{3,19},{19,3},{4,20},{20... | collective-permute-start | bytes 1572872 | tf_op jit(solution)/shard_map/ppermute | solution.py:12
  105.5 3.6 %copy-start.1 = (u32[2,4,65536]{2,1,0:T(4,128)S(1)}, u32[2,4,65536]{2,1,0:T(4,128)}, u32[]{:S(2)}) copy-start(u32[2,4,65536]{2,1,0:T(4,128)} %all-reduce.1) | copy-start | bytes 6291460
  145.7 18.6 %all-to-all-start.1 = ((f32[32,24,256]{2,1,0:T(8,128)}), f32[32,24,256]{2,1,0:T(8,128)S(1)}, u32[]{:S(2)}, u32[]{:S(2)}) async-start(f32[32,24,256]{2,1,0:T(8,128)} %broadcast_in_dim.152), calls=%async_computation.1 | async-start | bytes 1572864 | tf_op jit(solution)/shard_map/all_to_all | solution.py:42
  164.3 4.9 %copy-start.2 = (u32[2,4,65536]{2,1,0:T(4,128)S(1)}, u32[2,4,65536]{2,1,0:T(4,128)}, u32[]{:S(2)}) copy-start(u32[2,4,65536]{2,1,0:T(4,128)} %all-reduce.1) | copy-start | bytes 6291460
  169.2 2.9 %copy-start.4 = (bf16[4096,128]{1,0:T(8,128)(2,1)S(1)}, bf16[4096,128]{1,0:T(8,128)(2,1)}, u32[]{:S(2)}) copy-start(bf16[4096,128]{1,0:T(8,128)(2,1)} %param.4) | copy-start | bytes 3145732
  169.7 16.1 %collective-permute-start.2 = (bf16[2048,128]{1,0:T(8,128)(2,1)S(1)}, bf16[2048,128]{1,0:T(8,128)(2,1)S(1)}, u32[]{:S(2)}, u32[]{:S(2)}) collective-permute-start(bf16[2048,128]{1,0:T(8,128)(2,1)S(1)} %subtract_convert_fusion), channel_id=1, source_target_pairs={{0,16},{16,0},{1,17},{17,1},{2,18},{18,2},{3,19},{19,3},{4,20},{20... | collective-permute-start | bytes 1572872 | tf_op jit(solution)/shard_map/ppermute | solution.py:12

commit v8 on v4

--- a/solution.py
+++ b/solution.py
@@ -5,7 +5,6 @@
 
 RING = 16
 HALVES = 2
-SUMMED = ("row", "half")
 SCALE = 2.0**21
 
 
@@ -24,11 +23,10 @@
 
 def spread_panels(own, other, owners, half):
     slot = owners[:2].reshape(2, 1, 1)
-    level = jnp.where(slot % RING == lax.axis_index("z"), SCALE, 0.0)
-    from_own = jnp.where(slot // RING == half, level, 0.0)
-    from_other = jnp.where(slot // RING == half, 0.0, level)
-    sent = own.astype(jnp.float32) * from_own + other.astype(jnp.float32) * from_other
-    return lax.psum(sent.astype(jnp.float16), "z").astype(jnp.bfloat16)
+    block = jnp.where(slot // RING == half, own[None], other[None])
+    sent = jnp.where(slot % RING == lax.axis_index("z"), block, jnp.zeros_like(block))
+    scaled = (sent.astype(jnp.float32) * SCALE).astype(jnp.float16)
+    return lax.psum(scaled, "z")
 
 
 def contract(left, right, dims):
@@ -56,9 +54,9 @@
     own, away = parts_of(reflectors, half)
     other = swap(away)
     mine, guest = parts_of(eigvecs, half)
-    other, guest = lax.optimization_barrier((other, guest))
     theirs = swap(guest)
-    panels = spread_panels(own, other, owners, half)
+    whole = spread_panels(own, other, owners, half)
+    panels = [whole[p].astype(jnp.bfloat16) for p in range(2)]
 
     blocks = []
     for p in range(2):
@@ -66,7 +64,7 @@
         there = contract(theirs, panels[p], ((0,), (0,)))
         blocks += [jnp.where(half == 0, here, there), jnp.where(half == 0, there, here)]
     cross = contract(panels[1], panels[0], ((0,), (0,)))
-    summed = sum_over(jnp.concatenate(blocks + [cross], axis=0), SUMMED)
+    summed = sum_over(jnp.concatenate(blocks + [cross], axis=0), ("row", "half"))
     count = HALVES * columns
     first = summed[:count] * (1 / SCALE)
     second = summed[count : 2 * count] * (1 / SCALE)

time: 186 us -> 179 us (0.962)
  other arithmetic: 9.64 us -> 3.47 us
  starting transfers between devices: 13.5 us -> 9.81 us
  local copies, waits for them, and re-layouts: 0.91 us -> 2.85 us
    ppermute x3, starting transfers between devices: 13.5 us -> 9.81 us  [swap(): return lax.ppermute(block, 'half', [(0, 1), (1, 0)])]
    convert_element_type x3 -> x1, other arithmetic: 5.6 us -> 2.32 us  [spread_panels(): scaled = (sent.astype(jnp.float32) * SCALE).astype(jnp.float16)]
    mul x1 -> x0, other arithmetic: 2.82 us -> none  [spread_panels(): own.astype(jnp.float32) * from_own + other.astype(jnp.float32) * from_other]
    broadcast_in_dim x0 -> x1, local copies, waits for them, and re-layouts: none -> 2.73 us  [spread_panels(): block = jnp.where(slot // RING == half, own[None], other[None])]
  transfers between devices with their start and end apart: 3 -> 3, of which waited for: 2 -> 2; matrix products, arithmetic and copies ran while one was open for 4% -> 2% of each run, Pallas kernels for 0% -> 0%
where the time goes in v8:
time: 179 us
  blocking collectives  126 us (70%)
  waiting for transfers between devices  30.9 us (17%)
  starting transfers between devices  9.81 us (5%)
  matrix products  5.97 us (3%)
  other arithmetic  3.47 us (2%)
  local copies, waits for them, and re-layouts  2.85 us (2%)
    psum x1, blocking collectives, spread_panels(): return lax.psum(scaled, 'z')  73.4 us
    all_to_all x1, blocking collectives, sum_over(): share = jnp.sum(lax.all_to_all(cut, axes, 0, 0), axis=0)  34.2 us
    ppermute x3, waiting for transfers between devices, swap(): return lax.ppermute(block, 'half', [(0, 1), (1, 0)])  30.9 us
    all_to_all x1, blocking collectives, sum_over(): return lax.all_to_all(spread, axes, 0, 0).reshape(part.shape)  18.1 us
    ppermute x3, starting transfers between devices, swap(): return lax.ppermute(block, 'half', [(0, 1), (1, 0)])  9.81 us
    dot_general x9, matrix products, contract(): lax.dot_general(left, right, (dims, ((), ())), preferred_element_type=jnp...  4.82 us
  transfers between devices with their start and end apart: 3, of which 2 were waited for; matrix products, arithmetic and copies ran while one was open for 2% of the time, Pallas kernels for 0%

profile of v8, /device:TPU:1, one launch (start us, length us, event | category | flops | bytes accessed | tf_op | source)
XLA Modules:
  0.0 179.0 jit_solution(16499757311144458232)
XLA Ops:
  0.0 0.0 copy-start
  0.0 0.0 copy-start.4
  0.0 2.7 %dynamic-slice_bitcast_fusion.1 = (bf16[2048,256]{1,0:T(8,128)(2,1)S(1)}, bf16[2048,256]{1,0:T(8,128)(2,1)}) fusion(bf16[2,2048,256]{2,1,0:T(8,128)(2,1)} %bitcast.86, s32[]{:T(128)S(6)} %select_n.70, s32[]{:T(128)S(6)} %select_n.73), kind=kLoop, calls=%fused_computation.19 | loop fusion | bytes 4194312 | tf_op jit(solution)/shard_map/jit(_where)/broadcast_in_dim | solution.py:26
  2.7 5.5 %collective-permute-start = (bf16[2048,256]{1,0:T(8,128)(2,1)}, bf16[2048,256]{1,0:T(8,128)(2,1)S(1)}, u32[]{:S(2)}, u32[]{:S(2)}) collective-permute-start(bf16[2048,256]{1,0:T(8,128)(2,1)} %get-tuple-element.6), channel_id=1, source_target_pairs={{0,16},{16,0},{1,17},{17,1},{2,18},{18,2},{3,19},{19,3},{4,20},{20... | collective-permute-start | bytes 3145736 | tf_op jit(solution)/shard_map/ppermute | solution.py:12
  8.2 0.0 copy-done
  8.3 1.9 %collective-permute-start.1 = (bf16[2048,128]{1,0:T(8,128)(2,1)S(1)}, bf16[2048,128]{1,0:T(8,128)(2,1)S(1)}, u32[]{:S(2)}, u32[]{:S(2)}) collective-permute-start(bf16[2048,128]{1,0:T(8,128)(2,1)S(1)} %dynamic-slice_bitcast_fusion.2), channel_id=1, source_target_pairs={{0,16},{16,0},{1,17},{17,1},{2,18},{18,2},{3,19},{19,3},{4,20},{20... | collective-permute-start | bytes 1572872 | tf_op jit(solution)/shard_map/ppermute | solution.py:12
  10.2 0.0 copy-done.4
  10.2 17.7 %collective-permute-done = bf16[2048,256]{1,0:T(8,128)(2,1)S(1)} collective-permute-done((bf16[2048,256]{1,0:T(8,128)(2,1)}, bf16[2048,256]{1,0:T(8,128)(2,1)S(1)}, u32[]{:S(2)}, u32[]{:S(2)}) %collective-permute-start) | collective-permute-done | bytes 1048608 | tf_op jit(solution)/shard_map/ppermute | solution.py:12
  27.9 2.3 %multiply_convert_fusion = f16[2,2048,256]{2,1,0:T(8,128)(2,1)} fusion(pred[2]{0:T(512)(128)(4,1)S(1)} %get-tuple-element.10, pred[2]{0:T(512)(128)(4,1)S(1)} %get-tuple-element.9, bf16[2048,256]{1,0:T(8,128)(2,1)S(1)} %collective-permute-done, bf16[2048,256]{1,0:T(8,128)(2,1)S(1)} %get-tuple-element.5), kind=kLoop, calls=%fused_computation | loop fusion | flops 5242880 | bytes 4194308 | tf_op jit(solution)/shard_map/convert_element_type | solution.py:28
  30.2 73.4 %all-reduce.1 = u32[2,4,65536]{2,1,0:T(4,128)S(1)} all-reduce(u32[2,4,65536]{2,1,0:T(4,128)} %bitcast.79), channel_id=1, replica_groups=mesh['row'=16,'half'=2,'z'=16] {'z'}, use_global_device_ids=true, to_apply=%region_0.1.clone | all-reduce | flops 524288 | bytes 4194304 | tf_op jit(solution)/shard_map/psum | solution.py:29
  103.7 0.0 collective-permute-done.1
  103.7 0.3 fusion.8
  104.0 0.0 copy-start.1
  104.0 1.5 select_dynamic-update-slice_fusion.3
  105.5 0.3 fusion.17
  105.9 0.0 copy-done.1
  105.9 0.4 select_dynamic-update-slice_fusion.1
  106.3 0.5 convolution_dynamic-update-slice_fusion
  106.8 34.2 %all_to_all.10 = f32[32,24,256]{2,1,0:T(8,128)S(1)} all-to-all(f32[32,24,256]{2,1,0:T(8,128)S(1)} %bitcast.89), channel_id=1, replica_groups=mesh['row'=16,'half'=2,'z'=16] {'row','half'}, dimensions={0} | all-to-all | bytes 1572864 | tf_op jit(solution)/shard_map/all_to_all | solution.py:39
  141.0 0.1 reduce_sum.9
  141.0 0.0 copy-start.3
  141.0 0.1 broadcast_in_dim.51
  141.1 18.1 %all_to_all.11 = f32[32,24,256]{2,1,0:T(8,128)S(1)} all-to-all(f32[32,24,256]{2,1,0:T(8,128)S(1)} %broadcast_in_dim.51), channel_id=1, replica_groups=mesh['row'=16,'half'=2,'z'=16] {'row','half'}, dimensions={0} | all-to-all | bytes 1572864 | tf_op jit(solution)/shard_map/all_to_all | solution.py:41
  159.2 0.0 copy-done.3
  159.2 0.4 convolution_convert_fusion.1
  159.6 0.3 convolution_subtract_fusion
  160.0 0.4 convolution_convert_fusion
  160.4 0.4 convolution_multiply_fusion
  160.8 0.0 copy-start.2
  160.8 0.4 subtract_convert_fusion
  161.3 2.4 %collective-permute-start.2 = (bf16[2048,128]{1,0:T(8,128)(2,1)S(1)}, bf16[2048,128]{1,0:T(8,128)(2,1)S(1)}, u32[]{:S(2)}, u32[]{:S(2)}) collective-permute-start(bf16[2048,128]{1,0:T(8,128)(2,1)S(1)} %subtract_convert_fusion), channel_id=1, source_target_pairs={{0,16},{16,0},{1,17},{17,1},{2,18},{18,2},{3,19},{19,3},{4,20},{20... | collective-permute-start | bytes 1572872 | tf_op jit(solution)/shard_map/ppermute | solution.py:12
  163.7 0.0 copy-done.2
  163.7 0.5 fusion.1
  164.2 13.2 %collective-permute-done.2 = bf16[2048,128]{1,0:T(8,128)(2,1)S(1)} collective-permute-done((bf16[2048,128]{1,0:T(8,128)(2,1)S(1)}, bf16[2048,128]{1,0:T(8,128)(2,1)S(1)}, u32[]{:S(2)}, u32[]{:S(2)}) %collective-permute-start.2) | collective-permute-done | bytes 524320 | tf_op jit(solution)/shard_map/ppermute | solution.py:12
  177.4 0.5 broadcast_select_fusion.1
  177.9 1.0 pad_maximum_fusion
  (4 shorter events, 0.1 us)
Async XLA Ops:
  0.0 8.2 %copy-start = (bf16[4096,128]{1,0:T(8,128)(2,1)S(1)}, bf16[4096,128]{1,0:T(8,128)(2,1)}, u32[]{:S(2)}) copy-start(bf16[4096,128]{1,0:T(8,128)(2,1)} %param.4) | copy-start | bytes 3145732
  0.0 10.2 %copy-start.4 = (s32[32]{0:T(128)S(1)}, s32[32]{0:T(128)}, u32[]{:S(2)}) copy-start(s32[32]{0:T(128)} %param.7) | copy-start | bytes 388
  2.7 25.2 %collective-permute-start = (bf16[2048,256]{1,0:T(8,128)(2,1)}, bf16[2048,256]{1,0:T(8,128)(2,1)S(1)}, u32[]{:S(2)}, u32[]{:S(2)}) collective-permute-start(bf16[2048,256]{1,0:T(8,128)(2,1)} %get-tuple-element.6), channel_id=1, source_target_pairs={{0,16},{16,0},{1,17},{17,1},{2,18},{18,2},{3,19},{19,3},{4,20},{20... | collective-permute-start | bytes 3145736 | tf_op jit(solution)/shard_map/ppermute | solution.py:12
  8.3 95.4 %collective-permute-start.1 = (bf16[2048,128]{1,0:T(8,128)(2,1)S(1)}, bf16[2048,128]{1,0:T(8,128)(2,1)S(1)}, u32[]{:S(2)}, u32[]{:S(2)}) collective-permute-start(bf16[2048,128]{1,0:T(8,128)(2,1)S(1)} %dynamic-slice_bitcast_fusion.2), channel_id=1, source_target_pairs={{0,16},{16,0},{1,17},{17,1},{2,18},{18,2},{3,19},{19,3},{4,20},{20... | collective-permute-start | bytes 1572872 | tf_op jit(solution)/shard_map/ppermute | solution.py:12
  104.0 1.9 %copy-start.1 = (bf16[4096,128]{1,0:T(8,128)(2,1)S(1)}, bf16[4096,128]{1,0:T(8,128)(2,1)}, u32[]{:S(2)}) copy-start(bf16[4096,128]{1,0:T(8,128)(2,1)} %param.4) | copy-start | bytes 3145732
  141.0 18.2 %copy-start.3 = (f32[2,256,256]{2,1,0:T(8,128)S(1)}, f32[2,256,256]{2,1,0:T(8,128)}, u32[]{:S(2)}) copy-start(f32[2,256,256]{2,1,0:T(8,128)} %param.6) | copy-start | bytes 1572868
  160.8 2.9 %copy-start.2 = (bf16[4096,128]{1,0:T(8,128)(2,1)S(1)}, bf16[4096,128]{1,0:T(8,128)(2,1)}, u32[]{:S(2)}) copy-start(bf16[4096,128]{1,0:T(8,128)(2,1)} %param.4) | copy-start | bytes 3145732
  161.3 16.1 %collective-permute-start.2 = (bf16[2048,128]{1,0:T(8,128)(2,1)S(1)}, bf16[2048,128]{1,0:T(8,128)(2,1)S(1)}, u32[]{:S(2)}, u32[]{:S(2)}) collective-permute-start(bf16[2048,128]{1,0:T(8,128)(2,1)S(1)} %subtract_convert_fusion), channel_id=1, source_target_pairs={{0,16},{16,0},{1,17},{17,1},{2,18},{18,2},{3,19},{19,3},{4,20},{20... | collective-permute-start | bytes 1572872 | tf_op jit(solution)/shard_map/ppermute | solution.py:12

commit v9 on v5

--- a/solution.py
+++ b/solution.py
@@ -33,22 +33,14 @@
     return lax.dot_general(left, right, (dims, ((), ())), preferred_element_type=jnp.float32)
 
 
-def sum_over(part, axes):
+def sum_over_rows(part):
+    axes = ("chip", "half")
     count = lax.axis_size(axes)
     cut = part.reshape((count, part.shape[0] // count) + part.shape[1:])
     share = jnp.sum(lax.all_to_all(cut, axes, 0, 0), axis=0)
+    share = share + swap(share, "core")
     spread = jnp.broadcast_to(share[None], (count,) + share.shape)
     return lax.all_to_all(spread, axes, 0, 0).reshape(part.shape)
-
-
-def sum_over_rows(part):
-    core = lax.axis_index("core")
-    keep, give = parts_of(part, core)
-    kept = sum_over(keep + swap(give, "core"), ("chip", "half"))
-    rest = swap(kept, "core")
-    return jnp.concatenate(
-        [jnp.where(core == 0, kept, rest), jnp.where(core == 0, rest, kept)], axis=0
-    )
 
 
 def exact(left, right):
@@ -93,9 +85,9 @@
 
     got = swap(updated(theirs, 1 - half))
     kept = updated(mine, half)
-    first_rows = jnp.where(half == 0, kept, got)
-    last_rows = jnp.where(half == 0, got, kept)
-    return jnp.concatenate([first_rows, last_rows], axis=0)
+    rows = kept.shape[0]
+    result = lax.dynamic_update_slice_in_dim(jnp.zeros_like(eigvecs), kept, half * rows, 0)
+    return lax.dynamic_update_slice_in_dim(result, got, (1 - half) * rows, 0)
 
 
 def solution(mesh):

time: 182 us -> 180 us (0.989)
  blocking collectives: 100 us -> 90 us
  waiting for transfers between devices: 33.8 us -> 40.6 us
  other arithmetic: 6.14 us -> 2.43 us
  starting transfers between devices: 30.2 us -> 32.2 us
  matrix products: 5.96 us -> 7.91 us
    all_to_all x0 -> x1, waiting for transfers between devices: none -> 12.6 us  [sum_over_rows(): return lax.all_to_all(spread, axes, 0, 0).reshape(part.shape)]
    all_to_all x2 -> x1, blocking collectives: 26.9 us -> 16.6 us  [sum_over_rows(): share = jnp.sum(lax.all_to_all(cut, axes, 0, 0), axis=0)]
    ppermute x5 -> x4, waiting for transfers between devices: 33.8 us -> 28 us  [swap(): return lax.ppermute(block, axis, [(0, 1), (1, 0)])]
    all_to_all x0 -> x1, starting transfers between devices: none -> 3.61 us  [sum_over_rows(): return lax.all_to_all(spread, axes, 0, 0).reshape(part.shape)]
    dot_general x3, matrix products: 1.15 us -> 3.04 us  [exact(): lax.dot_general(left, right, (((1,), (1,)), ((), ())), precision=lax.Prec...]
    ppermute x5 -> x4, starting transfers between devices: 30.2 us -> 28.6 us  [swap(): return lax.ppermute(block, axis, [(0, 1), (1, 0)])]
where the time goes in v9:
time: 180 us; the launch traced here: 178 us
  blocking collectives  90 us (50%)
  waiting for transfers between devices  40.6 us (23%)
  starting transfers between devices  32.2 us (18%)
  matrix products  7.91 us (4%)
  local copies, waits for them, and re-layouts  4.72 us (3%)
  other arithmetic  2.43 us (1%)
    psum x1, blocking collectives, spread_panels(): return lax.psum(scaled, 'z')  73.4 us
    ppermute x4, starting transfers between devices, swap(): return lax.ppermute(block, axis, [(0, 1), (1, 0)])  28.6 us
    ppermute x4, waiting for transfers between devices, swap(): return lax.ppermute(block, axis, [(0, 1), (1, 0)])  28 us
    all_to_all x1, blocking collectives, sum_over_rows(): share = jnp.sum(lax.all_to_all(cut, axes, 0, 0), axis=0)  16.6 us
    all_to_all x1, waiting for transfers between devices, sum_over_rows(): return lax.all_to_all(spread, axes, 0, 0).reshape(part.shape)  12.6 us
    dot_general x9, matrix products, contract(): lax.dot_general(left, right, (dims, ((), ())), preferred_element_type=jnp...  4.86 us
    all_to_all x1, starting transfers between devices, sum_over_rows(): return lax.all_to_all(spread, axes, 0, 0).reshape(part.shape)  3.61 us
  transfers between devices with their start and end apart: 5, of which 4 were waited for; matrix products, arithmetic and copies ran while one was open for 2% of the time, Pallas kernels for 0%

profile of v9, /device:TPU:1, one launch (start us, length us, event | category | flops | bytes accessed | tf_op | source)
XLA Modules:
  0.0 178.2 jit_solution(1814490615877849990)
XLA Ops:
  0.0 0.0 copy-start
  0.0 0.0 copy-start.4
  0.0 2.7 %dynamic-slice_bitcast_fusion.1 = (bf16[2048,256]{1,0:T(8,128)(2,1)S(1)}, bf16[2048,256]{1,0:T(8,128)(2,1)}) fusion(bf16[2,2048,256]{2,1,0:T(8,128)(2,1)} %bitcast.82, s32[]{:T(128)S(6)} %select_n.63, s32[]{:T(128)S(6)} %select_n.66), kind=kLoop, calls=%fused_computation.19 | loop fusion | bytes 4194312 | tf_op jit(solution)/shard_map/jit(_where)/broadcast_in_dim | solution.py:26
  2.7 5.5 %collective-permute-start = (bf16[2048,256]{1,0:T(8,128)(2,1)}, bf16[2048,256]{1,0:T(8,128)(2,1)S(1)}, u32[]{:S(2)}, u32[]{:S(2)}) collective-permute-start(bf16[2048,256]{1,0:T(8,128)(2,1)} %get-tuple-element.6), channel_id=1, source_target_pairs={{0,16},{16,0},{1,17},{17,1},{2,18},{18,2},{3,19},{19,3},{4,20},{20... | collective-permute-start | bytes 3145736 | tf_op jit(solution)/shard_map/ppermute | solution.py:12
  8.2 0.0 copy-done
  8.3 1.9 %collective-permute-start.1 = (bf16[2048,128]{1,0:T(8,128)(2,1)S(1)}, bf16[2048,128]{1,0:T(8,128)(2,1)S(1)}, u32[]{:S(2)}, u32[]{:S(2)}) collective-permute-start(bf16[2048,128]{1,0:T(8,128)(2,1)S(1)} %dynamic-slice_bitcast_fusion.2), channel_id=1, source_target_pairs={{0,16},{16,0},{1,17},{17,1},{2,18},{18,2},{3,19},{19,3},{4,20},{20... | collective-permute-start | bytes 1572872 | tf_op jit(solution)/shard_map/ppermute | solution.py:12
  10.2 0.0 copy-done.4
  10.2 17.7 %collective-permute-done = bf16[2048,256]{1,0:T(8,128)(2,1)S(1)} collective-permute-done((bf16[2048,256]{1,0:T(8,128)(2,1)}, bf16[2048,256]{1,0:T(8,128)(2,1)S(1)}, u32[]{:S(2)}, u32[]{:S(2)}) %collective-permute-start) | collective-permute-done | bytes 1048608 | tf_op jit(solution)/shard_map/ppermute | solution.py:12
  27.9 2.3 %multiply_convert_fusion = f16[2,2048,256]{2,1,0:T(8,128)(2,1)} fusion(pred[2]{0:T(512)(128)(4,1)S(1)} %get-tuple-element.8, pred[2]{0:T(512)(128)(4,1)S(1)} %get-tuple-element.7, bf16[2048,256]{1,0:T(8,128)(2,1)S(1)} %collective-permute-done, bf16[2048,256]{1,0:T(8,128)(2,1)S(1)} %get-tuple-element.5), kind=kLoop, calls=%fused_computation | loop fusion | flops 5242880 | bytes 4194308 | tf_op jit(solution)/shard_map/convert_element_type | solution.py:28
  30.2 73.4 %all-reduce.1 = u32[2,4,65536]{2,1,0:T(4,128)S(1)} all-reduce(u32[2,4,65536]{2,1,0:T(4,128)} %bitcast.75), channel_id=1, replica_groups=mesh['chip'=8,'core'=2,'half'=2,'z'=16] {'z'}, use_global_device_ids=true, to_apply=%region_0.1.clone | all-reduce | flops 524288 | bytes 4194304 | tf_op jit(solution)/shard_map/psum | solution.py:29
  103.7 0.0 collective-permute-done.1
  103.7 0.3 fusion.9
  104.0 0.0 copy-start.1
  104.0 1.5 select_dynamic-update-slice_fusion.3
  105.5 0.3 fusion.18
  105.9 0.0 copy-done.1
  105.9 0.4 select_dynamic-update-slice_fusion.1
  106.3 0.5 convolution_dynamic-update-slice_fusion
  106.8 16.6 %all_to_all.10 = f32[16,48,256]{2,1,0:T(8,128)S(1)} all-to-all(f32[16,48,256]{2,1,0:T(8,128)S(1)} %bitcast.85), channel_id=1, replica_groups=mesh['chip'=8,'core'=2,'half'=2,'z'=16] {'chip','half'}, dimensions={0} | all-to-all | bytes 1572864 | tf_op jit(solution)/shard_map/all_to_all | solution.py:40
  123.4 0.1 reduce_sum.9
  123.5 16.7 %collective-permute-start.2 = (f32[48,256]{1,0:T(8,128)S(1)}, f32[48,256]{1,0:T(8,128)S(1)}, u32[]{:S(2)}, u32[]{:S(2)}) collective-permute-start(f32[48,256]{1,0:T(8,128)S(1)} %reduce_sum.9), channel_id=1, source_target_pairs={{0,32},{32,0},{1,33},{33,1},{2,34},{34,2},{3,35},{35,3},{4,36},{36... | collective-permute-start | bytes 147464 | tf_op jit(solution)/shard_map/ppermute | solution.py:12
  140.2 0.9 collective-permute-done.2
  141.0 1.0 broadcast_in_dim.55
  142.0 3.6 %all-to-all-start.1 = ((f32[16,48,256]{2,1,0:T(8,128)}), f32[16,48,256]{2,1,0:T(8,128)S(1)}, u32[]{:S(2)}, u32[]{:S(2)}) async-start(f32[16,48,256]{2,1,0:T(8,128)} %broadcast_in_dim.55), calls=%async_computation.1 | async-start | bytes 1572864 | tf_op jit(solution)/shard_map/all_to_all | solution.py:43
  145.6 12.6 %all-to-all-done.1 = f32[16,48,256]{2,1,0:T(8,128)S(1)} async-done(((f32[16,48,256]{2,1,0:T(8,128)}), f32[16,48,256]{2,1,0:T(8,128)S(1)}, u32[]{:S(2)}, u32[]{:S(2)}) %all-to-all-start.1) | async-done | bytes 786464 | tf_op jit(solution)/shard_map/all_to_all | solution.py:43
  158.2 1.4 convolution_convert_fusion.1
  159.5 0.3 convolution_subtract_fusion
  159.9 1.4 convolution_convert_fusion
  161.2 0.4 convolution_multiply_fusion
  161.7 0.0 copy-start.2
  161.7 0.4 subtract_convert_fusion
  162.1 4.5 %collective-permute-start.3 = (bf16[2048,128]{1,0:T(8,128)(2,1)S(1)}, bf16[2048,128]{1,0:T(8,128)(2,1)S(1)}, u32[]{:S(2)}, u32[]{:S(2)}) collective-permute-start(bf16[2048,128]{1,0:T(8,128)(2,1)S(1)} %subtract_convert_fusion), channel_id=1, source_target_pairs={{0,16},{16,0},{1,17},{17,1},{2,18},{18,2},{3,19},{19,3},{4,20},{20... | collective-permute-start | bytes 1572872 | tf_op jit(solution)/shard_map/ppermute | solution.py:12
  166.7 0.0 copy-done.2
  166.7 0.4 fusion.1
  167.1 0.1 broadcast_in_dim.48
  167.3 0.6 fusion.3
  167.8 0.0 copy-start.3
  167.9 9.5 %collective-permute-done.3 = bf16[2048,128]{1,0:T(8,128)(2,1)S(1)} collective-permute-done((bf16[2048,128]{1,0:T(8,128)(2,1)S(1)}, bf16[2048,128]{1,0:T(8,128)(2,1)S(1)}, u32[]{:S(2)}, u32[]{:S(2)}) %collective-permute-start.3) | collective-permute-done | bytes 524320 | tf_op jit(solution)/shard_map/ppermute | solution.py:12
  177.3 0.0 copy-done.3
  177.3 0.8 constant_dynamic-update-slice_fusion
  (5 shorter events, 0.1 us)
Async XLA Ops:
  0.0 8.2 %copy-start = (bf16[4096,128]{1,0:T(8,128)(2,1)S(1)}, bf16[4096,128]{1,0:T(8,128)(2,1)}, u32[]{:S(2)}) copy-start(bf16[4096,128]{1,0:T(8,128)(2,1)} %param.4) | copy-start | bytes 3145732
  0.0 10.2 %copy-start.4 = (s32[32]{0:T(128)S(1)}, s32[32]{0:T(128)}, u32[]{:S(2)}) copy-start(s32[32]{0:T(128)} %param.7) | copy-start | bytes 388
  2.7 25.2 %collective-permute-start = (bf16[2048,256]{1,0:T(8,128)(2,1)}, bf16[2048,256]{1,0:T(8,128)(2,1)S(1)}, u32[]{:S(2)}, u32[]{:S(2)}) collective-permute-start(bf16[2048,256]{1,0:T(8,128)(2,1)} %get-tuple-element.6), channel_id=1, source_target_pairs={{0,16},{16,0},{1,17},{17,1},{2,18},{18,2},{3,19},{19,3},{4,20},{20... | collective-permute-start | bytes 3145736 | tf_op jit(solution)/shard_map/ppermute | solution.py:12
  8.3 95.4 %collective-permute-start.1 = (bf16[2048,128]{1,0:T(8,128)(2,1)S(1)}, bf16[2048,128]{1,0:T(8,128)(2,1)S(1)}, u32[]{:S(2)}, u32[]{:S(2)}) collective-permute-start(bf16[2048,128]{1,0:T(8,128)(2,1)S(1)} %dynamic-slice_bitcast_fusion.2), channel_id=1, source_target_pairs={{0,16},{16,0},{1,17},{17,1},{2,18},{18,2},{3,19},{19,3},{4,20},{20... | collective-permute-start | bytes 1572872 | tf_op jit(solution)/shard_map/ppermute | solution.py:12
  104.0 1.9 %copy-start.1 = (bf16[4096,128]{1,0:T(8,128)(2,1)S(1)}, bf16[4096,128]{1,0:T(8,128)(2,1)}, u32[]{:S(2)}) copy-start(bf16[4096,128]{1,0:T(8,128)(2,1)} %param.4) | copy-start | bytes 3145732
  123.5 17.6 %collective-permute-start.2 = (f32[48,256]{1,0:T(8,128)S(1)}, f32[48,256]{1,0:T(8,128)S(1)}, u32[]{:S(2)}, u32[]{:S(2)}) collective-permute-start(f32[48,256]{1,0:T(8,128)S(1)} %reduce_sum.9), channel_id=1, source_target_pairs={{0,32},{32,0},{1,33},{33,1},{2,34},{34,2},{3,35},{35,3},{4,36},{36... | collective-permute-start | bytes 147464 | tf_op jit(solution)/shard_map/ppermute | solution.py:12
  142.0 16.2 %all-to-all-start.1 = ((f32[16,48,256]{2,1,0:T(8,128)}), f32[16,48,256]{2,1,0:T(8,128)S(1)}, u32[]{:S(2)}, u32[]{:S(2)}) async-start(f32[16,48,256]{2,1,0:T(8,128)} %broadcast_in_dim.55), calls=%async_computation.1 | async-start | bytes 1572864 | tf_op jit(solution)/shard_map/all_to_all | solution.py:43
  161.7 5.0 %copy-start.2 = (bf16[4096,128]{1,0:T(8,128)(2,1)S(1)}, bf16[4096,128]{1,0:T(8,128)(2,1)}, u32[]{:S(2)}) copy-start(bf16[4096,128]{1,0:T(8,128)(2,1)} %param.4) | copy-start | bytes 3145732
  162.1 15.2 %collective-permute-start.3 = (bf16[2048,128]{1,0:T(8,128)(2,1)S(1)}, bf16[2048,128]{1,0:T(8,128)(2,1)S(1)}, u32[]{:S(2)}, u32[]{:S(2)}) collective-permute-start(bf16[2048,128]{1,0:T(8,128)(2,1)S(1)} %subtract_convert_fusion), channel_id=1, source_target_pairs={{0,16},{16,0},{1,17},{17,1},{2,18},{18,2},{3,19},{19,3},{4,20},{20... | collective-permute-start | bytes 1572872 | tf_op jit(solution)/shard_map/ppermute | solution.py:12
  167.8 9.5 %copy-start.3 = (bf16[4096,128]{1,0:T(8,128)(2,1)}, bf16[4096,128]{1,0:T(8,128)(2,1)S(1)}, u32[]{:S(2)}) copy-start(bf16[4096,128]{1,0:T(8,128)(2,1)S(1)} %fusion.3) | copy-start | bytes 3145732

commit v10 on v9

--- a/solution.py
+++ b/solution.py
@@ -86,8 +86,9 @@
     got = swap(updated(theirs, 1 - half))
     kept = updated(mine, half)
     rows = kept.shape[0]
-    result = lax.dynamic_update_slice_in_dim(jnp.zeros_like(eigvecs), kept, half * rows, 0)
-    return lax.dynamic_update_slice_in_dim(result, got, (1 - half) * rows, 0)
+    return lax.dynamic_update_slice_in_dim(
+        jnp.concatenate([kept, kept], axis=0), got, (1 - half) * rows, 0
+    )
 
 
 def solution(mesh):

time: 180 us -> 180 us (level)
  no operation moved by 1% of the time
where the time goes in v10:
time: 180 us; the launch traced here: 179 us
  blocking collectives  90 us (50%)
  waiting for transfers between devices  40.3 us (22%)
  starting transfers between devices  32.2 us (18%)
  matrix products  7.92 us (4%)
  local copies, waits for them, and re-layouts  4.58 us (3%)
  other arithmetic  3.47 us (2%)
    psum x1, blocking collectives, spread_panels(): return lax.psum(scaled, 'z')  73.4 us
    ppermute x4, starting transfers between devices, swap(): return lax.ppermute(block, axis, [(0, 1), (1, 0)])  28.6 us
    ppermute x4, waiting for transfers between devices, swap(): return lax.ppermute(block, axis, [(0, 1), (1, 0)])  27.7 us
    all_to_all x1, blocking collectives, sum_over_rows(): share = jnp.sum(lax.all_to_all(cut, axes, 0, 0), axis=0)  16.6 us
    all_to_all x1, waiting for transfers between devices, sum_over_rows(): return lax.all_to_all(spread, axes, 0, 0).reshape(part.shape)  12.6 us
    dot_general x9, matrix products, contract(): lax.dot_general(left, right, (dims, ((), ())), preferred_element_type=jnp...  4.78 us
    all_to_all x1, starting transfers between devices, sum_over_rows(): return lax.all_to_all(spread, axes, 0, 0).reshape(part.shape)  3.61 us
  transfers between devices with their start and end apart: 5, of which 4 were waited for; matrix products, arithmetic and copies ran while one was open for 2% of the time, Pallas kernels for 0%

profile of v10, /device:TPU:1, one launch (start us, length us, event | category | flops | bytes accessed | tf_op | source)
XLA Modules:
  0.0 178.7 jit_solution(5899248091093464162)
XLA Ops:
  0.0 0.0 copy-start
  0.0 0.0 copy-start.3
  0.0 2.7 %dynamic-slice_bitcast_fusion.1 = (bf16[2048,256]{1,0:T(8,128)(2,1)S(1)}, bf16[2048,256]{1,0:T(8,128)(2,1)}) fusion(bf16[2,2048,256]{2,1,0:T(8,128)(2,1)} %bitcast.82, s32[]{:T(128)S(6)} %select_n.60, s32[]{:T(128)S(6)} %select_n.63), kind=kLoop, calls=%fused_computation.19 | loop fusion | bytes 4194312 | tf_op jit(solution)/shard_map/jit(_where)/broadcast_in_dim | solution.py:26
  2.7 5.5 %collective-permute-start = (bf16[2048,256]{1,0:T(8,128)(2,1)}, bf16[2048,256]{1,0:T(8,128)(2,1)S(1)}, u32[]{:S(2)}, u32[]{:S(2)}) collective-permute-start(bf16[2048,256]{1,0:T(8,128)(2,1)} %get-tuple-element.6), channel_id=1, source_target_pairs={{0,16},{16,0},{1,17},{17,1},{2,18},{18,2},{3,19},{19,3},{4,20},{20... | collective-permute-start | bytes 3145736 | tf_op jit(solution)/shard_map/ppermute | solution.py:12
  8.2 0.0 copy-done
  8.3 1.9 %collective-permute-start.1 = (bf16[2048,128]{1,0:T(8,128)(2,1)S(1)}, bf16[2048,128]{1,0:T(8,128)(2,1)S(1)}, u32[]{:S(2)}, u32[]{:S(2)}) collective-permute-start(bf16[2048,128]{1,0:T(8,128)(2,1)S(1)} %dynamic-slice_bitcast_fusion.2), channel_id=1, source_target_pairs={{0,16},{16,0},{1,17},{17,1},{2,18},{18,2},{3,19},{19,3},{4,20},{20... | collective-permute-start | bytes 1572872 | tf_op jit(solution)/shard_map/ppermute | solution.py:12
  10.2 0.0 copy-done.3
  10.2 17.7 %collective-permute-done = bf16[2048,256]{1,0:T(8,128)(2,1)S(1)} collective-permute-done((bf16[2048,256]{1,0:T(8,128)(2,1)}, bf16[2048,256]{1,0:T(8,128)(2,1)S(1)}, u32[]{:S(2)}, u32[]{:S(2)}) %collective-permute-start) | collective-permute-done | bytes 1048608 | tf_op jit(solution)/shard_map/ppermute | solution.py:12
  27.9 2.3 %multiply_convert_fusion = f16[2,2048,256]{2,1,0:T(8,128)(2,1)} fusion(pred[2]{0:T(512)(128)(4,1)S(1)} %get-tuple-element.8, pred[2]{0:T(512)(128)(4,1)S(1)} %get-tuple-element.7, bf16[2048,256]{1,0:T(8,128)(2,1)S(1)} %collective-permute-done, bf16[2048,256]{1,0:T(8,128)(2,1)S(1)} %get-tuple-element.5), kind=kLoop, calls=%fused_computation | loop fusion | flops 5242880 | bytes 4194308 | tf_op jit(solution)/shard_map/convert_element_type | solution.py:28
  30.2 73.4 %all-reduce.1 = u32[2,4,65536]{2,1,0:T(4,128)S(1)} all-reduce(u32[2,4,65536]{2,1,0:T(4,128)} %bitcast.75), channel_id=1, replica_groups=mesh['chip'=8,'core'=2,'half'=2,'z'=16] {'z'}, use_global_device_ids=true, to_apply=%region_0.1.clone | all-reduce | flops 524288 | bytes 4194304 | tf_op jit(solution)/shard_map/psum | solution.py:29
  103.7 0.0 collective-permute-done.1
  103.7 0.3 fusion.8
  104.0 0.0 copy-start.1
  104.0 1.5 select_dynamic-update-slice_fusion.3
  105.5 0.3 fusion.17
  105.9 0.0 copy-done.1
  105.9 0.4 select_dynamic-update-slice_fusion.1
  106.3 0.5 convolution_dynamic-update-slice_fusion
  106.8 16.6 %all_to_all.10 = f32[16,48,256]{2,1,0:T(8,128)S(1)} all-to-all(f32[16,48,256]{2,1,0:T(8,128)S(1)} %bitcast.85), channel_id=1, replica_groups=mesh['chip'=8,'core'=2,'half'=2,'z'=16] {'chip','half'}, dimensions={0} | all-to-all | bytes 1572864 | tf_op jit(solution)/shard_map/all_to_all | solution.py:40
  123.4 0.1 reduce_sum.9
  123.5 16.7 %collective-permute-start.2 = (f32[48,256]{1,0:T(8,128)S(1)}, f32[48,256]{1,0:T(8,128)S(1)}, u32[]{:S(2)}, u32[]{:S(2)}) collective-permute-start(f32[48,256]{1,0:T(8,128)S(1)} %reduce_sum.9), channel_id=1, source_target_pairs={{0,32},{32,0},{1,33},{33,1},{2,34},{34,2},{3,35},{35,3},{4,36},{36... | collective-permute-start | bytes 147464 | tf_op jit(solution)/shard_map/ppermute | solution.py:12
  140.2 0.9 collective-permute-done.2
  141.0 1.0 broadcast_in_dim.51
  142.0 3.6 %all-to-all-start.1 = ((f32[16,48,256]{2,1,0:T(8,128)}), f32[16,48,256]{2,1,0:T(8,128)S(1)}, u32[]{:S(2)}, u32[]{:S(2)}) async-start(f32[16,48,256]{2,1,0:T(8,128)} %broadcast_in_dim.51), calls=%async_computation.1 | async-start | bytes 1572864 | tf_op jit(solution)/shard_map/all_to_all | solution.py:43
  145.6 12.6 %all-to-all-done.1 = f32[16,48,256]{2,1,0:T(8,128)S(1)} async-done(((f32[16,48,256]{2,1,0:T(8,128)}), f32[16,48,256]{2,1,0:T(8,128)S(1)}, u32[]{:S(2)}, u32[]{:S(2)}) %all-to-all-start.1) | async-done | bytes 786464 | tf_op jit(solution)/shard_map/all_to_all | solution.py:43
  158.2 0.0 copy-start.2
  158.2 1.4 convolution_convert_fusion.1
  159.6 0.3 convolution_subtract_fusion
  160.0 1.4 convolution_convert_fusion
  161.3 0.4 convolution_multiply_fusion
  161.8 0.0 copy-done.2
  161.8 0.5 fusion.1
  162.3 0.4 subtract_convert_fusion
  162.7 4.5 %collective-permute-start.3 = (bf16[2048,128]{1,0:T(8,128)(2,1)S(1)}, bf16[2048,128]{1,0:T(8,128)(2,1)S(1)}, u32[]{:S(2)}, u32[]{:S(2)}) collective-permute-start(bf16[2048,128]{1,0:T(8,128)(2,1)S(1)} %subtract_convert_fusion), channel_id=1, source_target_pairs={{0,16},{16,0},{1,17},{17,1},{2,18},{18,2},{3,19},{19,3},{4,20},{20... | collective-permute-start | bytes 1572872 | tf_op jit(solution)/shard_map/ppermute | solution.py:12
  167.2 0.4 fusion.2
  167.7 1.0 pad_maximum_fusion
  168.7 9.2 %collective-permute-done.3 = bf16[2048,128]{1,0:T(8,128)(2,1)S(1)} collective-permute-done((bf16[2048,128]{1,0:T(8,128)(2,1)S(1)}, bf16[2048,128]{1,0:T(8,128)(2,1)S(1)}, u32[]{:S(2)}, u32[]{:S(2)}) %collective-permute-start.3) | collective-permute-done | bytes 524320 | tf_op jit(solution)/shard_map/ppermute | solution.py:12
  177.9 0.8 constant_dynamic-update-slice_fusion
  (5 shorter events, 0.1 us)
Async XLA Ops:
  0.0 8.2 %copy-start = (bf16[4096,128]{1,0:T(8,128)(2,1)S(1)}, bf16[4096,128]{1,0:T(8,128)(2,1)}, u32[]{:S(2)}) copy-start(bf16[4096,128]{1,0:T(8,128)(2,1)} %param.4) | copy-start | bytes 3145732
  0.0 10.2 %copy-start.3 = (s32[32]{0:T(128)S(1)}, s32[32]{0:T(128)}, u32[]{:S(2)}) copy-start(s32[32]{0:T(128)} %param.7) | copy-start | bytes 388
  2.7 25.2 %collective-permute-start = (bf16[2048,256]{1,0:T(8,128)(2,1)}, bf16[2048,256]{1,0:T(8,128)(2,1)S(1)}, u32[]{:S(2)}, u32[]{:S(2)}) collective-permute-start(bf16[2048,256]{1,0:T(8,128)(2,1)} %get-tuple-element.6), channel_id=1, source_target_pairs={{0,16},{16,0},{1,17},{17,1},{2,18},{18,2},{3,19},{19,3},{4,20},{20... | collective-permute-start | bytes 3145736 | tf_op jit(solution)/shard_map/ppermute | solution.py:12
  8.3 95.4 %collective-permute-start.1 = (bf16[2048,128]{1,0:T(8,128)(2,1)S(1)}, bf16[2048,128]{1,0:T(8,128)(2,1)S(1)}, u32[]{:S(2)}, u32[]{:S(2)}) collective-permute-start(bf16[2048,128]{1,0:T(8,128)(2,1)S(1)} %dynamic-slice_bitcast_fusion.2), channel_id=1, source_target_pairs={{0,16},{16,0},{1,17},{17,1},{2,18},{18,2},{3,19},{19,3},{4,20},{20... | collective-permute-start | bytes 1572872 | tf_op jit(solution)/shard_map/ppermute | solution.py:12
  104.0 1.9 %copy-start.1 = (bf16[4096,128]{1,0:T(8,128)(2,1)S(1)}, bf16[4096,128]{1,0:T(8,128)(2,1)}, u32[]{:S(2)}) copy-start(bf16[4096,128]{1,0:T(8,128)(2,1)} %param.4) | copy-start | bytes 3145732
  123.5 17.6 %collective-permute-start.2 = (f32[48,256]{1,0:T(8,128)S(1)}, f32[48,256]{1,0:T(8,128)S(1)}, u32[]{:S(2)}, u32[]{:S(2)}) collective-permute-start(f32[48,256]{1,0:T(8,128)S(1)} %reduce_sum.9), channel_id=1, source_target_pairs={{0,32},{32,0},{1,33},{33,1},{2,34},{34,2},{3,35},{35,3},{4,36},{36... | collective-permute-start | bytes 147464 | tf_op jit(solution)/shard_map/ppermute | solution.py:12
  142.0 16.2 %all-to-all-start.1 = ((f32[16,48,256]{2,1,0:T(8,128)}), f32[16,48,256]{2,1,0:T(8,128)S(1)}, u32[]{:S(2)}, u32[]{:S(2)}) async-start(f32[16,48,256]{2,1,0:T(8,128)} %broadcast_in_dim.51), calls=%async_computation.1 | async-start | bytes 1572864 | tf_op jit(solution)/shard_map/all_to_all | solution.py:43
  158.2 3.6 %copy-start.2 = (bf16[4096,128]{1,0:T(8,128)(2,1)S(1)}, bf16[4096,128]{1,0:T(8,128)(2,1)}, u32[]{:S(2)}) copy-start(bf16[4096,128]{1,0:T(8,128)(2,1)} %param.4) | copy-start | bytes 3145732
  162.7 15.2 %collective-permute-start.3 = (bf16[2048,128]{1,0:T(8,128)(2,1)S(1)}, bf16[2048,128]{1,0:T(8,128)(2,1)S(1)}, u32[]{:S(2)}, u32[]{:S(2)}) collective-permute-start(bf16[2048,128]{1,0:T(8,128)(2,1)S(1)} %subtract_convert_fusion), channel_id=1, source_target_pairs={{0,16},{16,0},{1,17},{17,1},{2,18},{18,2},{3,19},{19,3},{4,20},{20... | collective-permute-start | bytes 1572872 | tf_op jit(solution)/shard_map/ppermute | solution.py:12

commit v11 on v9

--- a/solution.py
+++ b/solution.py
@@ -85,9 +85,8 @@
 
     got = swap(updated(theirs, 1 - half))
     kept = updated(mine, half)
-    rows = kept.shape[0]
-    result = lax.dynamic_update_slice_in_dim(jnp.zeros_like(eigvecs), kept, half * rows, 0)
-    return lax.dynamic_update_slice_in_dim(result, got, (1 - half) * rows, 0)
+    both = jnp.stack([kept, kept])
+    return lax.dynamic_update_index_in_dim(both, got, 1 - half, 0).reshape(eigvecs.shape)
 
 
 def solution(mesh):

time: 180 us -> 176 us (0.978)
  blocking collectives: 90 us -> 106 us
  waiting for transfers between devices: 40.6 us -> 28.9 us
  starting transfers between devices: 32.2 us -> 27.6 us
  matrix products: 7.91 us -> 5.91 us
    all_to_all x0 -> x1, blocking collectives: none -> 16.1 us  [sum_over_rows(): return lax.all_to_all(spread, axes, 0, 0).reshape(part.shape)]
    all_to_all x1 -> x0, waiting for transfers between devices: 12.6 us -> none  [sum_over_rows(): return lax.all_to_all(spread, axes, 0, 0).reshape(part.shape)]
    all_to_all x1 -> x0, starting transfers between devices: 3.61 us -> none  [sum_over_rows(): return lax.all_to_all(spread, axes, 0, 0).reshape(part.shape)]
    dot_general x3, matrix products: 3.04 us -> 1.15 us  [exact(): lax.dot_general(left, right, (((1,), (1,)), ((), ())), precision=lax.Prec...]
  transfers between devices with their start and end apart: 5 -> 4, of which waited for: 4 -> 3; matrix products, arithmetic and copies ran while one was open for 2% -> 2% of each run, Pallas kernels for 0% -> 0%
where the time goes in v11:
time: 176 us; the launch traced here: 175 us
  blocking collectives  106 us (60%)
  waiting for transfers between devices  28.9 us (16%)
  starting transfers between devices  27.6 us (16%)
  matrix products  5.91 us (3%)
  local copies, waits for them, and re-layouts  3.9 us (2%)
  other arithmetic  2.51 us (1%)
    psum x1, blocking collectives, spread_panels(): return lax.psum(scaled, 'z')  73.4 us
    ppermute x4, waiting for transfers between devices, swap(): return lax.ppermute(block, axis, [(0, 1), (1, 0)])  28.9 us
    ppermute x4, starting transfers between devices, swap(): return lax.ppermute(block, axis, [(0, 1), (1, 0)])  27.6 us
    all_to_all x1, blocking collectives, sum_over_rows(): share = jnp.sum(lax.all_to_all(cut, axes, 0, 0), axis=0)  16.6 us
    all_to_all x1, blocking collectives, sum_over_rows(): return lax.all_to_all(spread, axes, 0, 0).reshape(part.shape)  16.1 us
    dot_general x9, matrix products, contract(): lax.dot_general(left, right, (dims, ((), ())), preferred_element_type=jnp...  4.76 us
  transfers between devices with their start and end apart: 4, of which 3 were waited for; matrix products, arithmetic and copies ran while one was open for 2% of the time, Pallas kernels for 0%

profile of v11, /device:TPU:1, one launch (start us, length us, event | category | flops | bytes accessed | tf_op | source)
XLA Modules:
  0.0 175.2 jit_solution(1462733093594194761)
XLA Ops:
  0.0 0.0 copy-start
  0.0 0.0 copy-start.5
  0.0 2.7 %dynamic-slice_bitcast_fusion.1 = (bf16[2048,256]{1,0:T(8,128)(2,1)S(1)}, bf16[2048,256]{1,0:T(8,128)(2,1)}) fusion(bf16[2,2048,256]{2,1,0:T(8,128)(2,1)} %bitcast.87, s32[]{:T(128)S(6)} %select_n.59, s32[]{:T(128)S(6)} %select_n.62), kind=kLoop, calls=%fused_computation.20 | loop fusion | bytes 4194312 | tf_op jit(solution)/shard_map/jit(_where)/broadcast_in_dim | solution.py:26
  2.7 5.5 %collective-permute-start = (bf16[2048,256]{1,0:T(8,128)(2,1)}, bf16[2048,256]{1,0:T(8,128)(2,1)S(1)}, u32[]{:S(2)}, u32[]{:S(2)}) collective-permute-start(bf16[2048,256]{1,0:T(8,128)(2,1)} %get-tuple-element.6), channel_id=1, source_target_pairs={{0,16},{16,0},{1,17},{17,1},{2,18},{18,2},{3,19},{19,3},{4,20},{20... | collective-permute-start | bytes 3145736 | tf_op jit(solution)/shard_map/ppermute | solution.py:12
  8.2 0.0 copy-done
  8.3 1.9 %collective-permute-start.1 = (bf16[2048,128]{1,0:T(8,128)(2,1)S(1)}, bf16[2048,128]{1,0:T(8,128)(2,1)S(1)}, u32[]{:S(2)}, u32[]{:S(2)}) collective-permute-start(bf16[2048,128]{1,0:T(8,128)(2,1)S(1)} %dynamic-slice_bitcast_fusion.2), channel_id=1, source_target_pairs={{0,16},{16,0},{1,17},{17,1},{2,18},{18,2},{3,19},{19,3},{4,20},{20... | collective-permute-start | bytes 1572872 | tf_op jit(solution)/shard_map/ppermute | solution.py:12
  10.2 0.0 copy-done.5
  10.2 17.7 %collective-permute-done = bf16[2048,256]{1,0:T(8,128)(2,1)S(1)} collective-permute-done((bf16[2048,256]{1,0:T(8,128)(2,1)}, bf16[2048,256]{1,0:T(8,128)(2,1)S(1)}, u32[]{:S(2)}, u32[]{:S(2)}) %collective-permute-start) | collective-permute-done | bytes 1048608 | tf_op jit(solution)/shard_map/ppermute | solution.py:12
  27.9 2.3 %multiply_convert_fusion = f16[2,2048,256]{2,1,0:T(8,128)(2,1)} fusion(pred[2]{0:T(512)(128)(4,1)S(1)} %get-tuple-element.8, pred[2]{0:T(512)(128)(4,1)S(1)} %get-tuple-element.7, bf16[2048,256]{1,0:T(8,128)(2,1)S(1)} %collective-permute-done, bf16[2048,256]{1,0:T(8,128)(2,1)S(1)} %get-tuple-element.5), kind=kLoop, calls=%fused_computation | loop fusion | flops 5242880 | bytes 4194308 | tf_op jit(solution)/shard_map/convert_element_type | solution.py:28
  30.2 73.4 %all-reduce.1 = u32[2,4,65536]{2,1,0:T(4,128)S(1)} all-reduce(u32[2,4,65536]{2,1,0:T(4,128)} %bitcast.80), channel_id=1, replica_groups=mesh['chip'=8,'core'=2,'half'=2,'z'=16] {'z'}, use_global_device_ids=true, to_apply=%region_0.1.clone | all-reduce | flops 524288 | bytes 4194304 | tf_op jit(solution)/shard_map/psum | solution.py:29
  103.7 0.0 collective-permute-done.1
  103.7 0.3 fusion.9
  104.0 0.0 copy-start.1
  104.0 1.5 select_dynamic-update-slice_fusion.3
  105.5 0.3 fusion.18
  105.9 0.0 copy-done.1
  105.9 0.4 select_dynamic-update-slice_fusion.1
  106.3 0.5 convolution_dynamic-update-slice_fusion
  106.8 16.6 %all_to_all.10 = f32[16,48,256]{2,1,0:T(8,128)S(1)} all-to-all(f32[16,48,256]{2,1,0:T(8,128)S(1)} %bitcast.90), channel_id=1, replica_groups=mesh['chip'=8,'core'=2,'half'=2,'z'=16] {'chip','half'}, dimensions={0} | all-to-all | bytes 1572864 | tf_op jit(solution)/shard_map/all_to_all | solution.py:40
  123.4 0.1 reduce_sum.9
  123.5 0.0 copy-start.4
  123.5 16.8 %collective-permute-start.2 = (f32[48,256]{1,0:T(8,128)S(1)}, f32[48,256]{1,0:T(8,128)S(1)}, u32[]{:S(2)}, u32[]{:S(2)}) collective-permute-start(f32[48,256]{1,0:T(8,128)S(1)} %reduce_sum.9), channel_id=1, source_target_pairs={{0,32},{32,0},{1,33},{33,1},{2,34},{34,2},{3,35},{35,3},{4,36},{36... | collective-permute-start | bytes 147464 | tf_op jit(solution)/shard_map/ppermute | solution.py:12
  140.3 0.9 collective-permute-done.2
  141.2 0.1 broadcast_in_dim.55
  141.2 16.1 %all_to_all.11 = f32[16,48,256]{2,1,0:T(8,128)S(1)} all-to-all(f32[16,48,256]{2,1,0:T(8,128)S(1)} %broadcast_in_dim.55), channel_id=1, replica_groups=mesh['chip'=8,'core'=2,'half'=2,'z'=16] {'chip','half'}, dimensions={0} | all-to-all | bytes 1572864 | tf_op jit(solution)/shard_map/all_to_all | solution.py:43
  157.3 0.0 copy-done.4
  157.3 0.4 convolution_convert_fusion.1
  157.7 0.3 convolution_subtract_fusion
  158.1 0.4 convolution_convert_fusion
  158.5 0.4 convolution_multiply_fusion
  158.9 0.0 copy-start.2
  158.9 0.4 subtract_convert_fusion
  159.4 3.4 %collective-permute-start.3 = (bf16[2048,128]{1,0:T(8,128)(2,1)S(1)}, bf16[2048,128]{1,0:T(8,128)(2,1)S(1)}, u32[]{:S(2)}, u32[]{:S(2)}) collective-permute-start(bf16[2048,128]{1,0:T(8,128)(2,1)S(1)} %subtract_convert_fusion), channel_id=1, source_target_pairs={{0,16},{16,0},{1,17},{17,1},{2,18},{18,2},{3,19},{19,3},{4,20},{20... | collective-permute-start | bytes 1572872 | tf_op jit(solution)/shard_map/ppermute | solution.py:12
  162.8 0.0 copy-done.2
  162.8 0.4 fusion.1
  163.3 0.4 fusion.3
  163.7 0.1 pad_maximum_fusion
  163.8 10.4 %collective-permute-done.3 = bf16[2048,128]{1,0:T(8,128)(2,1)S(1)} collective-permute-done((bf16[2048,128]{1,0:T(8,128)(2,1)S(1)}, bf16[2048,128]{1,0:T(8,128)(2,1)S(1)}, u32[]{:S(2)}, u32[]{:S(2)}) %collective-permute-start.3) | collective-permute-done | bytes 524320 | tf_op jit(solution)/shard_map/ppermute | solution.py:12
  174.2 0.1 bitcast_dynamic-update-slice_fusion
  174.3 0.0 copy-start.3
  174.3 1.0 copy-done.3
  (5 shorter events, 0.1 us)
Async XLA Ops:
  0.0 8.2 %copy-start = (bf16[4096,128]{1,0:T(8,128)(2,1)S(1)}, bf16[4096,128]{1,0:T(8,128)(2,1)}, u32[]{:S(2)}) copy-start(bf16[4096,128]{1,0:T(8,128)(2,1)} %param.4) | copy-start | bytes 3145732
  0.0 10.2 %copy-start.5 = (s32[32]{0:T(128)S(1)}, s32[32]{0:T(128)}, u32[]{:S(2)}) copy-start(s32[32]{0:T(128)} %param.7) | copy-start | bytes 388
  2.7 25.2 %collective-permute-start = (bf16[2048,256]{1,0:T(8,128)(2,1)}, bf16[2048,256]{1,0:T(8,128)(2,1)S(1)}, u32[]{:S(2)}, u32[]{:S(2)}) collective-permute-start(bf16[2048,256]{1,0:T(8,128)(2,1)} %get-tuple-element.6), channel_id=1, source_target_pairs={{0,16},{16,0},{1,17},{17,1},{2,18},{18,2},{3,19},{19,3},{4,20},{20... | collective-permute-start | bytes 3145736 | tf_op jit(solution)/shard_map/ppermute | solution.py:12
  8.3 95.4 %collective-permute-start.1 = (bf16[2048,128]{1,0:T(8,128)(2,1)S(1)}, bf16[2048,128]{1,0:T(8,128)(2,1)S(1)}, u32[]{:S(2)}, u32[]{:S(2)}) collective-permute-start(bf16[2048,128]{1,0:T(8,128)(2,1)S(1)} %dynamic-slice_bitcast_fusion.2), channel_id=1, source_target_pairs={{0,16},{16,0},{1,17},{17,1},{2,18},{18,2},{3,19},{19,3},{4,20},{20... | collective-permute-start | bytes 1572872 | tf_op jit(solution)/shard_map/ppermute | solution.py:12
  104.0 1.9 %copy-start.1 = (bf16[4096,128]{1,0:T(8,128)(2,1)S(1)}, bf16[4096,128]{1,0:T(8,128)(2,1)}, u32[]{:S(2)}) copy-start(bf16[4096,128]{1,0:T(8,128)(2,1)} %param.4) | copy-start | bytes 3145732
  123.5 33.8 %copy-start.4 = (f32[2,256,256]{2,1,0:T(8,128)S(1)}, f32[2,256,256]{2,1,0:T(8,128)}, u32[]{:S(2)}) copy-start(f32[2,256,256]{2,1,0:T(8,128)} %param.6) | copy-start | bytes 1572868
  123.5 17.7 %collective-permute-start.2 = (f32[48,256]{1,0:T(8,128)S(1)}, f32[48,256]{1,0:T(8,128)S(1)}, u32[]{:S(2)}, u32[]{:S(2)}) collective-permute-start(f32[48,256]{1,0:T(8,128)S(1)} %reduce_sum.9), channel_id=1, source_target_pairs={{0,32},{32,0},{1,33},{33,1},{2,34},{34,2},{3,35},{35,3},{4,36},{36... | collective-permute-start | bytes 147464 | tf_op jit(solution)/shard_map/ppermute | solution.py:12
  158.9 3.9 %copy-start.2 = (bf16[4096,128]{1,0:T(8,128)(2,1)S(1)}, bf16[4096,128]{1,0:T(8,128)(2,1)}, u32[]{:S(2)}) copy-start(bf16[4096,128]{1,0:T(8,128)(2,1)} %param.4) | copy-start | bytes 3145732
  159.4 14.8 %collective-permute-start.3 = (bf16[2048,128]{1,0:T(8,128)(2,1)S(1)}, bf16[2048,128]{1,0:T(8,128)(2,1)S(1)}, u32[]{:S(2)}, u32[]{:S(2)}) collective-permute-start(bf16[2048,128]{1,0:T(8,128)(2,1)S(1)} %subtract_convert_fusion), channel_id=1, source_target_pairs={{0,16},{16,0},{1,17},{17,1},{2,18},{18,2},{3,19},{19,3},{4,20},{20... | collective-permute-start | bytes 1572872 | tf_op jit(solution)/shard_map/ppermute | solution.py:12
  174.3 1.0 copy-start.3

commit v12 on v11

--- a/solution.py
+++ b/solution.py
@@ -12,21 +12,20 @@
     return lax.ppermute(block, axis, [(0, 1), (1, 0)])
 
 
-def parts_of(tile, half):
+def part_of(tile, half):
     rows = tile.shape[0] // HALVES
-    halves = tile.reshape(HALVES, rows, tile.shape[1])
-    return (
-        lax.dynamic_index_in_dim(halves, half, 0, False),
-        lax.dynamic_index_in_dim(halves, 1 - half, 0, False),
-    )
+    return lax.dynamic_index_in_dim(tile.reshape(HALVES, rows, tile.shape[1]), half, 0, False)
+
+
+def scaled(block):
+    return (block.astype(jnp.float32) * SCALE).astype(jnp.float16)
 
 
 def spread_panels(own, other, owners, half):
     slot = owners[:2].reshape(2, 1, 1)
     block = jnp.where(slot // RING == half, own[None], other[None])
     sent = jnp.where(slot % RING == lax.axis_index("z"), block, jnp.zeros_like(block))
-    scaled = (sent.astype(jnp.float32) * SCALE).astype(jnp.float16)
-    return lax.psum(scaled, "z")
+    return lax.psum(sent, "z")
 
 
 def contract(left, right, dims):
@@ -53,11 +52,14 @@
 def per_device(eigvecs, reflectors, factors, owners):
     columns = eigvecs.shape[1]
     half = lax.axis_index("half")
-    own, away = parts_of(reflectors, half)
+    away = part_of(reflectors, 1 - half)
     other = swap(away)
-    mine, guest = parts_of(eigvecs, half)
-    theirs = swap(guest)
-    whole = spread_panels(own, other, owners, half)
+    reflectors, _ = lax.optimization_barrier((reflectors, away))
+    theirs = swap(part_of(eigvecs, 1 - half))
+    own = scaled(part_of(reflectors, half))
+    mine = part_of(eigvecs, half)
+    own, mine, other = lax.optimization_barrier((own, mine, other))
+    whole = spread_panels(own, scaled(other), owners, half)
     panels = [whole[p].astype(jnp.bfloat16) for p in range(2)]
 
     blocks = []

time: 176 us -> 176 us (level)
  other arithmetic: 2.51 us -> 6.5 us
  waiting for transfers between devices: 28.9 us -> 26.3 us
    broadcast_in_dim x1 -> x0, local copies, waits for them, and re-layouts: 2.73 us -> none  [spread_panels(): block = jnp.where(slot // RING == half, own[None], other[None])]
    ppermute x4, waiting for transfers between devices: 28.9 us -> 26.3 us  [swap(): return lax.ppermute(block, axis, [(0, 1), (1, 0)])]
    select_n x0 -> x1, other arithmetic: none -> 2.21 us  [spread_panels(): jnp.where(slot % RING == lax.axis_index('z'), block, jnp.zeros_like(block))]
    squeeze x1 -> x2, local copies, waits for them, and re-layouts: 0.04 us -> 2.25 us  [part_of(): lax.dynamic_index_in_dim(tile.reshape(HALVES, rows, tile.shape[1]), half,...]
  transfers between devices with their start and end apart: 4 -> 4, of which waited for: 3 -> 3; matrix products, arithmetic and copies ran while one was open for 2% -> 4% of each run, Pallas kernels for 0% -> 0%
where the time goes in v12:
time: 176 us; the launch traced here: 175 us
  blocking collectives  106 us (60%)
  starting transfers between devices  27.6 us (16%)
  waiting for transfers between devices  26.3 us (15%)
  other arithmetic  6.5 us (4%)
  matrix products  4.77 us (3%)
  local copies, waits for them, and re-layouts  3.37 us (2%)
    psum x1, blocking collectives, spread_panels(): return lax.psum(sent, 'z')  73.6 us
    ppermute x4, starting transfers between devices, swap(): return lax.ppermute(block, axis, [(0, 1), (1, 0)])  27.6 us
    ppermute x4, waiting for transfers between devices, swap(): return lax.ppermute(block, axis, [(0, 1), (1, 0)])  26.3 us
    all_to_all x1, blocking collectives, sum_over_rows(): share = jnp.sum(lax.all_to_all(cut, axes, 0, 0), axis=0)  16.7 us
    all_to_all x1, blocking collectives, sum_over_rows(): return lax.all_to_all(spread, axes, 0, 0).reshape(part.shape)  16.1 us
    dot_general x9, matrix products, contract(): lax.dot_general(left, right, (dims, ((), ())), preferred_element_type=jnp...  3.62 us
  transfers between devices with their start and end apart: 4, of which 3 were waited for; matrix products, arithmetic and copies ran while one was open for 4% of the time, Pallas kernels for 0%

profile of v12, /device:TPU:1, one launch (start us, length us, event | category | flops | bytes accessed | tf_op | source)
XLA Modules:
  0.0 175.2 jit_solution(15575904519543336534)
XLA Ops:
  0.0 0.0 copy-start.1
  0.0 0.0 copy-start.3
  0.0 1.4 dynamic-slice_bitcast_fusion
  1.4 5.5 %collective-permute-start = (bf16[2048,256]{1,0:T(8,128)(2,1)S(1)}, bf16[2048,256]{1,0:T(8,128)(2,1)}, u32[]{:S(2)}, u32[]{:S(2)}) collective-permute-start(bf16[2048,256]{1,0:T(8,128)(2,1)S(1)} %dynamic-slice_bitcast_fusion), channel_id=1, source_target_pairs={{0,16},{16,0},{1,17},{17,1},{2,18},{18,2},{3,19},{19,3},{4,20},{20... | collective-permute-start | bytes 3145736 | tf_op jit(solution)/shard_map/ppermute | solution.py:12
  6.9 0.0 copy-done.1
  6.9 0.9 dynamic-slice_bitcast_fusion.1
  7.8 1.9 %collective-permute-start.1 = (bf16[2048,128]{1,0:T(8,128)(2,1)}, bf16[2048,128]{1,0:T(8,128)(2,1)S(1)}, u32[]{:S(2)}, u32[]{:S(2)}) collective-permute-start(bf16[2048,128]{1,0:T(8,128)(2,1)} %get-tuple-element.13), channel_id=1, source_target_pairs={{0,16},{16,0},{1,17},{17,1},{2,18},{18,2},{3,19},{19,3},{4,20},{20... | collective-permute-start | bytes 1572872 | tf_op jit(solution)/shard_map/ppermute | solution.py:12
  9.7 0.0 copy-done.3
  9.7 1.5 fusion
  11.2 15.1 %collective-permute-done = bf16[2048,256]{1,0:T(8,128)(2,1)} collective-permute-done((bf16[2048,256]{1,0:T(8,128)(2,1)S(1)}, bf16[2048,256]{1,0:T(8,128)(2,1)}, u32[]{:S(2)}, u32[]{:S(2)}) %collective-permute-start) | collective-permute-done | bytes 1048608 | tf_op jit(solution)/shard_map/ppermute | solution.py:12
  26.3 1.5 multiply_convert_fusion
  27.7 2.2 %select_select_fusion = f16[2,2048,256]{2,1,0:T(8,128)(2,1)} fusion(pred[2]{0:T(512)(128)(4,1)S(1)} %get-tuple-element.16, pred[2]{0:T(512)(128)(4,1)S(1)} %get-tuple-element.15, f16[2048,256]{1,0:T(8,128)(2,1)S(1)} %multiply_convert_fusion, f16[2048,256]{1,0:T(8,128)(2,1)S(1)} %fusion), kind=kLoop, calls=%fused_computation.4 | loop fusion | flops 2097152 | bytes 4194308 | tf_op jit(solution)/shard_map/jit(_where)/select_n | solution.py:27
  30.0 73.6 %all-reduce.1 = u32[2,4,65536]{2,1,0:T(4,128)S(1)} all-reduce(u32[2,4,65536]{2,1,0:T(4,128)} %bitcast.79), channel_id=1, replica_groups=mesh['chip'=8,'core'=2,'half'=2,'z'=16] {'z'}, use_global_device_ids=true, to_apply=%region_0.1.clone | all-reduce | flops 524288 | bytes 4194304 | tf_op jit(solution)/shard_map/psum | solution.py:28
  103.6 0.0 collective-permute-done.1
  103.6 0.3 fusion.6
  104.0 0.3 select_dynamic-update-slice_fusion.3
  104.3 0.3 fusion.20
  104.7 0.3 select_dynamic-update-slice_fusion.1
  105.1 0.5 convolution_dynamic-update-slice_fusion
  105.5 16.7 %all_to_all.10 = f32[16,48,256]{2,1,0:T(8,128)} all-to-all(f32[16,48,256]{2,1,0:T(8,128)S(1)} %bitcast.86), channel_id=1, replica_groups=mesh['chip'=8,'core'=2,'half'=2,'z'=16] {'chip','half'}, dimensions={0} | all-to-all | bytes 1572864 | tf_op jit(solution)/shard_map/all_to_all | solution.py:39
  122.3 1.2 reduce_sum.9
  123.5 0.0 copy-start.2
  123.5 16.8 %collective-permute-start.2 = (f32[48,256]{1,0:T(8,128)S(1)}, f32[48,256]{1,0:T(8,128)S(1)}, u32[]{:S(2)}, u32[]{:S(2)}) collective-permute-start(f32[48,256]{1,0:T(8,128)S(1)} %reduce_sum.9), channel_id=1, source_target_pairs={{0,32},{32,0},{1,33},{33,1},{2,34},{34,2},{3,35},{35,3},{4,36},{36... | collective-permute-start | bytes 147464 | tf_op jit(solution)/shard_map/ppermute | solution.py:12
  140.3 0.9 collective-permute-done.2
  141.2 0.1 broadcast_in_dim.52
  141.2 16.1 %all_to_all.11 = f32[16,48,256]{2,1,0:T(8,128)S(1)} all-to-all(f32[16,48,256]{2,1,0:T(8,128)S(1)} %broadcast_in_dim.52), channel_id=1, replica_groups=mesh['chip'=8,'core'=2,'half'=2,'z'=16] {'chip','half'}, dimensions={0} | all-to-all | bytes 1572864 | tf_op jit(solution)/shard_map/all_to_all | solution.py:42
  157.3 0.0 copy-done.2
  157.3 0.4 convolution_convert_fusion.1
  157.7 0.3 convolution_subtract_fusion
  158.1 0.4 convolution_convert_fusion
  158.5 0.4 convolution_multiply_fusion
  158.9 0.4 subtract_convert_fusion
  159.4 3.4 %collective-permute-start.3 = (bf16[2048,128]{1,0:T(8,128)(2,1)S(1)}, bf16[2048,128]{1,0:T(8,128)(2,1)S(1)}, u32[]{:S(2)}, u32[]{:S(2)}) collective-permute-start(bf16[2048,128]{1,0:T(8,128)(2,1)S(1)} %subtract_convert_fusion), channel_id=1, source_target_pairs={{0,16},{16,0},{1,17},{17,1},{2,18},{18,2},{3,19},{19,3},{4,20},{20... | collective-permute-start | bytes 1572872 | tf_op jit(solution)/shard_map/ppermute | solution.py:12
  162.8 0.4 convolution_multiply_fusion.2
  163.2 0.4 fusion.14
  163.7 0.1 pad_maximum_fusion
  163.8 10.4 %collective-permute-done.3 = bf16[2048,128]{1,0:T(8,128)(2,1)S(1)} collective-permute-done((bf16[2048,128]{1,0:T(8,128)(2,1)S(1)}, bf16[2048,128]{1,0:T(8,128)(2,1)S(1)}, u32[]{:S(2)}, u32[]{:S(2)}) %collective-permute-start.3) | collective-permute-done | bytes 524320 | tf_op jit(solution)/shard_map/ppermute | solution.py:12
  174.2 0.1 bitcast_dynamic-update-slice_fusion
  174.3 0.0 copy-start
  174.3 1.0 copy-done
  (4 shorter events, 0.1 us)
Async XLA Ops:
  0.0 6.9 %copy-start.1 = (bf16[4096,128]{1,0:T(8,128)(2,1)S(1)}, bf16[4096,128]{1,0:T(8,128)(2,1)}, u32[]{:S(2)}) copy-start(bf16[4096,128]{1,0:T(8,128)(2,1)} %param.4) | copy-start | bytes 3145732
  0.0 9.7 %copy-start.3 = (s32[32]{0:T(128)S(1)}, s32[32]{0:T(128)}, u32[]{:S(2)}) copy-start(s32[32]{0:T(128)} %param.7) | copy-start | bytes 388
  1.4 24.9 %collective-permute-start = (bf16[2048,256]{1,0:T(8,128)(2,1)S(1)}, bf16[2048,256]{1,0:T(8,128)(2,1)}, u32[]{:S(2)}, u32[]{:S(2)}) collective-permute-start(bf16[2048,256]{1,0:T(8,128)(2,1)S(1)} %dynamic-slice_bitcast_fusion), channel_id=1, source_target_pairs={{0,16},{16,0},{1,17},{17,1},{2,18},{18,2},{3,19},{19,3},{4,20},{20... | collective-permute-start | bytes 3145736 | tf_op jit(solution)/shard_map/ppermute | solution.py:12
  7.8 95.8 %collective-permute-start.1 = (bf16[2048,128]{1,0:T(8,128)(2,1)}, bf16[2048,128]{1,0:T(8,128)(2,1)S(1)}, u32[]{:S(2)}, u32[]{:S(2)}) collective-permute-start(bf16[2048,128]{1,0:T(8,128)(2,1)} %get-tuple-element.13), channel_id=1, source_target_pairs={{0,16},{16,0},{1,17},{17,1},{2,18},{18,2},{3,19},{19,3},{4,20},{20... | collective-permute-start | bytes 1572872 | tf_op jit(solution)/shard_map/ppermute | solution.py:12
  123.5 33.8 %copy-start.2 = (f32[2,256,256]{2,1,0:T(8,128)S(1)}, f32[2,256,256]{2,1,0:T(8,128)}, u32[]{:S(2)}) copy-start(f32[2,256,256]{2,1,0:T(8,128)} %param.6) | copy-start | bytes 1572868
  123.5 17.7 %collective-permute-start.2 = (f32[48,256]{1,0:T(8,128)S(1)}, f32[48,256]{1,0:T(8,128)S(1)}, u32[]{:S(2)}, u32[]{:S(2)}) collective-permute-start(f32[48,256]{1,0:T(8,128)S(1)} %reduce_sum.9), channel_id=1, source_target_pairs={{0,32},{32,0},{1,33},{33,1},{2,34},{34,2},{3,35},{35,3},{4,36},{36... | collective-permute-start | bytes 147464 | tf_op jit(solution)/shard_map/ppermute | solution.py:12
  159.4 14.8 %collective-permute-start.3 = (bf16[2048,128]{1,0:T(8,128)(2,1)S(1)}, bf16[2048,128]{1,0:T(8,128)(2,1)S(1)}, u32[]{:S(2)}, u32[]{:S(2)}) collective-permute-start(bf16[2048,128]{1,0:T(8,128)(2,1)S(1)} %subtract_convert_fusion), channel_id=1, source_target_pairs={{0,16},{16,0},{1,17},{17,1},{2,18},{18,2},{3,19},{19,3},{4,20},{20... | collective-permute-start | bytes 1572872 | tf_op jit(solution)/shard_map/ppermute | solution.py:12
  174.3 1.0 copy-start

commit v13 on v12

--- a/solution.py
+++ b/solution.py
@@ -17,15 +17,12 @@
     return lax.dynamic_index_in_dim(tile.reshape(HALVES, rows, tile.shape[1]), half, 0, False)
 
 
-def scaled(block):
-    return (block.astype(jnp.float32) * SCALE).astype(jnp.float16)
-
-
 def spread_panels(own, other, owners, half):
     slot = owners[:2].reshape(2, 1, 1)
     block = jnp.where(slot // RING == half, own[None], other[None])
     sent = jnp.where(slot % RING == lax.axis_index("z"), block, jnp.zeros_like(block))
-    return lax.psum(sent, "z")
+    scaled = (sent.astype(jnp.float32) * SCALE).astype(jnp.float16)
+    return lax.psum(scaled, "z")
 
 
 def contract(left, right, dims):
@@ -56,10 +53,10 @@
     other = swap(away)
     reflectors, _ = lax.optimization_barrier((reflectors, away))
     theirs = swap(part_of(eigvecs, 1 - half))
-    own = scaled(part_of(reflectors, half))
+    own = part_of(reflectors, half)
     mine = part_of(eigvecs, half)
     own, mine, other = lax.optimization_barrier((own, mine, other))
-    whole = spread_panels(own, scaled(other), owners, half)
+    whole = spread_panels(own, other, owners, half)
     panels = [whole[p].astype(jnp.bfloat16) for p in range(2)]
 
     blocks = []

time: 176 us -> 181 us (1.028)
  matrix products: 4.77 us -> 7.36 us
  local copies, waits for them, and re-layouts: 3.37 us -> 5.9 us
    dot_general x9, matrix products: 3.62 us -> 6.22 us  [contract(): lax.dot_general(left, right, (dims, ((), ())), preferred_element_type=jnp...]
    select_n x1 -> x0, other arithmetic: 2.21 us -> none  [spread_panels(): jnp.where(slot % RING == lax.axis_index('z'), block, jnp.zeros_like(block))]
where the time goes in v13:
time: 181 us; the launch traced here: 180 us
  blocking collectives  107 us (59%)
  starting transfers between devices  27.6 us (15%)
  waiting for transfers between devices  26.8 us (15%)
  matrix products  7.36 us (4%)
  local copies, waits for them, and re-layouts  5.9 us (3%)
  other arithmetic  4.81 us (3%)
    psum x1, blocking collectives, spread_panels(): return lax.psum(scaled, 'z')  74.1 us
    ppermute x4, starting transfers between devices, swap(): return lax.ppermute(block, axis, [(0, 1), (1, 0)])  27.6 us
    ppermute x4, waiting for transfers between devices, swap(): return lax.ppermute(block, axis, [(0, 1), (1, 0)])  26.8 us
    all_to_all x1, blocking collectives, sum_over_rows(): share = jnp.sum(lax.all_to_all(cut, axes, 0, 0), axis=0)  16.7 us
    all_to_all x1, blocking collectives, sum_over_rows(): return lax.all_to_all(spread, axes, 0, 0).reshape(part.shape)  16.2 us
    dot_general x9, matrix products, contract(): lax.dot_general(left, right, (dims, ((), ())), preferred_element_type=jnp...  6.22 us
  transfers between devices with their start and end apart: 4, of which 3 were waited for; matrix products, arithmetic and copies ran while one was open for 4% of the time, Pallas kernels for 0%

profile of v13, /device:TPU:1, one launch (start us, length us, event | category | flops | bytes accessed | tf_op | source)
XLA Modules:
  0.0 179.8 jit_solution(8045430999423527169)
XLA Ops:
  0.0 0.0 copy-start
  0.0 1.6 copy-done
  1.6 0.0 copy-start.5
  1.6 1.0 dynamic-slice_bitcast_fusion.1
  2.6 5.5 %collective-permute-start = (bf16[2048,256]{1,0:T(8,128)(2,1)}, bf16[2048,256]{1,0:T(8,128)(2,1)}, u32[]{:S(2)}, u32[]{:S(2)}) collective-permute-start(bf16[2048,256]{1,0:T(8,128)(2,1)} %dynamic-slice_bitcast_fusion.1), channel_id=1, source_target_pairs={{0,16},{16,0},{1,17},{17,1},{2,18},{18,2},{3,19},{19,3},{4,20},{20... | collective-permute-start | bytes 3145736 | tf_op jit(solution)/shard_map/ppermute | solution.py:12
  8.1 2.1 %dynamic-slice_bitcast_fusion.2 = (bf16[2048,128]{1,0:T(8,128)(2,1)}, bf16[2048,128]{1,0:T(8,128)(2,1)S(1)}) fusion(bf16[2,2048,128]{2,1,0:T(8,128)(2,1)} %bitcast.87, s32[]{:T(128)S(6)} %select_n.59, s32[]{:T(128)S(6)} %select_n.60), kind=kLoop, calls=%fused_computation.24 | loop fusion | bytes 2097160 | tf_op jit(solution)/shard_map/jit(dynamic_index_in_dim)/squeeze | solution.py:17
  10.2 1.9 %collective-permute-start.1 = (bf16[2048,128]{1,0:T(8,128)(2,1)}, bf16[2048,128]{1,0:T(8,128)(2,1)S(1)}, u32[]{:S(2)}, u32[]{:S(2)}) collective-permute-start(bf16[2048,128]{1,0:T(8,128)(2,1)} %get-tuple-element.13), channel_id=1, source_target_pairs={{0,16},{16,0},{1,17},{17,1},{2,18},{18,2},{3,19},{19,3},{4,20},{20... | collective-permute-start | bytes 1572872 | tf_op jit(solution)/shard_map/ppermute | solution.py:12
  12.1 0.0 copy-done.5
  12.1 0.1 dynamic-slice_bitcast_fusion
  12.2 15.6 %collective-permute-done = bf16[2048,256]{1,0:T(8,128)(2,1)} collective-permute-done((bf16[2048,256]{1,0:T(8,128)(2,1)}, bf16[2048,256]{1,0:T(8,128)(2,1)}, u32[]{:S(2)}, u32[]{:S(2)}) %collective-permute-start) | collective-permute-done | bytes 1048608 | tf_op jit(solution)/shard_map/ppermute | solution.py:12
  27.8 3.5 %multiply_convert_fusion = f16[2,2048,256]{2,1,0:T(8,128)(2,1)} fusion(pred[2]{0:T(512)(128)(4,1)S(1)} %get-tuple-element.16, pred[2]{0:T(512)(128)(4,1)S(1)} %get-tuple-element.15, bf16[2048,256]{1,0:T(8,128)(2,1)} %collective-permute-done, bf16[2048,256]{1,0:T(8,128)(2,1)S(1)} %dynamic-slice_bitcast_fusion), kind=kLoop, calls=%fused_computation | loop fusion | flops 5242880 | bytes 4194308 | tf_op jit(solution)/shard_map/convert_element_type | solution.py:24
  31.3 74.1 %all-reduce.1 = u32[2,4,65536]{2,1,0:T(4,128)} all-reduce(u32[2,4,65536]{2,1,0:T(4,128)} %bitcast.81), channel_id=1, replica_groups=mesh['chip'=8,'core'=2,'half'=2,'z'=16] {'z'}, use_global_device_ids=true, to_apply=%region_0.1.clone | all-reduce | flops 524288 | bytes 4194304 | tf_op jit(solution)/shard_map/psum | solution.py:25
  105.4 0.0 copy-start.1
  105.4 0.0 collective-permute-done.1
  105.4 1.7 fusion.5
  107.1 1.6 select_dynamic-update-slice_fusion.3
  108.7 0.0 copy-done.1
  108.7 0.3 fusion.19
  109.1 0.3 select_dynamic-update-slice_fusion.1
  109.4 0.5 convolution_dynamic-update-slice_fusion
  109.9 16.7 %all_to_all.10 = f32[16,48,256]{2,1,0:T(8,128)} all-to-all(f32[16,48,256]{2,1,0:T(8,128)S(1)} %bitcast.86), channel_id=1, replica_groups=mesh['chip'=8,'core'=2,'half'=2,'z'=16] {'chip','half'}, dimensions={0} | all-to-all | bytes 1572864 | tf_op jit(solution)/shard_map/all_to_all | solution.py:36
  126.7 1.2 reduce_sum.9
  127.8 0.0 copy-start.4
  127.9 16.8 %collective-permute-start.2 = (f32[48,256]{1,0:T(8,128)S(1)}, f32[48,256]{1,0:T(8,128)S(1)}, u32[]{:S(2)}, u32[]{:S(2)}) collective-permute-start(f32[48,256]{1,0:T(8,128)S(1)} %reduce_sum.9), channel_id=1, source_target_pairs={{0,32},{32,0},{1,33},{33,1},{2,34},{34,2},{3,35},{35,3},{4,36},{36... | collective-permute-start | bytes 147464 | tf_op jit(solution)/shard_map/ppermute | solution.py:12
  144.7 0.9 collective-permute-done.2
  145.6 0.0 copy-start.2
  145.6 0.1 broadcast_in_dim.52
  145.6 16.2 %all_to_all.11 = f32[16,48,256]{2,1,0:T(8,128)S(1)} all-to-all(f32[16,48,256]{2,1,0:T(8,128)S(1)} %broadcast_in_dim.52), channel_id=1, replica_groups=mesh['chip'=8,'core'=2,'half'=2,'z'=16] {'chip','half'}, dimensions={0} | all-to-all | bytes 1572864 | tf_op jit(solution)/shard_map/all_to_all | solution.py:39
  161.8 0.0 copy-done.4
  161.8 0.4 convolution_convert_fusion.1
  162.2 0.3 convolution_subtract_fusion
  162.6 0.4 convolution_convert_fusion
  163.0 0.0 copy-done.2
  163.0 0.4 convolution_multiply_fusion
  163.4 0.4 subtract_convert_fusion
  163.9 3.4 %collective-permute-start.3 = (bf16[2048,128]{1,0:T(8,128)(2,1)S(1)}, bf16[2048,128]{1,0:T(8,128)(2,1)S(1)}, u32[]{:S(2)}, u32[]{:S(2)}) collective-permute-start(bf16[2048,128]{1,0:T(8,128)(2,1)S(1)} %subtract_convert_fusion), channel_id=1, source_target_pairs={{0,16},{16,0},{1,17},{17,1},{2,18},{18,2},{3,19},{19,3},{4,20},{20... | collective-permute-start | bytes 1572872 | tf_op jit(solution)/shard_map/ppermute | solution.py:12
  167.3 0.4 convolution_multiply_fusion.2
  167.8 0.4 fusion.13
  168.2 0.1 pad_maximum_fusion
  168.3 10.4 %collective-permute-done.3 = bf16[2048,128]{1,0:T(8,128)(2,1)S(1)} collective-permute-done((bf16[2048,128]{1,0:T(8,128)(2,1)S(1)}, bf16[2048,128]{1,0:T(8,128)(2,1)S(1)}, u32[]{:S(2)}, u32[]{:S(2)}) %collective-permute-start.3) | collective-permute-done | bytes 524320 | tf_op jit(solution)/shard_map/ppermute | solution.py:12
  178.7 0.1 bitcast_dynamic-update-slice_fusion
  178.8 0.0 copy-start.3
  178.8 1.0 copy-done.3
  (4 shorter events, 0.1 us)
Async XLA Ops:
  0.0 1.6 copy-start
  1.6 10.5 %copy-start.5 = (s32[32]{0:T(128)S(1)}, s32[32]{0:T(128)}, u32[]{:S(2)}) copy-start(s32[32]{0:T(128)} %param.7) | copy-start | bytes 388
  2.6 25.2 %collective-permute-start = (bf16[2048,256]{1,0:T(8,128)(2,1)}, bf16[2048,256]{1,0:T(8,128)(2,1)}, u32[]{:S(2)}, u32[]{:S(2)}) collective-permute-start(bf16[2048,256]{1,0:T(8,128)(2,1)} %dynamic-slice_bitcast_fusion.1), channel_id=1, source_target_pairs={{0,16},{16,0},{1,17},{17,1},{2,18},{18,2},{3,19},{19,3},{4,20},{20... | collective-permute-start | bytes 3145736 | tf_op jit(solution)/shard_map/ppermute | solution.py:12
  10.2 95.2 %collective-permute-start.1 = (bf16[2048,128]{1,0:T(8,128)(2,1)}, bf16[2048,128]{1,0:T(8,128)(2,1)S(1)}, u32[]{:S(2)}, u32[]{:S(2)}) collective-permute-start(bf16[2048,128]{1,0:T(8,128)(2,1)} %get-tuple-element.13), channel_id=1, source_target_pairs={{0,16},{16,0},{1,17},{17,1},{2,18},{18,2},{3,19},{19,3},{4,20},{20... | collective-permute-start | bytes 1572872 | tf_op jit(solution)/shard_map/ppermute | solution.py:12
  105.4 3.3 %copy-start.1 = (u32[2,4,65536]{2,1,0:T(4,128)S(1)}, u32[2,4,65536]{2,1,0:T(4,128)}, u32[]{:S(2)}) copy-start(u32[2,4,65536]{2,1,0:T(4,128)} %all-reduce.1) | copy-start | bytes 6291460
  127.8 34.0 %copy-start.4 = (f32[2,256,256]{2,1,0:T(8,128)S(1)}, f32[2,256,256]{2,1,0:T(8,128)}, u32[]{:S(2)}) copy-start(f32[2,256,256]{2,1,0:T(8,128)} %param.6) | copy-start | bytes 1572868
  127.9 17.7 %collective-permute-start.2 = (f32[48,256]{1,0:T(8,128)S(1)}, f32[48,256]{1,0:T(8,128)S(1)}, u32[]{:S(2)}, u32[]{:S(2)}) collective-permute-start(f32[48,256]{1,0:T(8,128)S(1)} %reduce_sum.9), channel_id=1, source_target_pairs={{0,32},{32,0},{1,33},{33,1},{2,34},{34,2},{3,35},{35,3},{4,36},{36... | collective-permute-start | bytes 147464 | tf_op jit(solution)/shard_map/ppermute | solution.py:12
  145.6 17.4 %copy-start.2 = (u32[2,4,65536]{2,1,0:T(4,128)S(1)}, u32[2,4,65536]{2,1,0:T(4,128)}, u32[]{:S(2)}) copy-start(u32[2,4,65536]{2,1,0:T(4,128)} %all-reduce.1) | copy-start | bytes 6291460
  163.9 14.8 %collective-permute-start.3 = (bf16[2048,128]{1,0:T(8,128)(2,1)S(1)}, bf16[2048,128]{1,0:T(8,128)(2,1)S(1)}, u32[]{:S(2)}, u32[]{:S(2)}) collective-permute-start(bf16[2048,128]{1,0:T(8,128)(2,1)S(1)} %subtract_convert_fusion), channel_id=1, source_target_pairs={{0,16},{16,0},{1,17},{17,1},{2,18},{18,2},{3,19},{19,3},{4,20},{20... | collective-permute-start | bytes 1572872 | tf_op jit(solution)/shard_map/ppermute | solution.py:12
  178.8 1.0 copy-start.3

commit v14 on v11

--- a/solution.py
+++ b/solution.py
@@ -57,6 +57,7 @@
     other = swap(away)
     mine, guest = parts_of(eigvecs, half)
     theirs = swap(guest)
+    mine, other = lax.optimization_barrier((mine, other))
     whole = spread_panels(own, other, owners, half)
     panels = [whole[p].astype(jnp.bfloat16) for p in range(2)]
 

time: 176 us -> 176 us (level)
  no operation moved by 1% of the time
where the time goes in v14:
time: 176 us; the launch traced here: 175 us
  blocking collectives  106 us (60%)
  waiting for transfers between devices  28.1 us (16%)
  starting transfers between devices  27.7 us (16%)
  matrix products  4.77 us (3%)
  local copies, waits for them, and re-layouts  4.72 us (3%)
  other arithmetic  3.65 us (2%)
    psum x1, blocking collectives, spread_panels(): return lax.psum(scaled, 'z')  73.4 us
    ppermute x4, waiting for transfers between devices, swap(): return lax.ppermute(block, axis, [(0, 1), (1, 0)])  28.1 us
    ppermute x4, starting transfers between devices, swap(): return lax.ppermute(block, axis, [(0, 1), (1, 0)])  27.7 us
    all_to_all x1, blocking collectives, sum_over_rows(): share = jnp.sum(lax.all_to_all(cut, axes, 0, 0), axis=0)  16.7 us
    all_to_all x1, blocking collectives, sum_over_rows(): return lax.all_to_all(spread, axes, 0, 0).reshape(part.shape)  16.1 us
    dot_general x9, matrix products, contract(): lax.dot_general(left, right, (dims, ((), ())), preferred_element_type=jnp...  3.63 us
  transfers between devices with their start and end apart: 4, of which 3 were waited for; matrix products, arithmetic and copies ran while one was open for 2% of the time, Pallas kernels for 0%

profile of v14, /device:TPU:1, one launch (start us, length us, event | category | flops | bytes accessed | tf_op | source)
XLA Modules:
  0.0 175.4 jit_solution(1596617137580458089)
XLA Ops:
  0.0 0.0 copy-start.1
  0.0 2.7 %dynamic-slice_bitcast_fusion = (bf16[2048,256]{1,0:T(8,128)(2,1)S(1)}, bf16[2048,256]{1,0:T(8,128)(2,1)}) fusion(bf16[2,2048,256]{2,1,0:T(8,128)(2,1)} %bitcast.81, s32[]{:T(128)S(6)} %select_n.59, s32[]{:T(128)S(6)} %select_n.60), kind=kLoop, calls=%fused_computation.16 | loop fusion | bytes 4194312 | tf_op jit(solution)/shard_map/jit(_where)/broadcast_in_dim | solution.py:26
  2.7 0.0 copy-start.3
  2.7 5.6 %collective-permute-start = (bf16[2048,256]{1,0:T(8,128)(2,1)}, bf16[2048,256]{1,0:T(8,128)(2,1)S(1)}, u32[]{:S(2)}, u32[]{:S(2)}) collective-permute-start(bf16[2048,256]{1,0:T(8,128)(2,1)} %get-tuple-element.10), channel_id=1, source_target_pairs={{0,16},{16,0},{1,17},{17,1},{2,18},{18,2},{3,19},{19,3},{4,20},{20... | collective-permute-start | bytes 3145736 | tf_op jit(solution)/shard_map/ppermute | solution.py:12
  8.3 0.0 copy-done.1
  8.4 0.9 dynamic-slice_bitcast_fusion.2
  9.2 1.9 %collective-permute-start.1 = (bf16[2048,128]{1,0:T(8,128)(2,1)}, bf16[2048,128]{1,0:T(8,128)(2,1)S(1)}, u32[]{:S(2)}, u32[]{:S(2)}) collective-permute-start(bf16[2048,128]{1,0:T(8,128)(2,1)} %get-tuple-element.11), channel_id=1, source_target_pairs={{0,16},{16,0},{1,17},{17,1},{2,18},{18,2},{3,19},{19,3},{4,20},{20... | collective-permute-start | bytes 1572872 | tf_op jit(solution)/shard_map/ppermute | solution.py:12
  11.2 0.0 copy-done.3
  11.2 16.9 %collective-permute-done = bf16[2048,256]{1,0:T(8,128)(2,1)S(1)} collective-permute-done((bf16[2048,256]{1,0:T(8,128)(2,1)}, bf16[2048,256]{1,0:T(8,128)(2,1)S(1)}, u32[]{:S(2)}, u32[]{:S(2)}) %collective-permute-start) | collective-permute-done | bytes 1048608 | tf_op jit(solution)/shard_map/ppermute | solution.py:12
  28.1 2.3 %multiply_convert_fusion = f16[2,2048,256]{2,1,0:T(8,128)(2,1)} fusion(pred[2]{0:T(512)(128)(4,1)S(1)} %get-tuple-element.14, pred[2]{0:T(512)(128)(4,1)S(1)} %get-tuple-element.13, bf16[2048,256]{1,0:T(8,128)(2,1)S(1)} %collective-permute-done, bf16[2048,256]{1,0:T(8,128)(2,1)S(1)} %get-tuple-element.9), kind=kLoop, calls=%fused_computation | loop fusion | flops 5242880 | bytes 4194308 | tf_op jit(solution)/shard_map/convert_element_type | solution.py:28
  30.4 73.4 %all-reduce.1 = u32[2,4,65536]{2,1,0:T(4,128)S(1)} all-reduce(u32[2,4,65536]{2,1,0:T(4,128)} %bitcast.78), channel_id=1, replica_groups=mesh['chip'=8,'core'=2,'half'=2,'z'=16] {'z'}, use_global_device_ids=true, to_apply=%region_0.1.clone | all-reduce | flops 524288 | bytes 4194304 | tf_op jit(solution)/shard_map/psum | solution.py:29
  103.8 0.0 collective-permute-done.1
  103.8 0.3 fusion.5
  104.2 0.3 select_dynamic-update-slice_fusion.3
  104.5 0.3 fusion.19
  104.9 0.3 select_dynamic-update-slice_fusion.1
  105.3 0.5 convolution_dynamic-update-slice_fusion
  105.7 16.7 %all_to_all.10 = f32[16,48,256]{2,1,0:T(8,128)} all-to-all(f32[16,48,256]{2,1,0:T(8,128)S(1)} %bitcast.84), channel_id=1, replica_groups=mesh['chip'=8,'core'=2,'half'=2,'z'=16] {'chip','half'}, dimensions={0} | all-to-all | bytes 1572864 | tf_op jit(solution)/shard_map/all_to_all | solution.py:40
  122.5 1.2 reduce_sum.9
  123.7 0.0 copy-start.2
  123.7 16.8 %collective-permute-start.2 = (f32[48,256]{1,0:T(8,128)S(1)}, f32[48,256]{1,0:T(8,128)S(1)}, u32[]{:S(2)}, u32[]{:S(2)}) collective-permute-start(f32[48,256]{1,0:T(8,128)S(1)} %reduce_sum.9), channel_id=1, source_target_pairs={{0,32},{32,0},{1,33},{33,1},{2,34},{34,2},{3,35},{35,3},{4,36},{36... | collective-permute-start | bytes 147464 | tf_op jit(solution)/shard_map/ppermute | solution.py:12
  140.5 0.9 collective-permute-done.2
  141.4 0.1 broadcast_in_dim.55
  141.4 16.1 %all_to_all.11 = f32[16,48,256]{2,1,0:T(8,128)S(1)} all-to-all(f32[16,48,256]{2,1,0:T(8,128)S(1)} %broadcast_in_dim.55), channel_id=1, replica_groups=mesh['chip'=8,'core'=2,'half'=2,'z'=16] {'chip','half'}, dimensions={0} | all-to-all | bytes 1572864 | tf_op jit(solution)/shard_map/all_to_all | solution.py:43
  157.5 0.0 copy-done.2
  157.5 0.4 convolution_convert_fusion.1
  157.9 0.3 convolution_subtract_fusion
  158.3 0.4 convolution_convert_fusion
  158.7 0.4 convolution_multiply_fusion
  159.1 0.4 subtract_convert_fusion
  159.6 3.4 %collective-permute-start.3 = (bf16[2048,128]{1,0:T(8,128)(2,1)S(1)}, bf16[2048,128]{1,0:T(8,128)(2,1)S(1)}, u32[]{:S(2)}, u32[]{:S(2)}) collective-permute-start(bf16[2048,128]{1,0:T(8,128)(2,1)S(1)} %subtract_convert_fusion), channel_id=1, source_target_pairs={{0,16},{16,0},{1,17},{17,1},{2,18},{18,2},{3,19},{19,3},{4,20},{20... | collective-permute-start | bytes 1572872 | tf_op jit(solution)/shard_map/ppermute | solution.py:12
  163.0 0.4 convolution_multiply_fusion.2
  163.5 0.4 fusion.13
  163.9 0.1 pad_maximum_fusion
  164.0 10.4 %collective-permute-done.3 = bf16[2048,128]{1,0:T(8,128)(2,1)S(1)} collective-permute-done((bf16[2048,128]{1,0:T(8,128)(2,1)S(1)}, bf16[2048,128]{1,0:T(8,128)(2,1)S(1)}, u32[]{:S(2)}, u32[]{:S(2)}) %collective-permute-start.3) | collective-permute-done | bytes 524320 | tf_op jit(solution)/shard_map/ppermute | solution.py:12
  174.4 0.1 bitcast_dynamic-update-slice_fusion
  174.5 0.0 copy-start
  174.5 1.0 copy-done
  (4 shorter events, 0.1 us)
Async XLA Ops:
  0.0 8.3 %copy-start.1 = (bf16[4096,128]{1,0:T(8,128)(2,1)S(1)}, bf16[4096,128]{1,0:T(8,128)(2,1)}, u32[]{:S(2)}) copy-start(bf16[4096,128]{1,0:T(8,128)(2,1)} %param.4) | copy-start | bytes 3145732
  2.7 8.4 %copy-start.3 = (s32[32]{0:T(128)S(1)}, s32[32]{0:T(128)}, u32[]{:S(2)}) copy-start(s32[32]{0:T(128)} %param.7) | copy-start | bytes 388
  2.7 25.3 %collective-permute-start = (bf16[2048,256]{1,0:T(8,128)(2,1)}, bf16[2048,256]{1,0:T(8,128)(2,1)S(1)}, u32[]{:S(2)}, u32[]{:S(2)}) collective-permute-start(bf16[2048,256]{1,0:T(8,128)(2,1)} %get-tuple-element.10), channel_id=1, source_target_pairs={{0,16},{16,0},{1,17},{17,1},{2,18},{18,2},{3,19},{19,3},{4,20},{20... | collective-permute-start | bytes 3145736 | tf_op jit(solution)/shard_map/ppermute | solution.py:12
  9.2 94.6 %collective-permute-start.1 = (bf16[2048,128]{1,0:T(8,128)(2,1)}, bf16[2048,128]{1,0:T(8,128)(2,1)S(1)}, u32[]{:S(2)}, u32[]{:S(2)}) collective-permute-start(bf16[2048,128]{1,0:T(8,128)(2,1)} %get-tuple-element.11), channel_id=1, source_target_pairs={{0,16},{16,0},{1,17},{17,1},{2,18},{18,2},{3,19},{19,3},{4,20},{20... | collective-permute-start | bytes 1572872 | tf_op jit(solution)/shard_map/ppermute | solution.py:12
  123.7 33.8 %copy-start.2 = (f32[2,256,256]{2,1,0:T(8,128)S(1)}, f32[2,256,256]{2,1,0:T(8,128)}, u32[]{:S(2)}) copy-start(f32[2,256,256]{2,1,0:T(8,128)} %param.6) | copy-start | bytes 1572868
  123.7 17.7 %collective-permute-start.2 = (f32[48,256]{1,0:T(8,128)S(1)}, f32[48,256]{1,0:T(8,128)S(1)}, u32[]{:S(2)}, u32[]{:S(2)}) collective-permute-start(f32[48,256]{1,0:T(8,128)S(1)} %reduce_sum.9), channel_id=1, source_target_pairs={{0,32},{32,0},{1,33},{33,1},{2,34},{34,2},{3,35},{35,3},{4,36},{36... | collective-permute-start | bytes 147464 | tf_op jit(solution)/shard_map/ppermute | solution.py:12
  159.6 14.8 %collective-permute-start.3 = (bf16[2048,128]{1,0:T(8,128)(2,1)S(1)}, bf16[2048,128]{1,0:T(8,128)(2,1)S(1)}, u32[]{:S(2)}, u32[]{:S(2)}) collective-permute-start(bf16[2048,128]{1,0:T(8,128)(2,1)S(1)} %subtract_convert_fusion), channel_id=1, source_target_pairs={{0,16},{16,0},{1,17},{17,1},{2,18},{18,2},{3,19},{19,3},{4,20},{20... | collective-permute-start | bytes 1572872 | tf_op jit(solution)/shard_map/ppermute | solution.py:12
  174.5 1.0 copy-start

commit v15 on v12

--- a/solution.py
+++ b/solution.py
@@ -18,14 +18,14 @@
 
 
 def scaled(block):
-    return (block.astype(jnp.float32) * SCALE).astype(jnp.float16)
+    return block.astype(jnp.float32) * SCALE
 
 
 def spread_panels(own, other, owners, half):
     slot = owners[:2].reshape(2, 1, 1)
     block = jnp.where(slot // RING == half, own[None], other[None])
     sent = jnp.where(slot % RING == lax.axis_index("z"), block, jnp.zeros_like(block))
-    return lax.psum(sent, "z")
+    return lax.psum(sent.astype(jnp.float16), "z")
 
 
 def contract(left, right, dims):

time: 176 us -> 177 us (level)
    mul x0 -> x2, other arithmetic: none -> 2.73 us  [scaled(): return block.astype(jnp.float32) * SCALE]
    select_n x1 -> x0, other arithmetic: 2.21 us -> none  [spread_panels(): jnp.where(slot % RING == lax.axis_index('z'), block, jnp.zeros_like(block))]
where the time goes in v15:
time: 177 us; the launch traced here: 176 us
  blocking collectives  106 us (60%)
  starting transfers between devices  27.6 us (16%)
  waiting for transfers between devices  26.8 us (15%)
  other arithmetic  5.96 us (3%)
  matrix products  4.78 us (3%)
  local copies, waits for them, and re-layouts  4.34 us (2%)
    psum x1, blocking collectives, spread_panels(): return lax.psum(sent.astype(jnp.float16), 'z')  73.5 us
    ppermute x4, starting transfers between devices, swap(): return lax.ppermute(block, axis, [(0, 1), (1, 0)])  27.6 us
    ppermute x4, waiting for transfers between devices, swap(): return lax.ppermute(block, axis, [(0, 1), (1, 0)])  26.8 us
    all_to_all x1, blocking collectives, sum_over_rows(): share = jnp.sum(lax.all_to_all(cut, axes, 0, 0), axis=0)  16.7 us
    all_to_all x1, blocking collectives, sum_over_rows(): return lax.all_to_all(spread, axes, 0, 0).reshape(part.shape)  16.1 us
    dot_general x9, matrix products, contract(): lax.dot_general(left, right, (dims, ((), ())), preferred_element_type=jnp...  3.63 us
  transfers between devices with their start and end apart: 4, of which 3 were waited for; matrix products, arithmetic and copies ran while one was open for 4% of the time, Pallas kernels for 0%

profile of v15, /device:TPU:1, one launch (start us, length us, event | category | flops | bytes accessed | tf_op | source)
XLA Modules:
  0.0 176.0 jit_solution(17409410093042985715)
XLA Ops:
  0.0 0.0 copy-start.1
  0.0 0.0 copy-start.3
  0.0 2.3 %dynamic-slice_bitcast_fusion = bf16[2048,256]{1,0:T(8,128)(2,1)} fusion(bf16[2,2048,256]{2,1,0:T(8,128)(2,1)} %bitcast.82, s32[]{:T(128)S(6)} %select_n.59), kind=kLoop, calls=%fused_computation.18 | loop fusion | bytes 2097156 | tf_op jit(solution)/shard_map/jit(dynamic_index_in_dim)/squeeze | solution.py:17
  2.4 5.5 %collective-permute-start = (bf16[2048,256]{1,0:T(8,128)(2,1)}, bf16[2048,256]{1,0:T(8,128)(2,1)}, u32[]{:S(2)}, u32[]{:S(2)}) collective-permute-start(bf16[2048,256]{1,0:T(8,128)(2,1)} %dynamic-slice_bitcast_fusion), channel_id=1, source_target_pairs={{0,16},{16,0},{1,17},{17,1},{2,18},{18,2},{3,19},{19,3},{4,20},{20... | collective-permute-start | bytes 3145736 | tf_op jit(solution)/shard_map/ppermute | solution.py:12
  7.8 0.0 copy-done.1
  7.8 0.9 dynamic-slice_bitcast_fusion.1
  8.7 1.9 %collective-permute-start.1 = (bf16[2048,128]{1,0:T(8,128)(2,1)}, bf16[2048,128]{1,0:T(8,128)(2,1)S(1)}, u32[]{:S(2)}, u32[]{:S(2)}) collective-permute-start(bf16[2048,128]{1,0:T(8,128)(2,1)} %get-tuple-element.13), channel_id=1, source_target_pairs={{0,16},{16,0},{1,17},{17,1},{2,18},{18,2},{3,19},{19,3},{4,20},{20... | collective-permute-start | bytes 1572872 | tf_op jit(solution)/shard_map/ppermute | solution.py:12
  10.6 0.0 copy-done.3
  10.7 1.4 multiply_bitcast_fusion
  12.0 15.5 %collective-permute-done = bf16[2048,256]{1,0:T(8,128)(2,1)} collective-permute-done((bf16[2048,256]{1,0:T(8,128)(2,1)}, bf16[2048,256]{1,0:T(8,128)(2,1)}, u32[]{:S(2)}, u32[]{:S(2)}) %collective-permute-start) | collective-permute-done | bytes 1048608 | tf_op jit(solution)/shard_map/ppermute | solution.py:12
  27.5 1.4 convert_multiply_fusion
  28.9 1.9 %select_convert_fusion = f16[2,2048,256]{2,1,0:T(8,128)(2,1)} fusion(f32[2048,256]{1,0:T(8,128)S(1)} %convert_multiply_fusion, f32[2048,256]{1,0:T(8,128)S(1)} %multiply_bitcast_fusion, pred[2]{0:T(512)(128)(4,1)S(1)} %get-tuple-element.16, pred[2]{0:T(512)(128)(4,1)S(1)} %get-tuple-element.15), kind=kLoop, calls=%fused_computation | loop fusion | flops 3145728 | bytes 6291460 | tf_op jit(solution)/shard_map/convert_element_type | solution.py:28
  30.8 73.5 %all-reduce.1 = u32[2,4,65536]{2,1,0:T(4,128)S(1)} all-reduce(u32[2,4,65536]{2,1,0:T(4,128)} %bitcast.79), channel_id=1, replica_groups=mesh['chip'=8,'core'=2,'half'=2,'z'=16] {'z'}, use_global_device_ids=true, to_apply=%region_0.1.clone | all-reduce | flops 524288 | bytes 4194304 | tf_op jit(solution)/shard_map/psum | solution.py:28
  104.3 0.0 collective-permute-done.1
  104.3 0.3 fusion.5
  104.7 0.3 select_dynamic-update-slice_fusion.3
  105.1 0.3 fusion.19
  105.4 0.3 select_dynamic-update-slice_fusion.1
  105.8 0.5 convolution_dynamic-update-slice_fusion
  106.3 16.7 %all_to_all.10 = f32[16,48,256]{2,1,0:T(8,128)} all-to-all(f32[16,48,256]{2,1,0:T(8,128)S(1)} %bitcast.86), channel_id=1, replica_groups=mesh['chip'=8,'core'=2,'half'=2,'z'=16] {'chip','half'}, dimensions={0} | all-to-all | bytes 1572864 | tf_op jit(solution)/shard_map/all_to_all | solution.py:39
  123.0 1.2 reduce_sum.9
  124.2 0.0 copy-start.2
  124.2 16.8 %collective-permute-start.2 = (f32[48,256]{1,0:T(8,128)S(1)}, f32[48,256]{1,0:T(8,128)S(1)}, u32[]{:S(2)}, u32[]{:S(2)}) collective-permute-start(f32[48,256]{1,0:T(8,128)S(1)} %reduce_sum.9), channel_id=1, source_target_pairs={{0,32},{32,0},{1,33},{33,1},{2,34},{34,2},{3,35},{35,3},{4,36},{36... | collective-permute-start | bytes 147464 | tf_op jit(solution)/shard_map/ppermute | solution.py:12
  141.0 0.9 collective-permute-done.2
  141.9 0.1 broadcast_in_dim.52
  142.0 16.1 %all_to_all.11 = f32[16,48,256]{2,1,0:T(8,128)S(1)} all-to-all(f32[16,48,256]{2,1,0:T(8,128)S(1)} %broadcast_in_dim.52), channel_id=1, replica_groups=mesh['chip'=8,'core'=2,'half'=2,'z'=16] {'chip','half'}, dimensions={0} | all-to-all | bytes 1572864 | tf_op jit(solution)/shard_map/all_to_all | solution.py:42
  158.0 0.0 copy-done.2
  158.0 0.4 convolution_convert_fusion.1
  158.5 0.3 convolution_subtract_fusion
  158.8 0.4 convolution_convert_fusion
  159.2 0.4 convolution_multiply_fusion
  159.7 0.4 subtract_convert_fusion
  160.1 3.4 %collective-permute-start.3 = (bf16[2048,128]{1,0:T(8,128)(2,1)S(1)}, bf16[2048,128]{1,0:T(8,128)(2,1)S(1)}, u32[]{:S(2)}, u32[]{:S(2)}) collective-permute-start(bf16[2048,128]{1,0:T(8,128)(2,1)S(1)} %subtract_convert_fusion), channel_id=1, source_target_pairs={{0,16},{16,0},{1,17},{17,1},{2,18},{18,2},{3,19},{19,3},{4,20},{20... | collective-permute-start | bytes 1572872 | tf_op jit(solution)/shard_map/ppermute | solution.py:12
  163.5 0.4 convolution_multiply_fusion.2
  164.0 0.4 fusion.13
  164.4 0.1 pad_maximum_fusion
  164.5 10.4 %collective-permute-done.3 = bf16[2048,128]{1,0:T(8,128)(2,1)S(1)} collective-permute-done((bf16[2048,128]{1,0:T(8,128)(2,1)S(1)}, bf16[2048,128]{1,0:T(8,128)(2,1)S(1)}, u32[]{:S(2)}, u32[]{:S(2)}) %collective-permute-start.3) | collective-permute-done | bytes 524320 | tf_op jit(solution)/shard_map/ppermute | solution.py:12
  174.9 0.1 bitcast_dynamic-update-slice_fusion
  175.0 0.0 copy-start
  175.0 1.0 copy-done
  (4 shorter events, 0.1 us)
Async XLA Ops:
  0.0 7.8 %copy-start.1 = (bf16[4096,128]{1,0:T(8,128)(2,1)S(1)}, bf16[4096,128]{1,0:T(8,128)(2,1)}, u32[]{:S(2)}) copy-start(bf16[4096,128]{1,0:T(8,128)(2,1)} %param.4) | copy-start | bytes 3145732
  0.0 10.6 %copy-start.3 = (s32[32]{0:T(128)S(1)}, s32[32]{0:T(128)}, u32[]{:S(2)}) copy-start(s32[32]{0:T(128)} %param.7) | copy-start | bytes 388
  2.4 25.2 %collective-permute-start = (bf16[2048,256]{1,0:T(8,128)(2,1)}, bf16[2048,256]{1,0:T(8,128)(2,1)}, u32[]{:S(2)}, u32[]{:S(2)}) collective-permute-start(bf16[2048,256]{1,0:T(8,128)(2,1)} %dynamic-slice_bitcast_fusion), channel_id=1, source_target_pairs={{0,16},{16,0},{1,17},{17,1},{2,18},{18,2},{3,19},{19,3},{4,20},{20... | collective-permute-start | bytes 3145736 | tf_op jit(solution)/shard_map/ppermute | solution.py:12
  8.7 95.6 %collective-permute-start.1 = (bf16[2048,128]{1,0:T(8,128)(2,1)}, bf16[2048,128]{1,0:T(8,128)(2,1)S(1)}, u32[]{:S(2)}, u32[]{:S(2)}) collective-permute-start(bf16[2048,128]{1,0:T(8,128)(2,1)} %get-tuple-element.13), channel_id=1, source_target_pairs={{0,16},{16,0},{1,17},{17,1},{2,18},{18,2},{3,19},{19,3},{4,20},{20... | collective-permute-start | bytes 1572872 | tf_op jit(solution)/shard_map/ppermute | solution.py:12
  124.2 33.8 %copy-start.2 = (f32[2,256,256]{2,1,0:T(8,128)S(1)}, f32[2,256,256]{2,1,0:T(8,128)}, u32[]{:S(2)}) copy-start(f32[2,256,256]{2,1,0:T(8,128)} %param.6) | copy-start | bytes 1572868
  124.2 17.7 %collective-permute-start.2 = (f32[48,256]{1,0:T(8,128)S(1)}, f32[48,256]{1,0:T(8,128)S(1)}, u32[]{:S(2)}, u32[]{:S(2)}) collective-permute-start(f32[48,256]{1,0:T(8,128)S(1)} %reduce_sum.9), channel_id=1, source_target_pairs={{0,32},{32,0},{1,33},{33,1},{2,34},{34,2},{3,35},{35,3},{4,36},{36... | collective-permute-start | bytes 147464 | tf_op jit(solution)/shard_map/ppermute | solution.py:12
  160.1 14.8 %collective-permute-start.3 = (bf16[2048,128]{1,0:T(8,128)(2,1)S(1)}, bf16[2048,128]{1,0:T(8,128)(2,1)S(1)}, u32[]{:S(2)}, u32[]{:S(2)}) collective-permute-start(bf16[2048,128]{1,0:T(8,128)(2,1)S(1)} %subtract_convert_fusion), channel_id=1, source_target_pairs={{0,16},{16,0},{1,17},{17,1},{2,18},{18,2},{3,19},{19,3},{4,20},{20... | collective-permute-start | bytes 1572872 | tf_op jit(solution)/shard_map/ppermute | solution.py:12
  175.0 1.0 copy-start

commit v16 on v11

--- a/solution.py
+++ b/solution.py
@@ -8,8 +8,26 @@
 SCALE = 2.0**21
 
 
-def swap(block, axis="half"):
-    return lax.ppermute(block, axis, [(0, 1), (1, 0)])
+TURN = ("core", "half", "z")
+
+
+def device(core, half, z):
+    return (core % 2 * HALVES + half % 2) * RING + z
+
+
+TURNS = [
+    [device(first + z, half, z) for z in range(RING)] for first in range(2) for half in range(HALVES)
+]
+
+
+def turn(block, across):
+    pairs = [
+        (device(core, half, z), device(core + z, half + across, z))
+        for core in range(2)
+        for half in range(HALVES)
+        for z in range(RING)
+    ]
+    return lax.ppermute(block, TURN, pairs)
 
 
 def parts_of(tile, half):
@@ -26,7 +44,7 @@
     block = jnp.where(slot // RING == half, own[None], other[None])
     sent = jnp.where(slot % RING == lax.axis_index("z"), block, jnp.zeros_like(block))
     scaled = (sent.astype(jnp.float32) * SCALE).astype(jnp.float16)
-    return lax.psum(scaled, "z")
+    return lax.psum(scaled, TURN, axis_index_groups=TURNS)
 
 
 def contract(left, right, dims):
@@ -38,7 +56,7 @@
     count = lax.axis_size(axes)
     cut = part.reshape((count, part.shape[0] // count) + part.shape[1:])
     share = jnp.sum(lax.all_to_all(cut, axes, 0, 0), axis=0)
-    share = share + swap(share, "core")
+    share = share + lax.ppermute(share, "core", [(0, 1), (1, 0)])
     spread = jnp.broadcast_to(share[None], (count,) + share.shape)
     return lax.all_to_all(spread, axes, 0, 0).reshape(part.shape)
 
@@ -54,9 +72,10 @@
     columns = eigvecs.shape[1]
     half = lax.axis_index("half")
     own, away = parts_of(reflectors, half)
-    other = swap(away)
+    other = turn(away, 1)
     mine, guest = parts_of(eigvecs, half)
-    theirs = swap(guest)
+    theirs = turn(guest, 1)
+    own, mine = turn(own, 0), turn(mine, 0)
     whole = spread_panels(own, other, owners, half)
     panels = [whole[p].astype(jnp.bfloat16) for p in range(2)]
 
@@ -83,8 +102,8 @@
             total = total - contract(panels[p], part, ((1,), (1,))) * (1 / SCALE)
         return total.astype(jnp.bfloat16)
 
-    got = swap(updated(theirs, 1 - half))
-    kept = updated(mine, half)
+    got = turn(updated(theirs, 1 - half), 1)
+    kept = turn(updated(mine, half), 0)
     both = jnp.stack([kept, kept])
     return lax.dynamic_update_index_in_dim(both, got, 1 - half, 0).reshape(eigvecs.shape)
 

time: 176 us -> 182 us (1.034)
  the two profiles are of different devices: /device:TPU:1 before, /device:TPU:33 now
where the time goes in v16:
time: 182 us
  blocking collectives  112 us (62%)
  waiting for transfers between devices  33.9 us (19%)
  starting transfers between devices  20.8 us (11%)
  local copies, waits for them, and re-layouts  4.91 us (3%)
  other arithmetic  4.87 us (3%)
  matrix products  4.77 us (3%)
    psum x1, blocking collectives, spread_panels(): return lax.psum(scaled, TURN, axis_index_groups=TURNS)  74.1 us
    ppermute x6, waiting for transfers between devices, turn(): return lax.ppermute(block, TURN, pairs)  33.1 us
    all_to_all x1, blocking collectives, sum_over_rows(): share = jnp.sum(lax.all_to_all(cut, axes, 0, 0), axis=0)  20.9 us
    ppermute x6, starting transfers between devices, turn(): return lax.ppermute(block, TURN, pairs)  18.3 us
    all_to_all x1, blocking collectives, sum_over_rows(): return lax.all_to_all(spread, axes, 0, 0).reshape(part.shape)  16.9 us
  transfers between devices with their start and end apart: 7, of which 3 were waited for; matrix products, arithmetic and copies ran while one was open for 3% of the time, Pallas kernels for 0%

profile of v16, /device:TPU:33, one launch (start us, length us, event | category | flops | bytes accessed | tf_op | source)
XLA Modules:
  0.0 181.5 jit_solution(9996371670467085312)
XLA Ops:
  0.0 0.0 copy-start.1
  0.0 2.7 %dynamic-slice_bitcast_fusion.1 = (bf16[2048,256]{1,0:T(8,128)(2,1)}, bf16[2048,256]{1,0:T(8,128)(2,1)S(1)}) fusion(bf16[2,2048,256]{2,1,0:T(8,128)(2,1)} %bitcast.78, s32[]{:T(128)S(6)} %select_n.59, s32[]{:T(128)S(6)} %select_n.62), kind=kLoop, calls=%fused_computation.17 | loop fusion | bytes 4194312 | tf_op jit(solution)/shard_map/jit(dynamic_index_in_dim)/squeeze | solution.py:37
  2.7 0.0 copy-start.3
  2.7 2.7 %collective-permute-start.1 = (bf16[2048,256]{1,0:T(8,128)(2,1)}, bf16[2048,256]{1,0:T(8,128)(2,1)S(1)}, u32[]{:S(2)}, u32[]{:S(2)}) collective-permute-start(bf16[2048,256]{1,0:T(8,128)(2,1)} %get-tuple-element.5), channel_id=1, source_target_pairs={{0,0},{1,33},{2,2},{3,35},{4,4},{5,37},{6,6},{7,39},{8,8},{9,41},{... | collective-permute-start | bytes 3145736 | tf_op jit(solution)/shard_map/ppermute | solution.py:30
  5.4 4.6 %collective-permute-start.2 = (bf16[2048,256]{1,0:T(8,128)(2,1)S(1)}, bf16[2048,256]{1,0:T(8,128)(2,1)}, u32[]{:S(2)}, u32[]{:S(2)}) collective-permute-start(bf16[2048,256]{1,0:T(8,128)(2,1)S(1)} %get-tuple-element.6), channel_id=1, source_target_pairs={{0,16},{1,49},{2,18},{3,51},{4,20},{5,53},{6,22},{7,55},{8,24},{9,... | collective-permute-start | bytes 3145736 | tf_op jit(solution)/shard_map/ppermute | solution.py:30
  10.0 0.0 copy-done.1
  10.0 1.1 dynamic-slice_bitcast_fusion.2
  11.1 2.5 %collective-permute-start.3 = (bf16[2048,128]{1,0:T(8,128)(2,1)}, bf16[2048,128]{1,0:T(8,128)(2,1)S(1)}, u32[]{:S(2)}, u32[]{:S(2)}) collective-permute-start(bf16[2048,128]{1,0:T(8,128)(2,1)} %get-tuple-element.7), channel_id=1, source_target_pairs={{0,16},{1,49},{2,18},{3,51},{4,20},{5,53},{6,22},{7,55},{8,24},{9,... | collective-permute-start | bytes 1572872 | tf_op jit(solution)/shard_map/ppermute | solution.py:30
  13.6 1.9 %collective-permute-start = (bf16[2048,128]{1,0:T(8,128)(2,1)}, bf16[2048,128]{1,0:T(8,128)(2,1)S(1)}, u32[]{:S(2)}, u32[]{:S(2)}) collective-permute-start(bf16[2048,128]{1,0:T(8,128)(2,1)} %get-tuple-element.8), channel_id=1, source_target_pairs={{0,0},{1,33},{2,2},{3,35},{4,4},{5,37},{6,6},{7,39},{8,8},{9,41},{... | collective-permute-start | bytes 1572872 | tf_op jit(solution)/shard_map/ppermute | solution.py:30
  15.5 0.0 copy-done.3
  15.6 0.0 collective-permute-done.1
  15.6 19.0 %collective-permute-done.2 = bf16[2048,256]{1,0:T(8,128)(2,1)} collective-permute-done((bf16[2048,256]{1,0:T(8,128)(2,1)S(1)}, bf16[2048,256]{1,0:T(8,128)(2,1)}, u32[]{:S(2)}, u32[]{:S(2)}) %collective-permute-start.2) | collective-permute-done | bytes 1048608 | tf_op jit(solution)/shard_map/ppermute | solution.py:30
  34.6 3.5 %multiply_convert_fusion = f16[2,2048,256]{2,1,0:T(8,128)(2,1)} fusion(pred[2]{0:T(512)(128)(4,1)S(1)} %get-tuple-element.10, pred[2]{0:T(512)(128)(4,1)S(1)} %get-tuple-element.9, bf16[2048,256]{1,0:T(8,128)(2,1)} %collective-permute-done.2, bf16[2048,256]{1,0:T(8,128)(2,1)S(1)} %collective-permute-done.1), kind=kLoop, calls=%fused_computation | loop fusion | flops 5242880 | bytes 4194308 | tf_op jit(solution)/shard_map/convert_element_type | solution.py:46
  38.1 74.1 %all-reduce.1 = u32[2,4,65536]{2,1,0:T(4,128)S(1)} all-reduce(u32[2,4,65536]{2,1,0:T(4,128)} %bitcast.75), channel_id=1, replica_groups={{0,33,2,35,4,37,6,39,8,41,10,43,12,45,14,47},{16,49,18,51,20,53,22,55,2..., use_global_device_ids=true, to_apply=%region_0.1.clone | all-reduce | flops 524288 | bytes 4194304 | tf_op jit(solution)/shard_map/psum | solution.py:47
  112.2 0.0 collective-permute-done.3
  112.2 0.3 fusion.5
  112.6 0.0 collective-permute-done
  112.6 0.3 select_dynamic-update-slice_fusion.3
  113.0 0.3 fusion.16
  113.3 0.3 select_dynamic-update-slice_fusion.1
  113.7 0.5 convolution_dynamic-update-slice_fusion
  114.2 20.9 %all_to_all.10 = f32[16,48,256]{2,1,0:T(8,128)} all-to-all(f32[16,48,256]{2,1,0:T(8,128)S(1)} %bitcast.81), channel_id=1, replica_groups=mesh['chip'=8,'core'=2,'half'=2,'z'=16] {'chip','half'}, dimensions={0} | all-to-all | bytes 1572864 | tf_op jit(solution)/shard_map/all_to_all | solution.py:58
  135.1 1.2 reduce_sum.9
  136.3 0.0 copy-start.2
  136.3 2.5 %collective-permute-start.4 = (f32[48,256]{1,0:T(8,128)S(1)}, f32[48,256]{1,0:T(8,128)S(1)}, u32[]{:S(2)}, u32[]{:S(2)}) collective-permute-start(f32[48,256]{1,0:T(8,128)S(1)} %reduce_sum.9), channel_id=1, source_target_pairs={{0,32},{32,0},{1,33},{33,1},{2,34},{34,2},{3,35},{35,3},{4,36},{36... | collective-permute-start | bytes 147464 | tf_op jit(solution)/shard_map/ppermute | solution.py:59
  138.8 0.9 collective-permute-done.4
  139.7 0.1 broadcast_in_dim.52
  139.8 16.9 %all_to_all.11 = f32[16,48,256]{2,1,0:T(8,128)S(1)} all-to-all(f32[16,48,256]{2,1,0:T(8,128)S(1)} %broadcast_in_dim.52), channel_id=1, replica_groups=mesh['chip'=8,'core'=2,'half'=2,'z'=16] {'chip','half'}, dimensions={0} | all-to-all | bytes 1572864 | tf_op jit(solution)/shard_map/all_to_all | solution.py:61
  156.7 0.0 copy-done.2
  156.7 0.4 convolution_convert_fusion.1
  157.1 0.3 convolution_subtract_fusion
  157.4 0.4 convolution_convert_fusion
  157.8 0.4 convolution_multiply_fusion
  158.3 0.4 convolution_multiply_fusion.2
  158.7 0.4 subtract_convert_fusion.1
  159.2 3.9 %collective-permute-start.5 = (bf16[2048,128]{1,0:T(8,128)(2,1)S(1)}, bf16[2048,128]{1,0:T(8,128)(2,1)S(1)}, u32[]{:S(2)}, u32[]{:S(2)}) collective-permute-start(bf16[2048,128]{1,0:T(8,128)(2,1)S(1)} %subtract_convert_fusion.1), channel_id=1, source_target_pairs={{0,0},{1,33},{2,2},{3,35},{4,4},{5,37},{6,6},{7,39},{8,8},{9,41},{... | collective-permute-start | bytes 1572872 | tf_op jit(solution)/shard_map/ppermute | solution.py:30
  163.1 0.4 subtract_convert_fusion
  163.5 2.8 %collective-permute-start.6 = (bf16[2048,128]{1,0:T(8,128)(2,1)S(1)}, bf16[2048,128]{1,0:T(8,128)(2,1)S(1)}, u32[]{:S(2)}, u32[]{:S(2)}) collective-permute-start(bf16[2048,128]{1,0:T(8,128)(2,1)S(1)} %subtract_convert_fusion), channel_id=1, source_target_pairs={{0,16},{1,49},{2,18},{3,51},{4,20},{5,53},{6,22},{7,55},{8,24},{9,... | collective-permute-start | bytes 1572872 | tf_op jit(solution)/shard_map/ppermute | solution.py:30
  166.3 0.0 collective-permute-done.5
  166.3 0.1 pad_maximum_fusion
  166.4 14.1 %collective-permute-done.6 = bf16[2048,128]{1,0:T(8,128)(2,1)S(1)} collective-permute-done((bf16[2048,128]{1,0:T(8,128)(2,1)S(1)}, bf16[2048,128]{1,0:T(8,128)(2,1)S(1)}, u32[]{:S(2)}, u32[]{:S(2)}) %collective-permute-start.6) | collective-permute-done | bytes 524320 | tf_op jit(solution)/shard_map/ppermute | solution.py:30
  180.5 0.1 bitcast_dynamic-update-slice_fusion
  180.6 0.0 copy-start
  180.6 1.0 copy-done
  (4 shorter events, 0.1 us)
Async XLA Ops:
  0.0 10.0 %copy-start.1 = (bf16[4096,128]{1,0:T(8,128)(2,1)S(1)}, bf16[4096,128]{1,0:T(8,128)(2,1)}, u32[]{:S(2)}) copy-start(bf16[4096,128]{1,0:T(8,128)(2,1)} %param.4) | copy-start | bytes 3145732
  2.7 12.8 %copy-start.3 = (s32[32]{0:T(128)S(1)}, s32[32]{0:T(128)}, u32[]{:S(2)}) copy-start(s32[32]{0:T(128)} %param.7) | copy-start | bytes 388
  2.7 12.8 %collective-permute-start.1 = (bf16[2048,256]{1,0:T(8,128)(2,1)}, bf16[2048,256]{1,0:T(8,128)(2,1)S(1)}, u32[]{:S(2)}, u32[]{:S(2)}) collective-permute-start(bf16[2048,256]{1,0:T(8,128)(2,1)} %get-tuple-element.5), channel_id=1, source_target_pairs={{0,0},{1,33},{2,2},{3,35},{4,4},{5,37},{6,6},{7,39},{8,8},{9,41},{... | collective-permute-start | bytes 3145736 | tf_op jit(solution)/shard_map/ppermute | solution.py:30
  5.4 29.1 %collective-permute-start.2 = (bf16[2048,256]{1,0:T(8,128)(2,1)S(1)}, bf16[2048,256]{1,0:T(8,128)(2,1)}, u32[]{:S(2)}, u32[]{:S(2)}) collective-permute-start(bf16[2048,256]{1,0:T(8,128)(2,1)S(1)} %get-tuple-element.6), channel_id=1, source_target_pairs={{0,16},{1,49},{2,18},{3,51},{4,20},{5,53},{6,22},{7,55},{8,24},{9,... | collective-permute-start | bytes 3145736 | tf_op jit(solution)/shard_map/ppermute | solution.py:30
  11.1 101.2 %collective-permute-start.3 = (bf16[2048,128]{1,0:T(8,128)(2,1)}, bf16[2048,128]{1,0:T(8,128)(2,1)S(1)}, u32[]{:S(2)}, u32[]{:S(2)}) collective-permute-start(bf16[2048,128]{1,0:T(8,128)(2,1)} %get-tuple-element.7), channel_id=1, source_target_pairs={{0,16},{1,49},{2,18},{3,51},{4,20},{5,53},{6,22},{7,55},{8,24},{9,... | collective-permute-start | bytes 1572872 | tf_op jit(solution)/shard_map/ppermute | solution.py:30
  13.6 99.0 %collective-permute-start = (bf16[2048,128]{1,0:T(8,128)(2,1)}, bf16[2048,128]{1,0:T(8,128)(2,1)S(1)}, u32[]{:S(2)}, u32[]{:S(2)}) collective-permute-start(bf16[2048,128]{1,0:T(8,128)(2,1)} %get-tuple-element.8), channel_id=1, source_target_pairs={{0,0},{1,33},{2,2},{3,35},{4,4},{5,37},{6,6},{7,39},{8,8},{9,41},{... | collective-permute-start | bytes 1572872 | tf_op jit(solution)/shard_map/ppermute | solution.py:30
  136.3 20.3 %copy-start.2 = (f32[2,256,256]{2,1,0:T(8,128)S(1)}, f32[2,256,256]{2,1,0:T(8,128)}, u32[]{:S(2)}) copy-start(f32[2,256,256]{2,1,0:T(8,128)} %param.6) | copy-start | bytes 1572868
  136.3 3.3 %collective-permute-start.4 = (f32[48,256]{1,0:T(8,128)S(1)}, f32[48,256]{1,0:T(8,128)S(1)}, u32[]{:S(2)}, u32[]{:S(2)}) collective-permute-start(f32[48,256]{1,0:T(8,128)S(1)} %reduce_sum.9), channel_id=1, source_target_pairs={{0,32},{32,0},{1,33},{33,1},{2,34},{34,2},{3,35},{35,3},{4,36},{36... | collective-permute-start | bytes 147464 | tf_op jit(solution)/shard_map/ppermute | solution.py:59
  159.2 7.1 %collective-permute-start.5 = (bf16[2048,128]{1,0:T(8,128)(2,1)S(1)}, bf16[2048,128]{1,0:T(8,128)(2,1)S(1)}, u32[]{:S(2)}, u32[]{:S(2)}) collective-permute-start(bf16[2048,128]{1,0:T(8,128)(2,1)S(1)} %subtract_convert_fusion.1), channel_id=1, source_target_pairs={{0,0},{1,33},{2,2},{3,35},{4,4},{5,37},{6,6},{7,39},{8,8},{9,41},{... | collective-permute-start | bytes 1572872 | tf_op jit(solution)/shard_map/ppermute | solution.py:30
  163.5 17.0 %collective-permute-start.6 = (bf16[2048,128]{1,0:T(8,128)(2,1)S(1)}, bf16[2048,128]{1,0:T(8,128)(2,1)S(1)}, u32[]{:S(2)}, u32[]{:S(2)}) collective-permute-start(bf16[2048,128]{1,0:T(8,128)(2,1)S(1)} %subtract_convert_fusion), channel_id=1, source_target_pairs={{0,16},{1,49},{2,18},{3,51},{4,20},{5,53},{6,22},{7,55},{8,24},{9,... | collective-permute-start | bytes 1572872 | tf_op jit(solution)/shard_map/ppermute | solution.py:30
  180.6 1.0 copy-start

commit v17 on v16

--- a/solution.py
+++ b/solution.py
@@ -51,12 +51,10 @@
     return lax.dot_general(left, right, (dims, ((), ())), preferred_element_type=jnp.float32)
 
 
-def sum_over_rows(part):
-    axes = ("chip", "half")
+def sum_over(part, axes):
     count = lax.axis_size(axes)
     cut = part.reshape((count, part.shape[0] // count) + part.shape[1:])
     share = jnp.sum(lax.all_to_all(cut, axes, 0, 0), axis=0)
-    share = share + lax.ppermute(share, "core", [(0, 1), (1, 0)])
     spread = jnp.broadcast_to(share[None], (count,) + share.shape)
     return lax.all_to_all(spread, axes, 0, 0).reshape(part.shape)
 
@@ -74,6 +72,7 @@
     own, away = parts_of(reflectors, half)
     other = turn(away, 1)
     mine, guest = parts_of(eigvecs, half)
+    own, mine, guest = lax.optimization_barrier((own, mine, guest))
     theirs = turn(guest, 1)
     own, mine = turn(own, 0), turn(mine, 0)
     whole = spread_panels(own, other, owners, half)
@@ -85,7 +84,7 @@
         there = contract(theirs, panels[p], ((0,), (0,)))
         blocks += [jnp.where(half == 0, here, there), jnp.where(half == 0, there, here)]
     cross = contract(panels[1], panels[0], ((0,), (0,)))
-    summed = sum_over_rows(jnp.concatenate(blocks + [cross], axis=0))
+    summed = sum_over(jnp.concatenate(blocks + [cross], axis=0), ("chip", "core", "half"))
     count = HALVES * columns
     first = summed[:count] * (1 / SCALE)
     second = summed[count : 2 * count] * (1 / SCALE)
@@ -102,7 +101,8 @@
             total = total - contract(panels[p], part, ((1,), (1,))) * (1 / SCALE)
         return total.astype(jnp.bfloat16)
 
-    got = turn(updated(theirs, 1 - half), 1)
+    sent, mine = lax.optimization_barrier((updated(theirs, 1 - half), mine))
+    got = turn(sent, 1)
     kept = turn(updated(mine, half), 0)
     both = jnp.stack([kept, kept])
     return lax.dynamic_update_index_in_dim(both, got, 1 - half, 0).reshape(eigvecs.shape)

time: 182 us -> 180 us (0.989)
  the two profiles are of different devices: /device:TPU:33 before, /device:TPU:1 now
where the time goes in v17:
time: 180 us; the launch traced here: 178 us
  blocking collectives  120 us (67%)
  waiting for transfers between devices  29.3 us (16%)
  starting transfers between devices  14.1 us (8%)
  local copies, waits for them, and re-layouts  4.88 us (3%)
  other arithmetic  4.87 us (3%)
  matrix products  4.77 us (3%)
    psum x1, blocking collectives, spread_panels(): return lax.psum(scaled, TURN, axis_index_groups=TURNS)  80.7 us
    ppermute x6, waiting for transfers between devices, turn(): return lax.ppermute(block, TURN, pairs)  29.3 us
    all_to_all x1, blocking collectives, sum_over(): share = jnp.sum(lax.all_to_all(cut, axes, 0, 0), axis=0)  21 us
    all_to_all x1, blocking collectives, sum_over(): return lax.all_to_all(spread, axes, 0, 0).reshape(part.shape)  18.1 us
    ppermute x6, starting transfers between devices, turn(): return lax.ppermute(block, TURN, pairs)  14.1 us
    dot_general x9, matrix products, contract(): lax.dot_general(left, right, (dims, ((), ())), preferred_element_type=jnp...  3.63 us
  transfers between devices with their start and end apart: 6, of which 2 were waited for; matrix products, arithmetic and copies ran while one was open for 2% of the time, Pallas kernels for 0%

profile of v17, /device:TPU:1, one launch (start us, length us, event | category | flops | bytes accessed | tf_op | source)
XLA Modules:
  0.0 177.9 jit_solution(6535467007991321927)
XLA Ops:
  0.0 0.0 copy-start.1
  0.0 2.7 %dynamic-slice_bitcast_fusion.1 = (bf16[2048,256]{1,0:T(8,128)(2,1)}, bf16[2048,256]{1,0:T(8,128)(2,1)S(1)}) fusion(bf16[2,2048,256]{2,1,0:T(8,128)(2,1)} %bitcast.78, s32[]{:T(128)S(6)} %select_n.59, s32[]{:T(128)S(6)} %select_n.60), kind=kLoop, calls=%fused_computation.17 | loop fusion | bytes 4194312 | tf_op jit(solution)/shard_map/jit(dynamic_index_in_dim)/squeeze | solution.py:37
  2.7 0.0 copy-start.3
  2.7 0.0 copy-done.1
  2.7 1.1 dynamic-slice_bitcast_fusion.2
  3.8 1.9 %collective-permute-start.1 = (bf16[2048,256]{1,0:T(8,128)(2,1)}, bf16[2048,256]{1,0:T(8,128)(2,1)S(1)}, u32[]{:S(2)}, u32[]{:S(2)}) collective-permute-start(bf16[2048,256]{1,0:T(8,128)(2,1)} %get-tuple-element.11), channel_id=1, source_target_pairs={{0,0},{1,33},{2,2},{3,35},{4,4},{5,37},{6,6},{7,39},{8,8},{9,41},{... | collective-permute-start | bytes 3145736 | tf_op jit(solution)/shard_map/ppermute | solution.py:30
  5.7 5.5 %collective-permute-start.2 = (bf16[2048,256]{1,0:T(8,128)(2,1)S(1)}, bf16[2048,256]{1,0:T(8,128)(2,1)}, u32[]{:S(2)}, u32[]{:S(2)}) collective-permute-start(bf16[2048,256]{1,0:T(8,128)(2,1)S(1)} %get-tuple-element.16), channel_id=1, source_target_pairs={{0,16},{1,49},{2,18},{3,51},{4,20},{5,53},{6,22},{7,55},{8,24},{9,... | collective-permute-start | bytes 3145736 | tf_op jit(solution)/shard_map/ppermute | solution.py:30
  11.1 1.9 %collective-permute-start = (bf16[2048,128]{1,0:T(8,128)(2,1)}, bf16[2048,128]{1,0:T(8,128)(2,1)S(1)}, u32[]{:S(2)}, u32[]{:S(2)}) collective-permute-start(bf16[2048,128]{1,0:T(8,128)(2,1)} %get-tuple-element.10), channel_id=1, source_target_pairs={{0,16},{1,49},{2,18},{3,51},{4,20},{5,53},{6,22},{7,55},{8,24},{9,... | collective-permute-start | bytes 1572872 | tf_op jit(solution)/shard_map/ppermute | solution.py:30
  13.1 1.7 collective-permute-start.3
  14.8 0.0 copy-done.3
  14.8 0.0 collective-permute-done.1
  14.8 15.7 %collective-permute-done.2 = bf16[2048,256]{1,0:T(8,128)(2,1)} collective-permute-done((bf16[2048,256]{1,0:T(8,128)(2,1)S(1)}, bf16[2048,256]{1,0:T(8,128)(2,1)}, u32[]{:S(2)}, u32[]{:S(2)}) %collective-permute-start.2) | collective-permute-done | bytes 1048608 | tf_op jit(solution)/shard_map/ppermute | solution.py:30
  30.5 3.5 %multiply_convert_fusion = f16[2,2048,256]{2,1,0:T(8,128)(2,1)} fusion(pred[2]{0:T(512)(128)(4,1)S(1)} %get-tuple-element.20, pred[2]{0:T(512)(128)(4,1)S(1)} %get-tuple-element.19, bf16[2048,256]{1,0:T(8,128)(2,1)} %collective-permute-done.2, bf16[2048,256]{1,0:T(8,128)(2,1)S(1)} %collective-permute-done.1), kind=kLoop, calls=%fused_computation | loop fusion | flops 5242880 | bytes 4194308 | tf_op jit(solution)/shard_map/convert_element_type | solution.py:46
  34.1 80.7 %all-reduce.1 = u32[2,4,65536]{2,1,0:T(4,128)S(1)} all-reduce(u32[2,4,65536]{2,1,0:T(4,128)} %bitcast.75), channel_id=1, replica_groups={{0,33,2,35,4,37,6,39,8,41,10,43,12,45,14,47},{16,49,18,51,20,53,22,55,2..., use_global_device_ids=true, to_apply=%region_0.1.clone | all-reduce | flops 524288 | bytes 4194304 | tf_op jit(solution)/shard_map/psum | solution.py:47
  114.8 0.0 collective-permute-done
  114.8 0.3 fusion.5
  115.1 0.0 collective-permute-done.3
  115.1 0.3 select_dynamic-update-slice_fusion.3
  115.5 0.3 fusion.16
  115.9 0.3 select_dynamic-update-slice_fusion.1
  116.2 0.5 convolution_dynamic-update-slice_fusion
  116.7 21.0 %all_to_all.10 = f32[32,24,256]{2,1,0:T(8,128)} all-to-all(f32[32,24,256]{2,1,0:T(8,128)S(1)} %bitcast.81), channel_id=1, replica_groups=mesh['chip'=8,'core'=2,'half'=2,'z'=16] {'chip','core','half'}, dimensions={0} | all-to-all | bytes 1572864 | tf_op jit(solution)/shard_map/all_to_all | solution.py:57
  137.7 1.2 reduce_sum.9
  138.9 0.0 copy-start.2
  138.9 0.1 broadcast_in_dim.52
  139.0 18.1 %all_to_all.11 = f32[32,24,256]{2,1,0:T(8,128)S(1)} all-to-all(f32[32,24,256]{2,1,0:T(8,128)S(1)} %broadcast_in_dim.52), channel_id=1, replica_groups=mesh['chip'=8,'core'=2,'half'=2,'z'=16] {'chip','core','half'}, dimensions={0} | all-to-all | bytes 1572864 | tf_op jit(solution)/shard_map/all_to_all | solution.py:59
  157.1 0.0 copy-done.2
  157.1 0.4 convolution_convert_fusion.1
  157.5 0.3 convolution_subtract_fusion
  157.8 0.4 convolution_convert_fusion
  158.3 0.4 convolution_multiply_fusion.2
  158.7 0.4 convolution_multiply_fusion
  159.2 0.4 subtract_convert_fusion.1
  159.6 0.4 subtract_convert_fusion
  160.1 0.7 collective-permute-start.4
  160.8 2.4 %collective-permute-start.5 = (bf16[2048,128]{1,0:T(8,128)(2,1)S(1)}, bf16[2048,128]{1,0:T(8,128)(2,1)S(1)}, u32[]{:S(2)}, u32[]{:S(2)}) collective-permute-start(bf16[2048,128]{1,0:T(8,128)(2,1)S(1)} %subtract_convert_fusion.1), channel_id=1, source_target_pairs={{0,16},{1,49},{2,18},{3,51},{4,20},{5,53},{6,22},{7,55},{8,24},{9,... | collective-permute-start | bytes 1572872 | tf_op jit(solution)/shard_map/ppermute | solution.py:30
  163.2 0.0 collective-permute-done.4
  163.2 0.1 pad_maximum_fusion
  163.3 13.6 %collective-permute-done.5 = bf16[2048,128]{1,0:T(8,128)(2,1)S(1)} collective-permute-done((bf16[2048,128]{1,0:T(8,128)(2,1)S(1)}, bf16[2048,128]{1,0:T(8,128)(2,1)S(1)}, u32[]{:S(2)}, u32[]{:S(2)}) %collective-permute-start.5) | collective-permute-done | bytes 524320 | tf_op jit(solution)/shard_map/ppermute | solution.py:30
  176.9 0.1 bitcast_dynamic-update-slice_fusion
  177.0 0.0 copy-start
  177.0 1.0 copy-done
  (3 shorter events, 0.0 us)
Async XLA Ops:
  0.0 2.7 %copy-start.1 = (bf16[4096,128]{1,0:T(8,128)(2,1)S(1)}, bf16[4096,128]{1,0:T(8,128)(2,1)}, u32[]{:S(2)}) copy-start(bf16[4096,128]{1,0:T(8,128)(2,1)} %param.4) | copy-start | bytes 3145732
  2.7 12.0 %copy-start.3 = (s32[32]{0:T(128)S(1)}, s32[32]{0:T(128)}, u32[]{:S(2)}) copy-start(s32[32]{0:T(128)} %param.7) | copy-start | bytes 388
  3.8 11.0 %collective-permute-start.1 = (bf16[2048,256]{1,0:T(8,128)(2,1)}, bf16[2048,256]{1,0:T(8,128)(2,1)S(1)}, u32[]{:S(2)}, u32[]{:S(2)}) collective-permute-start(bf16[2048,256]{1,0:T(8,128)(2,1)} %get-tuple-element.11), channel_id=1, source_target_pairs={{0,0},{1,33},{2,2},{3,35},{4,4},{5,37},{6,6},{7,39},{8,8},{9,41},{... | collective-permute-start | bytes 3145736 | tf_op jit(solution)/shard_map/ppermute | solution.py:30
  5.7 24.9 %collective-permute-start.2 = (bf16[2048,256]{1,0:T(8,128)(2,1)S(1)}, bf16[2048,256]{1,0:T(8,128)(2,1)}, u32[]{:S(2)}, u32[]{:S(2)}) collective-permute-start(bf16[2048,256]{1,0:T(8,128)(2,1)S(1)} %get-tuple-element.16), channel_id=1, source_target_pairs={{0,16},{1,49},{2,18},{3,51},{4,20},{5,53},{6,22},{7,55},{8,24},{9,... | collective-permute-start | bytes 3145736 | tf_op jit(solution)/shard_map/ppermute | solution.py:30
  11.1 103.6 %collective-permute-start = (bf16[2048,128]{1,0:T(8,128)(2,1)}, bf16[2048,128]{1,0:T(8,128)(2,1)S(1)}, u32[]{:S(2)}, u32[]{:S(2)}) collective-permute-start(bf16[2048,128]{1,0:T(8,128)(2,1)} %get-tuple-element.10), channel_id=1, source_target_pairs={{0,16},{1,49},{2,18},{3,51},{4,20},{5,53},{6,22},{7,55},{8,24},{9,... | collective-permute-start | bytes 1572872 | tf_op jit(solution)/shard_map/ppermute | solution.py:30
  13.1 102.1 %collective-permute-start.3 = (bf16[2048,128]{1,0:T(8,128)(2,1)}, bf16[2048,128]{1,0:T(8,128)(2,1)S(1)}, u32[]{:S(2)}, u32[]{:S(2)}) collective-permute-start(bf16[2048,128]{1,0:T(8,128)(2,1)} %get-tuple-element.12), channel_id=1, source_target_pairs={{0,0},{1,33},{2,2},{3,35},{4,4},{5,37},{6,6},{7,39},{8,8},{9,41},{... | collective-permute-start | bytes 1572872 | tf_op jit(solution)/shard_map/ppermute | solution.py:30
  138.9 18.2 %copy-start.2 = (f32[2,256,256]{2,1,0:T(8,128)S(1)}, f32[2,256,256]{2,1,0:T(8,128)}, u32[]{:S(2)}) copy-start(f32[2,256,256]{2,1,0:T(8,128)} %param.6) | copy-start | bytes 1572868
  160.1 3.1 %collective-permute-start.4 = (bf16[2048,128]{1,0:T(8,128)(2,1)S(1)}, bf16[2048,128]{1,0:T(8,128)(2,1)S(1)}, u32[]{:S(2)}, u32[]{:S(2)}) collective-permute-start(bf16[2048,128]{1,0:T(8,128)(2,1)S(1)} %subtract_convert_fusion), channel_id=1, source_target_pairs={{0,0},{1,33},{2,2},{3,35},{4,4},{5,37},{6,6},{7,39},{8,8},{9,41},{... | collective-permute-start | bytes 1572872 | tf_op jit(solution)/shard_map/ppermute | solution.py:30
  160.8 16.1 %collective-permute-start.5 = (bf16[2048,128]{1,0:T(8,128)(2,1)S(1)}, bf16[2048,128]{1,0:T(8,128)(2,1)S(1)}, u32[]{:S(2)}, u32[]{:S(2)}) collective-permute-start(bf16[2048,128]{1,0:T(8,128)(2,1)S(1)} %subtract_convert_fusion.1), channel_id=1, source_target_pairs={{0,16},{1,49},{2,18},{3,51},{4,20},{5,53},{6,22},{7,55},{8,24},{9,... | collective-permute-start | bytes 1572872 | tf_op jit(solution)/shard_map/ppermute | solution.py:30
  177.0 1.0 copy-start

commit v18 on v11

--- a/solution.py
+++ b/solution.py
@@ -57,12 +57,13 @@
     other = swap(away)
     mine, guest = parts_of(eigvecs, half)
     theirs = swap(guest)
+    early, other = lax.optimization_barrier((mine, other))
     whole = spread_panels(own, other, owners, half)
     panels = [whole[p].astype(jnp.bfloat16) for p in range(2)]
 
     blocks = []
     for p in range(2):
-        here = contract(mine, panels[p], ((0,), (0,)))
+        here = contract(early, panels[p], ((0,), (0,)))
         there = contract(theirs, panels[p], ((0,), (0,)))
         blocks += [jnp.where(half == 0, here, there), jnp.where(half == 0, there, here)]
     cross = contract(panels[1], panels[0], ((0,), (0,)))

time: 176 us -> 176 us (level)
  transfers between devices with their start and end apart: 4 -> 4, of which waited for: 3 -> 3; matrix products, arithmetic and copies ran while one was open for 2% -> 3% of each run, Pallas kernels for 0% -> 0%
where the time goes in v18:
time: 176 us
  blocking collectives  106 us (60%)
  waiting for transfers between devices  28.1 us (16%)
  starting transfers between devices  27.7 us (16%)
  matrix products  4.79 us (3%)
  local copies, waits for them, and re-layouts  4.72 us (3%)
  other arithmetic  3.74 us (2%)
    psum x1, blocking collectives, spread_panels(): return lax.psum(scaled, 'z')  73.5 us
    ppermute x4, waiting for transfers between devices, swap(): return lax.ppermute(block, axis, [(0, 1), (1, 0)])  28.1 us
    ppermute x4, starting transfers between devices, swap(): return lax.ppermute(block, axis, [(0, 1), (1, 0)])  27.7 us
    all_to_all x1, blocking collectives, sum_over_rows(): share = jnp.sum(lax.all_to_all(cut, axes, 0, 0), axis=0)  16.6 us
    all_to_all x1, blocking collectives, sum_over_rows(): return lax.all_to_all(spread, axes, 0, 0).reshape(part.shape)  16.1 us
    dot_general x9, matrix products, contract(): lax.dot_general(left, right, (dims, ((), ())), preferred_element_type=jnp...  3.64 us
    convert_element_type x1, other arithmetic, spread_panels(): scaled = (sent.astype(jnp.float32) * SCALE).astype(jnp.float16)  3.54 us
  transfers between devices with their start and end apart: 4, of which 3 were waited for; matrix products, arithmetic and copies ran while one was open for 3% of the time, Pallas kernels for 0%

profile of v18, /device:TPU:1, one launch (start us, length us, event | category | flops | bytes accessed | tf_op | source)
XLA Modules:
  0.0 175.6 jit_solution(6571263974168058460)
XLA Ops:
  0.0 0.0 copy-start
  0.0 2.7 %dynamic-slice_bitcast_fusion.1 = (bf16[2048,256]{1,0:T(8,128)(2,1)S(1)}, bf16[2048,256]{1,0:T(8,128)(2,1)}) fusion(bf16[2,2048,256]{2,1,0:T(8,128)(2,1)} %bitcast.81, s32[]{:T(128)S(6)} %select_n.59, s32[]{:T(128)S(6)} %select_n.62), kind=kLoop, calls=%fused_computation.20 | loop fusion | bytes 4194312 | tf_op jit(solution)/shard_map/jit(_where)/broadcast_in_dim | solution.py:26
  2.7 0.0 copy-start.4
  2.7 5.6 %collective-permute-start = (bf16[2048,256]{1,0:T(8,128)(2,1)}, bf16[2048,256]{1,0:T(8,128)(2,1)}, u32[]{:S(2)}, u32[]{:S(2)}) collective-permute-start(bf16[2048,256]{1,0:T(8,128)(2,1)} %get-tuple-element.10), channel_id=1, source_target_pairs={{0,16},{16,0},{1,17},{17,1},{2,18},{18,2},{3,19},{19,3},{4,20},{20... | collective-permute-start | bytes 3145736 | tf_op jit(solution)/shard_map/ppermute | solution.py:12
  8.3 0.0 copy-done
  8.4 0.9 dynamic-slice_bitcast_fusion.2
  9.2 1.9 %collective-permute-start.1 = (bf16[2048,128]{1,0:T(8,128)(2,1)}, bf16[2048,128]{1,0:T(8,128)(2,1)S(1)}, u32[]{:S(2)}, u32[]{:S(2)}) collective-permute-start(bf16[2048,128]{1,0:T(8,128)(2,1)} %get-tuple-element.11), channel_id=1, source_target_pairs={{0,16},{16,0},{1,17},{17,1},{2,18},{18,2},{3,19},{19,3},{4,20},{20... | collective-permute-start | bytes 1572872 | tf_op jit(solution)/shard_map/ppermute | solution.py:12
  11.2 0.0 copy-done.4
  11.2 16.9 %collective-permute-done = bf16[2048,256]{1,0:T(8,128)(2,1)} collective-permute-done((bf16[2048,256]{1,0:T(8,128)(2,1)}, bf16[2048,256]{1,0:T(8,128)(2,1)}, u32[]{:S(2)}, u32[]{:S(2)}) %collective-permute-start) | collective-permute-done | bytes 1048608 | tf_op jit(solution)/shard_map/ppermute | solution.py:12
  28.1 3.5 %multiply_convert_fusion = f16[2,2048,256]{2,1,0:T(8,128)(2,1)} fusion(pred[2]{0:T(512)(128)(4,1)S(1)} %get-tuple-element.14, pred[2]{0:T(512)(128)(4,1)S(1)} %get-tuple-element.13, bf16[2048,256]{1,0:T(8,128)(2,1)} %collective-permute-done, bf16[2048,256]{1,0:T(8,128)(2,1)S(1)} %get-tuple-element.9), kind=kLoop, calls=%fused_computation | loop fusion | flops 5242880 | bytes 4194308 | tf_op jit(solution)/shard_map/convert_element_type | solution.py:28
  31.6 73.5 %all-reduce.1 = u32[2,4,65536]{2,1,0:T(4,128)S(1)} all-reduce(u32[2,4,65536]{2,1,0:T(4,128)} %bitcast.76), channel_id=1, replica_groups=mesh['chip'=8,'core'=2,'half'=2,'z'=16] {'z'}, use_global_device_ids=true, to_apply=%region_0.1.clone | all-reduce | flops 524288 | bytes 4194304 | tf_op jit(solution)/shard_map/psum | solution.py:29
  105.1 0.0 collective-permute-done.1
  105.1 0.3 fusion.9
  105.5 0.3 select_dynamic-update-slice_fusion.3
  105.9 0.3 fusion.18
  106.2 0.3 select_dynamic-update-slice_fusion.1
  106.6 0.5 convolution_dynamic-update-slice_fusion
  107.1 16.6 %all_to_all.10 = f32[16,48,256]{2,1,0:T(8,128)S(1)} all-to-all(f32[16,48,256]{2,1,0:T(8,128)S(1)} %bitcast.84), channel_id=1, replica_groups=mesh['chip'=8,'core'=2,'half'=2,'z'=16] {'chip','half'}, dimensions={0} | all-to-all | bytes 1572864 | tf_op jit(solution)/shard_map/all_to_all | solution.py:40
  123.7 0.1 reduce_sum.9
  123.8 0.0 copy-start.3
  123.8 16.8 %collective-permute-start.2 = (f32[48,256]{1,0:T(8,128)S(1)}, f32[48,256]{1,0:T(8,128)S(1)}, u32[]{:S(2)}, u32[]{:S(2)}) collective-permute-start(f32[48,256]{1,0:T(8,128)S(1)} %reduce_sum.9), channel_id=1, source_target_pairs={{0,32},{32,0},{1,33},{33,1},{2,34},{34,2},{3,35},{35,3},{4,36},{36... | collective-permute-start | bytes 147464 | tf_op jit(solution)/shard_map/ppermute | solution.py:12
  140.6 0.9 collective-permute-done.2
  141.5 0.1 broadcast_in_dim.55
  141.5 16.1 %all_to_all.11 = f32[16,48,256]{2,1,0:T(8,128)S(1)} all-to-all(f32[16,48,256]{2,1,0:T(8,128)S(1)} %broadcast_in_dim.55), channel_id=1, replica_groups=mesh['chip'=8,'core'=2,'half'=2,'z'=16] {'chip','half'}, dimensions={0} | all-to-all | bytes 1572864 | tf_op jit(solution)/shard_map/all_to_all | solution.py:43
  157.6 0.0 copy-done.3
  157.6 0.4 convolution_convert_fusion.1
  158.0 0.3 convolution_subtract_fusion
  158.4 0.4 convolution_convert_fusion
  158.8 0.4 convolution_multiply_fusion
  159.2 0.0 copy-start.1
  159.2 0.4 subtract_convert_fusion
  159.7 3.4 %collective-permute-start.3 = (bf16[2048,128]{1,0:T(8,128)(2,1)S(1)}, bf16[2048,128]{1,0:T(8,128)(2,1)S(1)}, u32[]{:S(2)}, u32[]{:S(2)}) collective-permute-start(bf16[2048,128]{1,0:T(8,128)(2,1)S(1)} %subtract_convert_fusion), channel_id=1, source_target_pairs={{0,16},{16,0},{1,17},{17,1},{2,18},{18,2},{3,19},{19,3},{4,20},{20... | collective-permute-start | bytes 1572872 | tf_op jit(solution)/shard_map/ppermute | solution.py:12
  163.1 0.0 copy-done.1
  163.1 0.5 fusion.1
  163.6 0.4 fusion.3
  164.0 0.1 pad_maximum_fusion
  164.1 10.4 %collective-permute-done.3 = bf16[2048,128]{1,0:T(8,128)(2,1)S(1)} collective-permute-done((bf16[2048,128]{1,0:T(8,128)(2,1)S(1)}, bf16[2048,128]{1,0:T(8,128)(2,1)S(1)}, u32[]{:S(2)}, u32[]{:S(2)}) %collective-permute-start.3) | collective-permute-done | bytes 524320 | tf_op jit(solution)/shard_map/ppermute | solution.py:12
  174.5 0.1 bitcast_dynamic-update-slice_fusion
  174.6 0.0 copy-start.2
  174.6 1.0 copy-done.2
  (4 shorter events, 0.1 us)
Async XLA Ops:
  0.0 8.4 %copy-start = (bf16[4096,128]{1,0:T(8,128)(2,1)S(1)}, bf16[4096,128]{1,0:T(8,128)(2,1)}, u32[]{:S(2)}) copy-start(bf16[4096,128]{1,0:T(8,128)(2,1)} %param.4) | copy-start | bytes 3145732
  2.7 8.4 %copy-start.4 = (s32[32]{0:T(128)S(1)}, s32[32]{0:T(128)}, u32[]{:S(2)}) copy-start(s32[32]{0:T(128)} %param.7) | copy-start | bytes 388
  2.7 25.3 %collective-permute-start = (bf16[2048,256]{1,0:T(8,128)(2,1)}, bf16[2048,256]{1,0:T(8,128)(2,1)}, u32[]{:S(2)}, u32[]{:S(2)}) collective-permute-start(bf16[2048,256]{1,0:T(8,128)(2,1)} %get-tuple-element.10), channel_id=1, source_target_pairs={{0,16},{16,0},{1,17},{17,1},{2,18},{18,2},{3,19},{19,3},{4,20},{20... | collective-permute-start | bytes 3145736 | tf_op jit(solution)/shard_map/ppermute | solution.py:12
  9.2 95.9 %collective-permute-start.1 = (bf16[2048,128]{1,0:T(8,128)(2,1)}, bf16[2048,128]{1,0:T(8,128)(2,1)S(1)}, u32[]{:S(2)}, u32[]{:S(2)}) collective-permute-start(bf16[2048,128]{1,0:T(8,128)(2,1)} %get-tuple-element.11), channel_id=1, source_target_pairs={{0,16},{16,0},{1,17},{17,1},{2,18},{18,2},{3,19},{19,3},{4,20},{20... | collective-permute-start | bytes 1572872 | tf_op jit(solution)/shard_map/ppermute | solution.py:12
  123.8 33.8 %copy-start.3 = (f32[2,256,256]{2,1,0:T(8,128)S(1)}, f32[2,256,256]{2,1,0:T(8,128)}, u32[]{:S(2)}) copy-start(f32[2,256,256]{2,1,0:T(8,128)} %param.6) | copy-start | bytes 1572868
  123.8 17.7 %collective-permute-start.2 = (f32[48,256]{1,0:T(8,128)S(1)}, f32[48,256]{1,0:T(8,128)S(1)}, u32[]{:S(2)}, u32[]{:S(2)}) collective-permute-start(f32[48,256]{1,0:T(8,128)S(1)} %reduce_sum.9), channel_id=1, source_target_pairs={{0,32},{32,0},{1,33},{33,1},{2,34},{34,2},{3,35},{35,3},{4,36},{36... | collective-permute-start | bytes 147464 | tf_op jit(solution)/shard_map/ppermute | solution.py:12
  159.2 3.9 %copy-start.1 = (bf16[4096,128]{1,0:T(8,128)(2,1)S(1)}, bf16[4096,128]{1,0:T(8,128)(2,1)}, u32[]{:S(2)}) copy-start(bf16[4096,128]{1,0:T(8,128)(2,1)} %param.4) | copy-start | bytes 3145732
  159.7 14.8 %collective-permute-start.3 = (bf16[2048,128]{1,0:T(8,128)(2,1)S(1)}, bf16[2048,128]{1,0:T(8,128)(2,1)S(1)}, u32[]{:S(2)}, u32[]{:S(2)}) collective-permute-start(bf16[2048,128]{1,0:T(8,128)(2,1)S(1)} %subtract_convert_fusion), channel_id=1, source_target_pairs={{0,16},{16,0},{1,17},{17,1},{2,18},{18,2},{3,19},{19,3},{4,20},{20... | collective-permute-start | bytes 1572872 | tf_op jit(solution)/shard_map/ppermute | solution.py:12
  174.6 1.0 copy-start.2

commit v19 on v12

--- a/solution.py
+++ b/solution.py
@@ -58,13 +58,13 @@
     theirs = swap(part_of(eigvecs, 1 - half))
     own = scaled(part_of(reflectors, half))
     mine = part_of(eigvecs, half)
-    own, mine, other = lax.optimization_barrier((own, mine, other))
+    own, early, other = lax.optimization_barrier((own, mine, other))
     whole = spread_panels(own, scaled(other), owners, half)
     panels = [whole[p].astype(jnp.bfloat16) for p in range(2)]
 
     blocks = []
     for p in range(2):
-        here = contract(mine, panels[p], ((0,), (0,)))
+        here = contract(early, panels[p], ((0,), (0,)))
         there = contract(theirs, panels[p], ((0,), (0,)))
         blocks += [jnp.where(half == 0, here, there), jnp.where(half == 0, there, here)]
     cross = contract(panels[1], panels[0], ((0,), (0,)))

time: 176 us -> 177 us (level)
  no operation moved by 1% of the time
where the time goes in v19:
time: 177 us; the launch traced here: 176 us
  blocking collectives  106 us (60%)
  starting transfers between devices  27.6 us (16%)
  waiting for transfers between devices  26.3 us (15%)
  other arithmetic  6.5 us (4%)
  matrix products  5.73 us (3%)
  local copies, waits for them, and re-layouts  3.37 us (2%)
    psum x1, blocking collectives, spread_panels(): return lax.psum(sent, 'z')  73.6 us
    ppermute x4, starting transfers between devices, swap(): return lax.ppermute(block, axis, [(0, 1), (1, 0)])  27.6 us
    ppermute x4, waiting for transfers between devices, swap(): return lax.ppermute(block, axis, [(0, 1), (1, 0)])  26.3 us
    all_to_all x1, blocking collectives, sum_over_rows(): share = jnp.sum(lax.all_to_all(cut, axes, 0, 0), axis=0)  16.7 us
    all_to_all x1, blocking collectives, sum_over_rows(): return lax.all_to_all(spread, axes, 0, 0).reshape(part.shape)  16.1 us
    dot_general x9, matrix products, contract(): lax.dot_general(left, right, (dims, ((), ())), preferred_element_type=jnp...  3.63 us
  transfers between devices with their start and end apart: 4, of which 3 were waited for; matrix products, arithmetic and copies ran while one was open for 4% of the time, Pallas kernels for 0%

profile of v19, /device:TPU:1, one launch (start us, length us, event | category | flops | bytes accessed | tf_op | source)
XLA Modules:
  0.0 176.2 jit_solution(9561639728753686037)
XLA Ops:
  0.0 0.0 copy-start
  0.0 0.0 copy-start.4
  0.0 1.4 dynamic-slice_bitcast_fusion
  1.4 5.5 %collective-permute-start = (bf16[2048,256]{1,0:T(8,128)(2,1)S(1)}, bf16[2048,256]{1,0:T(8,128)(2,1)}, u32[]{:S(2)}, u32[]{:S(2)}) collective-permute-start(bf16[2048,256]{1,0:T(8,128)(2,1)S(1)} %dynamic-slice_bitcast_fusion), channel_id=1, source_target_pairs={{0,16},{16,0},{1,17},{17,1},{2,18},{18,2},{3,19},{19,3},{4,20},{20... | collective-permute-start | bytes 3145736 | tf_op jit(solution)/shard_map/ppermute | solution.py:12
  6.9 0.0 copy-done
  6.9 0.9 dynamic-slice_bitcast_fusion.1
  7.8 1.9 %collective-permute-start.1 = (bf16[2048,128]{1,0:T(8,128)(2,1)}, bf16[2048,128]{1,0:T(8,128)(2,1)S(1)}, u32[]{:S(2)}, u32[]{:S(2)}) collective-permute-start(bf16[2048,128]{1,0:T(8,128)(2,1)} %get-tuple-element.13), channel_id=1, source_target_pairs={{0,16},{16,0},{1,17},{17,1},{2,18},{18,2},{3,19},{19,3},{4,20},{20... | collective-permute-start | bytes 1572872 | tf_op jit(solution)/shard_map/ppermute | solution.py:12
  9.7 0.0 copy-done.4
  9.7 1.5 fusion.4
  11.2 15.1 %collective-permute-done = bf16[2048,256]{1,0:T(8,128)(2,1)} collective-permute-done((bf16[2048,256]{1,0:T(8,128)(2,1)S(1)}, bf16[2048,256]{1,0:T(8,128)(2,1)}, u32[]{:S(2)}, u32[]{:S(2)}) %collective-permute-start) | collective-permute-done | bytes 1048608 | tf_op jit(solution)/shard_map/ppermute | solution.py:12
  26.3 1.5 multiply_convert_fusion
  27.7 2.2 %select_select_fusion = f16[2,2048,256]{2,1,0:T(8,128)(2,1)} fusion(pred[2]{0:T(512)(128)(4,1)S(1)} %get-tuple-element.16, pred[2]{0:T(512)(128)(4,1)S(1)} %get-tuple-element.15, f16[2048,256]{1,0:T(8,128)(2,1)S(1)} %multiply_convert_fusion, f16[2048,256]{1,0:T(8,128)(2,1)S(1)} %fusion.4), kind=kLoop, calls=%fused_computation.8 | loop fusion | flops 2097152 | bytes 4194308 | tf_op jit(solution)/shard_map/jit(_where)/select_n | solution.py:27
  30.0 73.6 %all-reduce.1 = u32[2,4,65536]{2,1,0:T(4,128)S(1)} all-reduce(u32[2,4,65536]{2,1,0:T(4,128)} %bitcast.77), channel_id=1, replica_groups=mesh['chip'=8,'core'=2,'half'=2,'z'=16] {'z'}, use_global_device_ids=true, to_apply=%region_0.1.clone | all-reduce | flops 524288 | bytes 4194304 | tf_op jit(solution)/shard_map/psum | solution.py:28
  103.6 0.0 collective-permute-done.1
  103.6 0.3 fusion.10
  104.0 0.3 select_dynamic-update-slice_fusion.3
  104.3 0.3 fusion.19
  104.7 0.3 select_dynamic-update-slice_fusion.1
  105.1 0.5 convolution_dynamic-update-slice_fusion
  105.5 16.7 %all_to_all.10 = f32[16,48,256]{2,1,0:T(8,128)} all-to-all(f32[16,48,256]{2,1,0:T(8,128)S(1)} %bitcast.86), channel_id=1, replica_groups=mesh['chip'=8,'core'=2,'half'=2,'z'=16] {'chip','half'}, dimensions={0} | all-to-all | bytes 1572864 | tf_op jit(solution)/shard_map/all_to_all | solution.py:39
  122.3 1.2 reduce_sum.9
  123.5 0.0 copy-start.3
  123.5 16.8 %collective-permute-start.2 = (f32[48,256]{1,0:T(8,128)S(1)}, f32[48,256]{1,0:T(8,128)S(1)}, u32[]{:S(2)}, u32[]{:S(2)}) collective-permute-start(f32[48,256]{1,0:T(8,128)S(1)} %reduce_sum.9), channel_id=1, source_target_pairs={{0,32},{32,0},{1,33},{33,1},{2,34},{34,2},{3,35},{35,3},{4,36},{36... | collective-permute-start | bytes 147464 | tf_op jit(solution)/shard_map/ppermute | solution.py:12
  140.3 0.9 collective-permute-done.2
  141.2 0.1 broadcast_in_dim.52
  141.2 16.1 %all_to_all.11 = f32[16,48,256]{2,1,0:T(8,128)S(1)} all-to-all(f32[16,48,256]{2,1,0:T(8,128)S(1)} %broadcast_in_dim.52), channel_id=1, replica_groups=mesh['chip'=8,'core'=2,'half'=2,'z'=16] {'chip','half'}, dimensions={0} | all-to-all | bytes 1572864 | tf_op jit(solution)/shard_map/all_to_all | solution.py:42
  157.3 1.4 convolution_convert_fusion.1
  158.7 0.3 convolution_subtract_fusion
  159.0 0.0 copy-done.3
  159.0 0.4 convolution_convert_fusion
  159.4 0.4 convolution_multiply_fusion
  159.9 0.0 copy-start.1
  159.9 0.4 subtract_convert_fusion
  160.3 3.4 %collective-permute-start.3 = (bf16[2048,128]{1,0:T(8,128)(2,1)S(1)}, bf16[2048,128]{1,0:T(8,128)(2,1)S(1)}, u32[]{:S(2)}, u32[]{:S(2)}) collective-permute-start(bf16[2048,128]{1,0:T(8,128)(2,1)S(1)} %subtract_convert_fusion), channel_id=1, source_target_pairs={{0,16},{16,0},{1,17},{17,1},{2,18},{18,2},{3,19},{19,3},{4,20},{20... | collective-permute-start | bytes 1572872 | tf_op jit(solution)/shard_map/ppermute | solution.py:12
  163.8 0.0 copy-done.1
  163.8 0.5 fusion.1
  164.2 0.4 fusion.3
  164.7 0.1 pad_maximum_fusion
  164.8 10.4 %collective-permute-done.3 = bf16[2048,128]{1,0:T(8,128)(2,1)S(1)} collective-permute-done((bf16[2048,128]{1,0:T(8,128)(2,1)S(1)}, bf16[2048,128]{1,0:T(8,128)(2,1)S(1)}, u32[]{:S(2)}, u32[]{:S(2)}) %collective-permute-start.3) | collective-permute-done | bytes 524320 | tf_op jit(solution)/shard_map/ppermute | solution.py:12
  175.2 0.1 bitcast_dynamic-update-slice_fusion
  175.2 0.0 copy-start.2
  175.2 1.0 copy-done.2
  (4 shorter events, 0.1 us)
Async XLA Ops:
  0.0 6.9 %copy-start = (bf16[4096,128]{1,0:T(8,128)(2,1)S(1)}, bf16[4096,128]{1,0:T(8,128)(2,1)}, u32[]{:S(2)}) copy-start(bf16[4096,128]{1,0:T(8,128)(2,1)} %param.4) | copy-start | bytes 3145732
  0.0 9.7 %copy-start.4 = (s32[32]{0:T(128)S(1)}, s32[32]{0:T(128)}, u32[]{:S(2)}) copy-start(s32[32]{0:T(128)} %param.7) | copy-start | bytes 388
  1.4 24.9 %collective-permute-start = (bf16[2048,256]{1,0:T(8,128)(2,1)S(1)}, bf16[2048,256]{1,0:T(8,128)(2,1)}, u32[]{:S(2)}, u32[]{:S(2)}) collective-permute-start(bf16[2048,256]{1,0:T(8,128)(2,1)S(1)} %dynamic-slice_bitcast_fusion), channel_id=1, source_target_pairs={{0,16},{16,0},{1,17},{17,1},{2,18},{18,2},{3,19},{19,3},{4,20},{20... | collective-permute-start | bytes 3145736 | tf_op jit(solution)/shard_map/ppermute | solution.py:12
  7.8 95.8 %collective-permute-start.1 = (bf16[2048,128]{1,0:T(8,128)(2,1)}, bf16[2048,128]{1,0:T(8,128)(2,1)S(1)}, u32[]{:S(2)}, u32[]{:S(2)}) collective-permute-start(bf16[2048,128]{1,0:T(8,128)(2,1)} %get-tuple-element.13), channel_id=1, source_target_pairs={{0,16},{16,0},{1,17},{17,1},{2,18},{18,2},{3,19},{19,3},{4,20},{20... | collective-permute-start | bytes 1572872 | tf_op jit(solution)/shard_map/ppermute | solution.py:12
  123.5 35.5 %copy-start.3 = (f32[2,256,256]{2,1,0:T(8,128)S(1)}, f32[2,256,256]{2,1,0:T(8,128)}, u32[]{:S(2)}) copy-start(f32[2,256,256]{2,1,0:T(8,128)} %param.6) | copy-start | bytes 1572868
  123.5 17.7 %collective-permute-start.2 = (f32[48,256]{1,0:T(8,128)S(1)}, f32[48,256]{1,0:T(8,128)S(1)}, u32[]{:S(2)}, u32[]{:S(2)}) collective-permute-start(f32[48,256]{1,0:T(8,128)S(1)} %reduce_sum.9), channel_id=1, source_target_pairs={{0,32},{32,0},{1,33},{33,1},{2,34},{34,2},{3,35},{35,3},{4,36},{36... | collective-permute-start | bytes 147464 | tf_op jit(solution)/shard_map/ppermute | solution.py:12
  159.9 3.9 %copy-start.1 = (bf16[4096,128]{1,0:T(8,128)(2,1)S(1)}, bf16[4096,128]{1,0:T(8,128)(2,1)}, u32[]{:S(2)}) copy-start(bf16[4096,128]{1,0:T(8,128)(2,1)} %param.4) | copy-start | bytes 3145732
  160.3 14.8 %collective-permute-start.3 = (bf16[2048,128]{1,0:T(8,128)(2,1)S(1)}, bf16[2048,128]{1,0:T(8,128)(2,1)S(1)}, u32[]{:S(2)}, u32[]{:S(2)}) collective-permute-start(bf16[2048,128]{1,0:T(8,128)(2,1)S(1)} %subtract_convert_fusion), channel_id=1, source_target_pairs={{0,16},{16,0},{1,17},{17,1},{2,18},{18,2},{3,19},{19,3},{4,20},{20... | collective-permute-start | bytes 1572872 | tf_op jit(solution)/shard_map/ppermute | solution.py:12
  175.2 1.0 copy-start.2

commit v20 on v17

--- a/solution.py
+++ b/solution.py
@@ -41,7 +41,7 @@
 
 def spread_panels(own, other, owners, half):
     slot = owners[:2].reshape(2, 1, 1)
-    block = jnp.where(slot // RING == half, own[None], other[None])
+    block = jnp.where(slot // RING != half, other[None], own[None])
     sent = jnp.where(slot % RING == lax.axis_index("z"), block, jnp.zeros_like(block))
     scaled = (sent.astype(jnp.float32) * SCALE).astype(jnp.float16)
     return lax.psum(scaled, TURN, axis_index_groups=TURNS)
@@ -70,11 +70,10 @@
     columns = eigvecs.shape[1]
     half = lax.axis_index("half")
     own, away = parts_of(reflectors, half)
+    own = turn(own, 0)
     other = turn(away, 1)
     mine, guest = parts_of(eigvecs, half)
-    own, mine, guest = lax.optimization_barrier((own, mine, guest))
-    theirs = turn(guest, 1)
-    own, mine = turn(own, 0), turn(mine, 0)
+    theirs, mine = turn(guest, 1), turn(mine, 0)
     whole = spread_panels(own, other, owners, half)
     panels = [whole[p].astype(jnp.bfloat16) for p in range(2)]
 
@@ -101,9 +100,8 @@
             total = total - contract(panels[p], part, ((1,), (1,))) * (1 / SCALE)
         return total.astype(jnp.bfloat16)
 
-    sent, mine = lax.optimization_barrier((updated(theirs, 1 - half), mine))
-    got = turn(sent, 1)
     kept = turn(updated(mine, half), 0)
+    got = turn(updated(theirs, 1 - half), 1)
     both = jnp.stack([kept, kept])
     return lax.dynamic_update_index_in_dim(both, got, 1 - half, 0).reshape(eigvecs.shape)
 

time: 180 us -> 178 us (0.989)
  waiting for transfers between devices: 29.3 us -> 27 us
    squeeze x1 -> x0, local copies, waits for them, and re-layouts: 2.73 us -> none  [parts_of(): lax.dynamic_index_in_dim(halves, half, 0, False)]
    squeeze x1 -> x2, local copies, waits for them, and re-layouts: 1.05 us -> 3.78 us  [parts_of(): lax.dynamic_index_in_dim(halves, 1 - half, 0, False)]
    ppermute x6, waiting for transfers between devices: 29.3 us -> 27 us  [turn(): return lax.ppermute(block, TURN, pairs)]
  transfers between devices with their start and end apart: 6 -> 6, of which waited for: 2 -> 2; matrix products, arithmetic and copies ran while one was open for 2% -> 3% of each run, Pallas kernels for 0% -> 0%
where the time goes in v20:
time: 178 us; the launch traced here: 177 us
  blocking collectives  121 us (68%)
  waiting for transfers between devices  27 us (15%)
  starting transfers between devices  14 us (8%)
  local copies, waits for them, and re-layouts  4.88 us (3%)
  other arithmetic  4.87 us (3%)
  matrix products  4.76 us (3%)
    psum x1, blocking collectives, spread_panels(): return lax.psum(scaled, TURN, axis_index_groups=TURNS)  81.3 us
    ppermute x6, waiting for transfers between devices, turn(): return lax.ppermute(block, TURN, pairs)  27 us
    all_to_all x1, blocking collectives, sum_over(): share = jnp.sum(lax.all_to_all(cut, axes, 0, 0), axis=0)  22 us
    all_to_all x1, blocking collectives, sum_over(): return lax.all_to_all(spread, axes, 0, 0).reshape(part.shape)  18.1 us
    ppermute x6, starting transfers between devices, turn(): return lax.ppermute(block, TURN, pairs)  14 us
    squeeze x2, local copies, waits for them, and re-layouts, parts_of(): lax.dynamic_index_in_dim(halves, 1 - half, 0, False)  3.78 us
    dot_general x9, matrix products, contract(): lax.dot_general(left, right, (dims, ((), ())), preferred_element_type=jnp...  3.62 us
  transfers between devices with their start and end apart: 6, of which 2 were waited for; matrix products, arithmetic and copies ran while one was open for 3% of the time, Pallas kernels for 0%

profile of v20, /device:TPU:1, one launch (start us, length us, event | category | flops | bytes accessed | tf_op | source)
XLA Modules:
  0.0 177.1 jit_solution(6982198590050532312)
XLA Ops:
  0.0 0.0 copy-start.1
  0.0 2.7 %dynamic-slice_bitcast_fusion.1 = (bf16[2048,256]{1,0:T(8,128)(2,1)}, bf16[2048,256]{1,0:T(8,128)(2,1)S(1)}) fusion(bf16[2,2048,256]{2,1,0:T(8,128)(2,1)} %bitcast.78, s32[]{:T(128)S(6)} %select_n.62, s32[]{:T(128)S(6)} %select_n.59), kind=kLoop, calls=%fused_computation.17 | loop fusion | bytes 4194312 | tf_op jit(solution)/shard_map/jit(dynamic_index_in_dim)/squeeze | solution.py:38
  2.7 0.0 copy-start.3
  2.7 5.6 %collective-permute-start.1 = (bf16[2048,256]{1,0:T(8,128)(2,1)}, bf16[2048,256]{1,0:T(8,128)(2,1)S(1)}, u32[]{:S(2)}, u32[]{:S(2)}) collective-permute-start(bf16[2048,256]{1,0:T(8,128)(2,1)} %get-tuple-element.5), channel_id=1, source_target_pairs={{0,16},{1,49},{2,18},{3,51},{4,20},{5,53},{6,22},{7,55},{8,24},{9,... | collective-permute-start | bytes 3145736 | tf_op jit(solution)/shard_map/ppermute | solution.py:30
  8.3 1.6 collective-permute-start.2
  10.0 0.0 copy-done.1
  10.0 1.1 dynamic-slice_bitcast_fusion.2
  11.0 1.9 %collective-permute-start.3 = (bf16[2048,128]{1,0:T(8,128)(2,1)}, bf16[2048,128]{1,0:T(8,128)(2,1)S(1)}, u32[]{:S(2)}, u32[]{:S(2)}) collective-permute-start(bf16[2048,128]{1,0:T(8,128)(2,1)} %get-tuple-element.7), channel_id=1, source_target_pairs={{0,16},{1,49},{2,18},{3,51},{4,20},{5,53},{6,22},{7,55},{8,24},{9,... | collective-permute-start | bytes 1572872 | tf_op jit(solution)/shard_map/ppermute | solution.py:30
  13.0 1.7 collective-permute-start
  14.7 0.0 copy-done.3
  14.7 13.4 %collective-permute-done.1 = bf16[2048,256]{1,0:T(8,128)(2,1)S(1)} collective-permute-done((bf16[2048,256]{1,0:T(8,128)(2,1)}, bf16[2048,256]{1,0:T(8,128)(2,1)S(1)}, u32[]{:S(2)}, u32[]{:S(2)}) %collective-permute-start.1) | collective-permute-done | bytes 1048608 | tf_op jit(solution)/shard_map/ppermute | solution.py:30
  28.1 0.0 collective-permute-done.2
  28.1 3.5 %multiply_convert_fusion = f16[2,2048,256]{2,1,0:T(8,128)(2,1)} fusion(pred[2]{0:T(512)(128)(4,1)S(1)} %get-tuple-element.10, pred[2]{0:T(512)(128)(4,1)S(1)} %get-tuple-element.9, bf16[2048,256]{1,0:T(8,128)(2,1)} %collective-permute-done.2, bf16[2048,256]{1,0:T(8,128)(2,1)S(1)} %collective-permute-done.1), kind=kLoop, calls=%fused_computation | loop fusion | flops 5242880 | bytes 4194308 | tf_op jit(solution)/shard_map/convert_element_type | solution.py:46
  31.6 81.3 %all-reduce.1 = u32[2,4,65536]{2,1,0:T(4,128)S(1)} all-reduce(u32[2,4,65536]{2,1,0:T(4,128)} %bitcast.75), channel_id=1, replica_groups={{0,33,2,35,4,37,6,39,8,41,10,43,12,45,14,47},{16,49,18,51,20,53,22,55,2..., use_global_device_ids=true, to_apply=%region_0.1.clone | all-reduce | flops 524288 | bytes 4194304 | tf_op jit(solution)/shard_map/psum | solution.py:47
  112.9 0.0 collective-permute-done.3
  112.9 0.3 fusion.5
  113.3 0.0 collective-permute-done
  113.3 0.3 select_dynamic-update-slice_fusion.3
  113.7 0.3 fusion.16
  114.0 0.3 select_dynamic-update-slice_fusion.1
  114.4 0.5 convolution_dynamic-update-slice_fusion
  114.9 22.0 %all_to_all.10 = f32[32,24,256]{2,1,0:T(8,128)} all-to-all(f32[32,24,256]{2,1,0:T(8,128)S(1)} %bitcast.81), channel_id=1, replica_groups=mesh['chip'=8,'core'=2,'half'=2,'z'=16] {'chip','core','half'}, dimensions={0} | all-to-all | bytes 1572864 | tf_op jit(solution)/shard_map/all_to_all | solution.py:57
  136.9 1.2 reduce_sum.9
  138.1 0.0 copy-start.2
  138.1 0.1 broadcast_in_dim.52
  138.2 18.1 %all_to_all.11 = f32[32,24,256]{2,1,0:T(8,128)S(1)} all-to-all(f32[32,24,256]{2,1,0:T(8,128)S(1)} %broadcast_in_dim.52), channel_id=1, replica_groups=mesh['chip'=8,'core'=2,'half'=2,'z'=16] {'chip','core','half'}, dimensions={0} | all-to-all | bytes 1572864 | tf_op jit(solution)/shard_map/all_to_all | solution.py:59
  156.3 0.0 copy-done.2
  156.3 0.4 convolution_convert_fusion.1
  156.7 0.3 convolution_subtract_fusion
  157.0 0.4 convolution_convert_fusion
  157.4 0.4 convolution_multiply_fusion
  157.9 0.4 convolution_multiply_fusion.2
  158.3 0.4 subtract_convert_fusion.1
  158.8 0.7 collective-permute-start.4
  159.5 0.4 subtract_convert_fusion
  159.9 2.4 %collective-permute-start.5 = (bf16[2048,128]{1,0:T(8,128)(2,1)S(1)}, bf16[2048,128]{1,0:T(8,128)(2,1)S(1)}, u32[]{:S(2)}, u32[]{:S(2)}) collective-permute-start(bf16[2048,128]{1,0:T(8,128)(2,1)S(1)} %subtract_convert_fusion), channel_id=1, source_target_pairs={{0,16},{1,49},{2,18},{3,51},{4,20},{5,53},{6,22},{7,55},{8,24},{9,... | collective-permute-start | bytes 1572872 | tf_op jit(solution)/shard_map/ppermute | solution.py:30
  162.4 0.0 collective-permute-done.4
  162.4 0.1 pad_maximum_fusion
  162.5 13.6 %collective-permute-done.5 = bf16[2048,128]{1,0:T(8,128)(2,1)S(1)} collective-permute-done((bf16[2048,128]{1,0:T(8,128)(2,1)S(1)}, bf16[2048,128]{1,0:T(8,128)(2,1)S(1)}, u32[]{:S(2)}, u32[]{:S(2)}) %collective-permute-start.5) | collective-permute-done | bytes 524320 | tf_op jit(solution)/shard_map/ppermute | solution.py:30
  176.1 0.1 bitcast_dynamic-update-slice_fusion
  176.1 0.0 copy-start
  176.2 1.0 copy-done
  (3 shorter events, 0.1 us)
Async XLA Ops:
  0.0 10.0 %copy-start.1 = (bf16[4096,128]{1,0:T(8,128)(2,1)S(1)}, bf16[4096,128]{1,0:T(8,128)(2,1)}, u32[]{:S(2)}) copy-start(bf16[4096,128]{1,0:T(8,128)(2,1)} %param.4) | copy-start | bytes 3145732
  2.7 11.9 %copy-start.3 = (s32[32]{0:T(128)S(1)}, s32[32]{0:T(128)}, u32[]{:S(2)}) copy-start(s32[32]{0:T(128)} %param.7) | copy-start | bytes 388
  2.7 25.3 %collective-permute-start.1 = (bf16[2048,256]{1,0:T(8,128)(2,1)}, bf16[2048,256]{1,0:T(8,128)(2,1)S(1)}, u32[]{:S(2)}, u32[]{:S(2)}) collective-permute-start(bf16[2048,256]{1,0:T(8,128)(2,1)} %get-tuple-element.5), channel_id=1, source_target_pairs={{0,16},{1,49},{2,18},{3,51},{4,20},{5,53},{6,22},{7,55},{8,24},{9,... | collective-permute-start | bytes 3145736 | tf_op jit(solution)/shard_map/ppermute | solution.py:30
  8.3 19.7 %collective-permute-start.2 = (bf16[2048,256]{1,0:T(8,128)(2,1)S(1)}, bf16[2048,256]{1,0:T(8,128)(2,1)}, u32[]{:S(2)}, u32[]{:S(2)}) collective-permute-start(bf16[2048,256]{1,0:T(8,128)(2,1)S(1)} %get-tuple-element.6), channel_id=1, source_target_pairs={{0,0},{1,33},{2,2},{3,35},{4,4},{5,37},{6,6},{7,39},{8,8},{9,41},{... | collective-permute-start | bytes 3145736 | tf_op jit(solution)/shard_map/ppermute | solution.py:30
  11.0 101.9 %collective-permute-start.3 = (bf16[2048,128]{1,0:T(8,128)(2,1)}, bf16[2048,128]{1,0:T(8,128)(2,1)S(1)}, u32[]{:S(2)}, u32[]{:S(2)}) collective-permute-start(bf16[2048,128]{1,0:T(8,128)(2,1)} %get-tuple-element.7), channel_id=1, source_target_pairs={{0,16},{1,49},{2,18},{3,51},{4,20},{5,53},{6,22},{7,55},{8,24},{9,... | collective-permute-start | bytes 1572872 | tf_op jit(solution)/shard_map/ppermute | solution.py:30
  13.0 100.3 %collective-permute-start = (bf16[2048,128]{1,0:T(8,128)(2,1)}, bf16[2048,128]{1,0:T(8,128)(2,1)S(1)}, u32[]{:S(2)}, u32[]{:S(2)}) collective-permute-start(bf16[2048,128]{1,0:T(8,128)(2,1)} %get-tuple-element.8), channel_id=1, source_target_pairs={{0,0},{1,33},{2,2},{3,35},{4,4},{5,37},{6,6},{7,39},{8,8},{9,41},{... | collective-permute-start | bytes 1572872 | tf_op jit(solution)/shard_map/ppermute | solution.py:30
  138.1 18.2 %copy-start.2 = (f32[2,256,256]{2,1,0:T(8,128)S(1)}, f32[2,256,256]{2,1,0:T(8,128)}, u32[]{:S(2)}) copy-start(f32[2,256,256]{2,1,0:T(8,128)} %param.6) | copy-start | bytes 1572868
  158.8 3.6 %collective-permute-start.4 = (bf16[2048,128]{1,0:T(8,128)(2,1)S(1)}, bf16[2048,128]{1,0:T(8,128)(2,1)S(1)}, u32[]{:S(2)}, u32[]{:S(2)}) collective-permute-start(bf16[2048,128]{1,0:T(8,128)(2,1)S(1)} %subtract_convert_fusion.1), channel_id=1, source_target_pairs={{0,0},{1,33},{2,2},{3,35},{4,4},{5,37},{6,6},{7,39},{8,8},{9,41},{... | collective-permute-start | bytes 1572872 | tf_op jit(solution)/shard_map/ppermute | solution.py:30
  159.9 16.1 %collective-permute-start.5 = (bf16[2048,128]{1,0:T(8,128)(2,1)S(1)}, bf16[2048,128]{1,0:T(8,128)(2,1)S(1)}, u32[]{:S(2)}, u32[]{:S(2)}) collective-permute-start(bf16[2048,128]{1,0:T(8,128)(2,1)S(1)} %subtract_convert_fusion), channel_id=1, source_target_pairs={{0,16},{1,49},{2,18},{3,51},{4,20},{5,53},{6,22},{7,55},{8,24},{9,... | collective-permute-start | bytes 1572872 | tf_op jit(solution)/shard_map/ppermute | solution.py:30
  176.1 1.0 copy-start

commit v21 on v18

--- a/solution.py
+++ b/solution.py
@@ -78,11 +78,9 @@
     coeffs = [part.reshape(HALVES, columns, part.shape[1]) for part in (lead, tail)]
 
     def updated(tile, which):
-        total = tile.astype(jnp.float32)
-        for p in range(2):
-            part = lax.dynamic_index_in_dim(coeffs[p], which, 0, False)
-            total = total - contract(panels[p], part, ((1,), (1,))) * (1 / SCALE)
-        return total.astype(jnp.bfloat16)
+        part = jnp.stack([lax.dynamic_index_in_dim(c, which, 0, False) for c in coeffs])
+        update = contract(whole.astype(jnp.bfloat16), part, ((0, 2), (0, 2)))
+        return (tile.astype(jnp.float32) - update * (1 / SCALE)).astype(jnp.bfloat16)
 
     got = swap(updated(theirs, 1 - half))
     kept = updated(mine, half)

time: 176 us -> 175 us (level)
    dot_general x9 -> x7, matrix products: 3.64 us -> 3.29 us  [contract(): lax.dot_general(left, right, (dims, ((), ())), preferred_element_type=jnp...]
  transfers between devices with their start and end apart: 4 -> 4, of which waited for: 3 -> 3; matrix products, arithmetic and copies ran while one was open for 3% -> 2% of each run, Pallas kernels for 0% -> 0%
where the time goes in v21:
time: 175 us; the launch traced here: 174 us
  blocking collectives  106 us (61%)
  waiting for transfers between devices  28.3 us (16%)
  starting transfers between devices  27.7 us (16%)
  local copies, waits for them, and re-layouts  4.76 us (3%)
  matrix products  4.44 us (3%)
  other arithmetic  2.51 us (1%)
    psum x1, blocking collectives, spread_panels(): return lax.psum(scaled, 'z')  73.4 us
    ppermute x4, waiting for transfers between devices, swap(): return lax.ppermute(block, axis, [(0, 1), (1, 0)])  28.3 us
    ppermute x4, starting transfers between devices, swap(): return lax.ppermute(block, axis, [(0, 1), (1, 0)])  27.7 us
    all_to_all x1, blocking collectives, sum_over_rows(): share = jnp.sum(lax.all_to_all(cut, axes, 0, 0), axis=0)  16.6 us
    all_to_all x1, blocking collectives, sum_over_rows(): return lax.all_to_all(spread, axes, 0, 0).reshape(part.shape)  16.2 us
  transfers between devices with their start and end apart: 4, of which 3 were waited for; matrix products, arithmetic and copies ran while one was open for 2% of the time, Pallas kernels for 0%

profile of v21, /device:TPU:1, one launch (start us, length us, event | category | flops | bytes accessed | tf_op | source)
XLA Modules:
  0.0 174.3 jit_solution(9955761088864368914)
XLA Ops:
  0.0 0.0 copy-start.3
  0.0 2.7 %dynamic-slice_bitcast_fusion.1 = (bf16[2048,256]{1,0:T(8,128)(2,1)S(1)}, bf16[2048,256]{1,0:T(8,128)(2,1)}) fusion(bf16[2,2048,256]{2,1,0:T(8,128)(2,1)} %bitcast.73, s32[]{:T(128)S(6)} %select_n.59, s32[]{:T(128)S(6)} %select_n.62), kind=kLoop, calls=%fused_computation.21 | loop fusion | bytes 4194312 | tf_op jit(solution)/shard_map/jit(_where)/broadcast_in_dim | solution.py:26
  2.7 0.0 copy-start.5
  2.7 5.6 %collective-permute-start = (bf16[2048,256]{1,0:T(8,128)(2,1)}, bf16[2048,256]{1,0:T(8,128)(2,1)S(1)}, u32[]{:S(2)}, u32[]{:S(2)}) collective-permute-start(bf16[2048,256]{1,0:T(8,128)(2,1)} %get-tuple-element.10), channel_id=1, source_target_pairs={{0,16},{16,0},{1,17},{17,1},{2,18},{18,2},{3,19},{19,3},{4,20},{20... | collective-permute-start | bytes 3145736 | tf_op jit(solution)/shard_map/ppermute | solution.py:12
  8.3 0.0 copy-done.3
  8.4 0.9 dynamic-slice_bitcast_fusion.2
  9.2 1.9 %collective-permute-start.1 = (bf16[2048,128]{1,0:T(8,128)(2,1)}, bf16[2048,128]{1,0:T(8,128)(2,1)S(1)}, u32[]{:S(2)}, u32[]{:S(2)}) collective-permute-start(bf16[2048,128]{1,0:T(8,128)(2,1)} %get-tuple-element.11), channel_id=1, source_target_pairs={{0,16},{16,0},{1,17},{17,1},{2,18},{18,2},{3,19},{19,3},{4,20},{20... | collective-permute-start | bytes 1572872 | tf_op jit(solution)/shard_map/ppermute | solution.py:12
  11.2 0.0 copy-done.5
  11.2 16.9 %collective-permute-done = bf16[2048,256]{1,0:T(8,128)(2,1)S(1)} collective-permute-done((bf16[2048,256]{1,0:T(8,128)(2,1)}, bf16[2048,256]{1,0:T(8,128)(2,1)S(1)}, u32[]{:S(2)}, u32[]{:S(2)}) %collective-permute-start) | collective-permute-done | bytes 1048608 | tf_op jit(solution)/shard_map/ppermute | solution.py:12
  28.1 2.3 %multiply_convert_fusion = f16[2,2048,256]{2,1,0:T(8,128)(2,1)} fusion(pred[2]{0:T(512)(128)(4,1)S(1)} %get-tuple-element.18, pred[2]{0:T(512)(128)(4,1)S(1)} %get-tuple-element.17, bf16[2048,256]{1,0:T(8,128)(2,1)S(1)} %collective-permute-done, bf16[2048,256]{1,0:T(8,128)(2,1)S(1)} %get-tuple-element.9), kind=kLoop, calls=%fused_computation | loop fusion | flops 5242880 | bytes 4194308 | tf_op jit(solution)/shard_map/convert_element_type | solution.py:28
  30.4 73.4 %all-reduce.1 = u32[2,4,65536]{2,1,0:T(4,128)S(1)} all-reduce(u32[2,4,65536]{2,1,0:T(4,128)} %bitcast.70), channel_id=1, replica_groups=mesh['chip'=8,'core'=2,'half'=2,'z'=16] {'z'}, use_global_device_ids=true, to_apply=%region_0.1.clone | all-reduce | flops 524288 | bytes 4194304 | tf_op jit(solution)/shard_map/psum | solution.py:29
  103.8 0.0 collective-permute-done.1
  103.8 0.0 copy-start
  103.8 0.3 fusion.10
  104.2 0.3 select_dynamic-update-slice_fusion.3
  104.5 0.3 fusion.15
  104.9 0.0 copy-done
  104.9 0.3 select_dynamic-update-slice_fusion.1
  105.3 0.5 convolution_dynamic-update-slice_fusion
  105.8 16.6 %all_to_all.10 = f32[16,48,256]{2,1,0:T(8,128)S(1)} all-to-all(f32[16,48,256]{2,1,0:T(8,128)S(1)} %bitcast.75), channel_id=1, replica_groups=mesh['chip'=8,'core'=2,'half'=2,'z'=16] {'chip','half'}, dimensions={0} | all-to-all | bytes 1572864 | tf_op jit(solution)/shard_map/all_to_all | solution.py:40
  122.4 0.1 reduce_sum.9
  122.5 0.0 copy-start.4
  122.5 16.8 %collective-permute-start.2 = (f32[48,256]{1,0:T(8,128)S(1)}, f32[48,256]{1,0:T(8,128)S(1)}, u32[]{:S(2)}, u32[]{:S(2)}) collective-permute-start(f32[48,256]{1,0:T(8,128)S(1)} %reduce_sum.9), channel_id=1, source_target_pairs={{0,32},{32,0},{1,33},{33,1},{2,34},{34,2},{3,35},{35,3},{4,36},{36... | collective-permute-start | bytes 147464 | tf_op jit(solution)/shard_map/ppermute | solution.py:12
  139.3 0.9 collective-permute-done.2
  140.2 0.1 broadcast_in_dim.55
  140.2 0.0 copy-start.1
  140.2 16.2 %all_to_all.11 = f32[16,48,256]{2,1,0:T(8,128)S(1)} all-to-all(f32[16,48,256]{2,1,0:T(8,128)S(1)} %broadcast_in_dim.55), channel_id=1, replica_groups=mesh['chip'=8,'core'=2,'half'=2,'z'=16] {'chip','half'}, dimensions={0} | all-to-all | bytes 1572864 | tf_op jit(solution)/shard_map/all_to_all | solution.py:43
  156.4 0.0 copy-done.4
  156.4 0.4 convolution_convert_fusion.1
  156.9 0.3 convolution_subtract_fusion
  157.2 0.4 convolution_convert_fusion
  157.6 0.0 copy-done.1
  157.7 0.7 subtract_convert_fusion
  158.4 3.4 %collective-permute-start.3 = (bf16[2048,128]{1,0:T(8,128)(2,1)S(1)}, bf16[2048,128]{1,0:T(8,128)(2,1)S(1)}, u32[]{:S(2)}, u32[]{:S(2)}) collective-permute-start(bf16[2048,128]{1,0:T(8,128)(2,1)S(1)} %subtract_convert_fusion), channel_id=1, source_target_pairs={{0,16},{16,0},{1,17},{17,1},{2,18},{18,2},{3,19},{19,3},{4,20},{20... | collective-permute-start | bytes 1572872 | tf_op jit(solution)/shard_map/ppermute | solution.py:12
  161.8 0.7 fusion.4
  162.5 0.1 pad_maximum_fusion
  162.6 10.6 %collective-permute-done.3 = bf16[2048,128]{1,0:T(8,128)(2,1)S(1)} collective-permute-done((bf16[2048,128]{1,0:T(8,128)(2,1)S(1)}, bf16[2048,128]{1,0:T(8,128)(2,1)S(1)}, u32[]{:S(2)}, u32[]{:S(2)}) %collective-permute-start.3) | collective-permute-done | bytes 524320 | tf_op jit(solution)/shard_map/ppermute | solution.py:12
  173.2 0.1 bitcast_dynamic-update-slice_fusion
  173.3 0.0 copy-start.2
  173.3 1.0 copy-done.2
  (5 shorter events, 0.1 us)
Async XLA Ops:
  0.0 8.3 %copy-start.3 = (bf16[4096,128]{1,0:T(8,128)(2,1)S(1)}, bf16[4096,128]{1,0:T(8,128)(2,1)}, u32[]{:S(2)}) copy-start(bf16[4096,128]{1,0:T(8,128)(2,1)} %param.4) | copy-start | bytes 3145732
  2.7 8.4 %copy-start.5 = (s32[32]{0:T(128)S(1)}, s32[32]{0:T(128)}, u32[]{:S(2)}) copy-start(s32[32]{0:T(128)} %param.7) | copy-start | bytes 388
  2.7 25.3 %collective-permute-start = (bf16[2048,256]{1,0:T(8,128)(2,1)}, bf16[2048,256]{1,0:T(8,128)(2,1)S(1)}, u32[]{:S(2)}, u32[]{:S(2)}) collective-permute-start(bf16[2048,256]{1,0:T(8,128)(2,1)} %get-tuple-element.10), channel_id=1, source_target_pairs={{0,16},{16,0},{1,17},{17,1},{2,18},{18,2},{3,19},{19,3},{4,20},{20... | collective-permute-start | bytes 3145736 | tf_op jit(solution)/shard_map/ppermute | solution.py:12
  9.2 94.6 %collective-permute-start.1 = (bf16[2048,128]{1,0:T(8,128)(2,1)}, bf16[2048,128]{1,0:T(8,128)(2,1)S(1)}, u32[]{:S(2)}, u32[]{:S(2)}) collective-permute-start(bf16[2048,128]{1,0:T(8,128)(2,1)} %get-tuple-element.11), channel_id=1, source_target_pairs={{0,16},{16,0},{1,17},{17,1},{2,18},{18,2},{3,19},{19,3},{4,20},{20... | collective-permute-start | bytes 1572872 | tf_op jit(solution)/shard_map/ppermute | solution.py:12
  103.8 1.1 copy-start
  122.5 34.0 %copy-start.4 = (f32[2,256,256]{2,1,0:T(8,128)S(1)}, f32[2,256,256]{2,1,0:T(8,128)}, u32[]{:S(2)}) copy-start(f32[2,256,256]{2,1,0:T(8,128)} %param.6) | copy-start | bytes 1572868
  122.5 17.7 %collective-permute-start.2 = (f32[48,256]{1,0:T(8,128)S(1)}, f32[48,256]{1,0:T(8,128)S(1)}, u32[]{:S(2)}, u32[]{:S(2)}) collective-permute-start(f32[48,256]{1,0:T(8,128)S(1)} %reduce_sum.9), channel_id=1, source_target_pairs={{0,32},{32,0},{1,33},{33,1},{2,34},{34,2},{3,35},{35,3},{4,36},{36... | collective-permute-start | bytes 147464 | tf_op jit(solution)/shard_map/ppermute | solution.py:12
  140.2 17.4 %copy-start.1 = (bf16[2048,128]{1,0:T(8,128)(2,1)S(1)}, bf16[2048,128]{1,0:T(8,128)(2,1)}, u32[]{:S(2)}) copy-start(bf16[2048,128]{1,0:T(8,128)(2,1)} %copy-done) | copy-start | bytes 1572868
  158.4 14.8 %collective-permute-start.3 = (bf16[2048,128]{1,0:T(8,128)(2,1)S(1)}, bf16[2048,128]{1,0:T(8,128)(2,1)S(1)}, u32[]{:S(2)}, u32[]{:S(2)}) collective-permute-start(bf16[2048,128]{1,0:T(8,128)(2,1)S(1)} %subtract_convert_fusion), channel_id=1, source_target_pairs={{0,16},{16,0},{1,17},{17,1},{2,18},{18,2},{3,19},{19,3},{4,20},{20... | collective-permute-start | bytes 1572872 | tf_op jit(solution)/shard_map/ppermute | solution.py:12
  173.3 1.0 copy-start.2

commit v22 on v21

--- a/solution.py
+++ b/solution.py
@@ -61,11 +61,11 @@
     whole = spread_panels(own, other, owners, half)
     panels = [whole[p].astype(jnp.bfloat16) for p in range(2)]
 
+    here = contract(whole.astype(jnp.bfloat16), early, ((1,), (0,)))
+    there = contract(whole.astype(jnp.bfloat16), theirs, ((1,), (0,)))
     blocks = []
     for p in range(2):
-        here = contract(early, panels[p], ((0,), (0,)))
-        there = contract(theirs, panels[p], ((0,), (0,)))
-        blocks += [jnp.where(half == 0, here, there), jnp.where(half == 0, there, here)]
+        blocks += [jnp.where(half == 0, here[p].T, there[p].T), jnp.where(half == 0, there[p].T, here[p].T)]
     cross = contract(panels[1], panels[0], ((0,), (0,)))
     summed = sum_over_rows(jnp.concatenate(blocks + [cross], axis=0))
     count = HALVES * columns

time: 175 us -> 179 us (1.023)
  matrix products: 4.44 us -> 6.26 us
    dot_general x7 -> x5, matrix products: 3.29 us -> 5.11 us  [contract(): lax.dot_general(left, right, (dims, ((), ())), preferred_element_type=jnp...]
  transfers between devices with their start and end apart: 4 -> 4, of which waited for: 3 -> 3; matrix products, arithmetic and copies ran while one was open for 2% -> 3% of each run, Pallas kernels for 0% -> 0%
where the time goes in v22:
time: 179 us; the launch traced here: 178 us
  blocking collectives  106 us (59%)
  waiting for transfers between devices  28.5 us (16%)
  starting transfers between devices  28.3 us (16%)
  matrix products  6.26 us (3%)
  local copies, waits for them, and re-layouts  4.7 us (3%)
  other arithmetic  3.78 us (2%)
    psum x1, blocking collectives, spread_panels(): return lax.psum(scaled, 'z')  73.7 us
    ppermute x4, waiting for transfers between devices, swap(): return lax.ppermute(block, axis, [(0, 1), (1, 0)])  28.5 us
    ppermute x4, starting transfers between devices, swap(): return lax.ppermute(block, axis, [(0, 1), (1, 0)])  28.3 us
    all_to_all x1, blocking collectives, sum_over_rows(): share = jnp.sum(lax.all_to_all(cut, axes, 0, 0), axis=0)  16.6 us
    all_to_all x1, blocking collectives, sum_over_rows(): return lax.all_to_all(spread, axes, 0, 0).reshape(part.shape)  16.1 us
    dot_general x5, matrix products, contract(): lax.dot_general(left, right, (dims, ((), ())), preferred_element_type=jnp...  5.11 us
  transfers between devices with their start and end apart: 4, of which 3 were waited for; matrix products, arithmetic and copies ran while one was open for 3% of the time, Pallas kernels for 0%

profile of v22, /device:TPU:1, one launch (start us, length us, event | category | flops | bytes accessed | tf_op | source)
XLA Modules:
  0.0 178.2 jit_solution(17130976403876408140)
XLA Ops:
  0.0 0.0 copy-start
  0.0 2.7 %dynamic-slice_bitcast_fusion.1 = (bf16[2048,256]{1,0:T(8,128)(2,1)S(1)}, bf16[2048,256]{1,0:T(8,128)(2,1)}) fusion(bf16[2,2048,256]{2,1,0:T(8,128)(2,1)} %bitcast.81, s32[]{:T(128)S(6)} %select_n.83, s32[]{:T(128)S(6)} %select_n.86), kind=kLoop, calls=%fused_computation.25 | loop fusion | bytes 4194312 | tf_op jit(solution)/shard_map/jit(_where)/broadcast_in_dim | solution.py:26
  2.7 5.5 %collective-permute-start = (bf16[2048,256]{1,0:T(8,128)(2,1)}, bf16[2048,256]{1,0:T(8,128)(2,1)}, u32[]{:S(2)}, u32[]{:S(2)}) collective-permute-start(bf16[2048,256]{1,0:T(8,128)(2,1)} %get-tuple-element.10), channel_id=1, source_target_pairs={{0,16},{16,0},{1,17},{17,1},{2,18},{18,2},{3,19},{19,3},{4,20},{20... | collective-permute-start | bytes 3145736 | tf_op jit(solution)/shard_map/ppermute | solution.py:12
  8.2 0.0 copy-done
  8.2 0.0 copy-start.2
  8.2 0.1 constant_dynamic-slice_fusion.4
  8.3 0.2 copy.19
  8.5 1.9 %collective-permute-start.1 = (bf16[2048,128]{0,1:T(8,128)(2,1)S(1)}, bf16[2048,128]{0,1:T(8,128)(2,1)}, u32[]{:S(2)}, u32[]{:S(2)}) collective-permute-start(bf16[2048,128]{0,1:T(8,128)(2,1)S(1)} %bitcast.85), channel_id=1, source_target_pairs={{0,16},{16,0},{1,17},{17,1},{2,18},{18,2},{3,19},{19,3},{4,20},{20... | collective-permute-start | bytes 1572872 | tf_op jit(solution)/shard_map/ppermute | solution.py:12
  10.5 0.2 copy.18
  10.7 0.0 copy-done.2
  10.7 17.2 %collective-permute-done = bf16[2048,256]{1,0:T(8,128)(2,1)} collective-permute-done((bf16[2048,256]{1,0:T(8,128)(2,1)}, bf16[2048,256]{1,0:T(8,128)(2,1)}, u32[]{:S(2)}, u32[]{:S(2)}) %collective-permute-start) | collective-permute-done | bytes 1048608 | tf_op jit(solution)/shard_map/ppermute | solution.py:12
  27.9 3.5 %multiply_convert_fusion = f16[2,2048,256]{2,1,0:T(8,128)(2,1)} fusion(pred[2]{0:T(512)(128)(4,1)S(1)} %get-tuple-element.18, pred[2]{0:T(512)(128)(4,1)S(1)} %get-tuple-element.17, bf16[2048,256]{1,0:T(8,128)(2,1)} %collective-permute-done, bf16[2048,256]{1,0:T(8,128)(2,1)S(1)} %get-tuple-element.9), kind=kLoop, calls=%fused_computation | loop fusion | flops 5242880 | bytes 4194308 | tf_op jit(solution)/shard_map/convert_element_type | solution.py:28
  31.5 73.7 %all-reduce.1 = u32[2,4,65536]{2,1,0:T(4,128)S(1)} all-reduce(u32[2,4,65536]{2,1,0:T(4,128)} %bitcast.77), channel_id=1, replica_groups=mesh['chip'=8,'core'=2,'half'=2,'z'=16] {'z'}, use_global_device_ids=true, to_apply=%region_0.1.clone | all-reduce | flops 524288 | bytes 4194304 | tf_op jit(solution)/shard_map/psum | solution.py:29
  105.2 0.4 fusion.7
  105.6 0.0 collective-permute-done.1
  105.7 1.5 fusion.9
  107.2 0.5 convolution_dynamic-update-slice_fusion
  107.7 16.6 %all_to_all.10 = f32[16,48,256]{2,1,0:T(8,128)S(1)} all-to-all(f32[16,48,256]{2,1,0:T(8,128)S(1)} %bitcast.83), channel_id=1, replica_groups=mesh['chip'=8,'core'=2,'half'=2,'z'=16] {'chip','half'}, dimensions={0} | all-to-all | bytes 1572864 | tf_op jit(solution)/shard_map/all_to_all | solution.py:40
  124.4 0.1 reduce_sum.9
  124.4 0.0 copy-start.1
  124.4 17.5 %collective-permute-start.2 = (f32[48,256]{1,0:T(8,128)S(1)}, f32[48,256]{1,0:T(8,128)S(1)}, u32[]{:S(2)}, u32[]{:S(2)}) collective-permute-start(f32[48,256]{1,0:T(8,128)S(1)} %reduce_sum.9), channel_id=1, source_target_pairs={{0,32},{32,0},{1,33},{33,1},{2,34},{34,2},{3,35},{35,3},{4,36},{36... | collective-permute-start | bytes 147464 | tf_op jit(solution)/shard_map/ppermute | solution.py:12
  141.9 0.9 collective-permute-done.2
  142.8 0.1 broadcast_in_dim.55
  142.8 16.1 %all_to_all.11 = f32[16,48,256]{2,1,0:T(8,128)S(1)} all-to-all(f32[16,48,256]{2,1,0:T(8,128)S(1)} %broadcast_in_dim.55), channel_id=1, replica_groups=mesh['chip'=8,'core'=2,'half'=2,'z'=16] {'chip','half'}, dimensions={0} | all-to-all | bytes 1572864 | tf_op jit(solution)/shard_map/all_to_all | solution.py:43
  158.9 0.0 copy-done.1
  158.9 0.4 convolution_convert_fusion.1
  159.3 0.3 convolution_subtract_fusion
  159.7 0.4 convolution_convert_fusion
  160.1 1.9 %subtract_convert_fusion = bf16[2048,128]{0,1:T(8,128)(2,1)S(1)} fusion(bf16[2048,128]{0,1:T(8,128)(2,1)} %collective-permute-done.1, f16[2,2048,256]{2,1,0:T(8,128)(2,1)S(1)} %bitcast.75, bf16[1,128,256]{2,1,0:T(8,128)(2,1)S(1)} %get-tuple-element.15, bf16[1,128,256]{2,1,0:T(8,128)(2,1)S(1)} %get-tuple-element.20), kind=kOutput, calls=%fused_computation.23 | convolution fusion | flops 270598144 | bytes 3276800 | tf_op jit(solution)/shard_map/dot_general | solution.py:33
  162.0 3.4 %collective-permute-start.3 = (bf16[2048,128]{0,1:T(8,128)(2,1)S(1)}, bf16[2048,128]{0,1:T(8,128)(2,1)S(1)}, u32[]{:S(2)}, u32[]{:S(2)}) collective-permute-start(bf16[2048,128]{0,1:T(8,128)(2,1)S(1)} %subtract_convert_fusion), channel_id=1, source_target_pairs={{0,16},{16,0},{1,17},{17,1},{2,18},{18,2},{3,19},{19,3},{4,20},{20... | collective-permute-start | bytes 1572872 | tf_op jit(solution)/shard_map/ppermute | solution.py:12
  165.4 0.8 fusion.4
  166.3 0.1 pad_maximum_fusion
  166.4 10.5 %collective-permute-done.3 = bf16[2048,128]{0,1:T(8,128)(2,1)S(1)} collective-permute-done((bf16[2048,128]{0,1:T(8,128)(2,1)S(1)}, bf16[2048,128]{0,1:T(8,128)(2,1)S(1)}, u32[]{:S(2)}, u32[]{:S(2)}) %collective-permute-start.3) | collective-permute-done | bytes 524320 | tf_op jit(solution)/shard_map/ppermute | solution.py:12
  176.9 1.3 copy.13
  (8 shorter events, 0.2 us)
Async XLA Ops:
  0.0 8.2 %copy-start = (bf16[4096,128]{1,0:T(8,128)(2,1)S(1)}, bf16[4096,128]{1,0:T(8,128)(2,1)}, u32[]{:S(2)}) copy-start(bf16[4096,128]{1,0:T(8,128)(2,1)} %param.4) | copy-start | bytes 3145732
  2.7 25.2 %collective-permute-start = (bf16[2048,256]{1,0:T(8,128)(2,1)}, bf16[2048,256]{1,0:T(8,128)(2,1)}, u32[]{:S(2)}, u32[]{:S(2)}) collective-permute-start(bf16[2048,256]{1,0:T(8,128)(2,1)} %get-tuple-element.10), channel_id=1, source_target_pairs={{0,16},{16,0},{1,17},{17,1},{2,18},{18,2},{3,19},{19,3},{4,20},{20... | collective-permute-start | bytes 3145736 | tf_op jit(solution)/shard_map/ppermute | solution.py:12
  8.2 2.5 %copy-start.2 = (s32[32]{0:T(128)S(1)}, s32[32]{0:T(128)}, u32[]{:S(2)}) copy-start(s32[32]{0:T(128)} %param.7) | copy-start | bytes 388
  8.5 97.1 %collective-permute-start.1 = (bf16[2048,128]{0,1:T(8,128)(2,1)S(1)}, bf16[2048,128]{0,1:T(8,128)(2,1)}, u32[]{:S(2)}, u32[]{:S(2)}) collective-permute-start(bf16[2048,128]{0,1:T(8,128)(2,1)S(1)} %bitcast.85), channel_id=1, source_target_pairs={{0,16},{16,0},{1,17},{17,1},{2,18},{18,2},{3,19},{19,3},{4,20},{20... | collective-permute-start | bytes 1572872 | tf_op jit(solution)/shard_map/ppermute | solution.py:12
  124.4 34.5 %copy-start.1 = (f32[2,256,256]{2,1,0:T(8,128)S(1)}, f32[2,256,256]{2,1,0:T(8,128)}, u32[]{:S(2)}) copy-start(f32[2,256,256]{2,1,0:T(8,128)} %param.6) | copy-start | bytes 1572868
  124.4 18.3 %collective-permute-start.2 = (f32[48,256]{1,0:T(8,128)S(1)}, f32[48,256]{1,0:T(8,128)S(1)}, u32[]{:S(2)}, u32[]{:S(2)}) collective-permute-start(f32[48,256]{1,0:T(8,128)S(1)} %reduce_sum.9), channel_id=1, source_target_pairs={{0,32},{32,0},{1,33},{33,1},{2,34},{34,2},{3,35},{35,3},{4,36},{36... | collective-permute-start | bytes 147464 | tf_op jit(solution)/shard_map/ppermute | solution.py:12
  162.0 14.8 %collective-permute-start.3 = (bf16[2048,128]{0,1:T(8,128)(2,1)S(1)}, bf16[2048,128]{0,1:T(8,128)(2,1)S(1)}, u32[]{:S(2)}, u32[]{:S(2)}) collective-permute-start(bf16[2048,128]{0,1:T(8,128)(2,1)S(1)} %subtract_convert_fusion), channel_id=1, source_target_pairs={{0,16},{16,0},{1,17},{17,1},{2,18},{18,2},{3,19},{19,3},{4,20},{20... | collective-permute-start | bytes 1572872 | tf_op jit(solution)/shard_map/ppermute | solution.py:12

commit v23 on v21

--- a/solution.py
+++ b/solution.py
@@ -23,7 +23,7 @@
 
 def spread_panels(own, other, owners, half):
     slot = owners[:2].reshape(2, 1, 1)
-    block = jnp.where(slot // RING == half, own[None], other[None])
+    block = jnp.where(slot // RING != half, other[None], own[None])
     sent = jnp.where(slot % RING == lax.axis_index("z"), block, jnp.zeros_like(block))
     scaled = (sent.astype(jnp.float32) * SCALE).astype(jnp.float16)
     return lax.psum(scaled, "z")

time: 175 us -> 175 us (level)
    broadcast_in_dim x1 -> x0, local copies, waits for them, and re-layouts: 2.73 us -> none  [spread_panels(): block = jnp.where(slot // RING == half, own[None], other[None])]
    squeeze x1 -> x2, local copies, waits for them, and re-layouts: 0.87 us -> 3.61 us  [parts_of(): lax.dynamic_index_in_dim(halves, 1 - half, 0, False)]
where the time goes in v23:
time: 175 us; the launch traced here: 174 us
  blocking collectives  106 us (61%)
  waiting for transfers between devices  28.3 us (16%)
  starting transfers between devices  27.7 us (16%)
  local copies, waits for them, and re-layouts  4.76 us (3%)
  matrix products  4.44 us (3%)
  other arithmetic  2.51 us (1%)
    psum x1, blocking collectives, spread_panels(): return lax.psum(scaled, 'z')  73.4 us
    ppermute x4, waiting for transfers between devices, swap(): return lax.ppermute(block, axis, [(0, 1), (1, 0)])  28.3 us
    ppermute x4, starting transfers between devices, swap(): return lax.ppermute(block, axis, [(0, 1), (1, 0)])  27.7 us
    all_to_all x1, blocking collectives, sum_over_rows(): share = jnp.sum(lax.all_to_all(cut, axes, 0, 0), axis=0)  16.6 us
    all_to_all x1, blocking collectives, sum_over_rows(): return lax.all_to_all(spread, axes, 0, 0).reshape(part.shape)  16.2 us
    squeeze x2, local copies, waits for them, and re-layouts, parts_of(): lax.dynamic_index_in_dim(halves, 1 - half, 0, False)  3.61 us
  transfers between devices with their start and end apart: 4, of which 3 were waited for; matrix products, arithmetic and copies ran while one was open for 2% of the time, Pallas kernels for 0%

profile of v23, /device:TPU:1, one launch (start us, length us, event | category | flops | bytes accessed | tf_op | source)
XLA Modules:
  0.0 174.3 jit_solution(14137158484155901006)
XLA Ops:
  0.0 0.0 copy-start.3
  0.0 2.7 %dynamic-slice_bitcast_fusion.1 = (bf16[2048,256]{1,0:T(8,128)(2,1)}, bf16[2048,256]{1,0:T(8,128)(2,1)S(1)}) fusion(bf16[2,2048,256]{2,1,0:T(8,128)(2,1)} %bitcast.73, s32[]{:T(128)S(6)} %select_n.62, s32[]{:T(128)S(6)} %select_n.59), kind=kLoop, calls=%fused_computation.21 | loop fusion | bytes 4194312 | tf_op jit(solution)/shard_map/jit(dynamic_index_in_dim)/squeeze | solution.py:20
  2.7 0.0 copy-start.5
  2.7 5.6 %collective-permute-start = (bf16[2048,256]{1,0:T(8,128)(2,1)}, bf16[2048,256]{1,0:T(8,128)(2,1)S(1)}, u32[]{:S(2)}, u32[]{:S(2)}) collective-permute-start(bf16[2048,256]{1,0:T(8,128)(2,1)} %get-tuple-element.9), channel_id=1, source_target_pairs={{0,16},{16,0},{1,17},{17,1},{2,18},{18,2},{3,19},{19,3},{4,20},{20... | collective-permute-start | bytes 3145736 | tf_op jit(solution)/shard_map/ppermute | solution.py:12
  8.3 0.0 copy-done.3
  8.4 0.9 dynamic-slice_bitcast_fusion.2
  9.2 1.9 %collective-permute-start.1 = (bf16[2048,128]{1,0:T(8,128)(2,1)}, bf16[2048,128]{1,0:T(8,128)(2,1)S(1)}, u32[]{:S(2)}, u32[]{:S(2)}) collective-permute-start(bf16[2048,128]{1,0:T(8,128)(2,1)} %get-tuple-element.11), channel_id=1, source_target_pairs={{0,16},{16,0},{1,17},{17,1},{2,18},{18,2},{3,19},{19,3},{4,20},{20... | collective-permute-start | bytes 1572872 | tf_op jit(solution)/shard_map/ppermute | solution.py:12
  11.2 0.0 copy-done.5
  11.2 16.9 %collective-permute-done = bf16[2048,256]{1,0:T(8,128)(2,1)S(1)} collective-permute-done((bf16[2048,256]{1,0:T(8,128)(2,1)}, bf16[2048,256]{1,0:T(8,128)(2,1)S(1)}, u32[]{:S(2)}, u32[]{:S(2)}) %collective-permute-start) | collective-permute-done | bytes 1048608 | tf_op jit(solution)/shard_map/ppermute | solution.py:12
  28.1 2.3 %multiply_convert_fusion = f16[2,2048,256]{2,1,0:T(8,128)(2,1)} fusion(pred[2]{0:T(512)(128)(4,1)S(1)} %get-tuple-element.18, pred[2]{0:T(512)(128)(4,1)S(1)} %get-tuple-element.17, bf16[2048,256]{1,0:T(8,128)(2,1)S(1)} %get-tuple-element.10, bf16[2048,256]{1,0:T(8,128)(2,1)S(1)} %collective-permute-done), kind=kLoop, calls=%fused_computation | loop fusion | flops 5242880 | bytes 4194308 | tf_op jit(solution)/shard_map/convert_element_type | solution.py:28
  30.4 73.4 %all-reduce.1 = u32[2,4,65536]{2,1,0:T(4,128)S(1)} all-reduce(u32[2,4,65536]{2,1,0:T(4,128)} %bitcast.70), channel_id=1, replica_groups=mesh['chip'=8,'core'=2,'half'=2,'z'=16] {'z'}, use_global_device_ids=true, to_apply=%region_0.1.clone | all-reduce | flops 524288 | bytes 4194304 | tf_op jit(solution)/shard_map/psum | solution.py:29
  103.8 0.0 collective-permute-done.1
  103.8 0.0 copy-start
  103.8 0.3 fusion.10
  104.2 0.3 select_dynamic-update-slice_fusion.3
  104.5 0.3 fusion.15
  104.9 0.0 copy-done
  104.9 0.3 select_dynamic-update-slice_fusion.1
  105.3 0.5 convolution_dynamic-update-slice_fusion
  105.8 16.6 %all_to_all.10 = f32[16,48,256]{2,1,0:T(8,128)S(1)} all-to-all(f32[16,48,256]{2,1,0:T(8,128)S(1)} %bitcast.75), channel_id=1, replica_groups=mesh['chip'=8,'core'=2,'half'=2,'z'=16] {'chip','half'}, dimensions={0} | all-to-all | bytes 1572864 | tf_op jit(solution)/shard_map/all_to_all | solution.py:40
  122.4 0.1 reduce_sum.9
  122.5 0.0 copy-start.4
  122.5 16.8 %collective-permute-start.2 = (f32[48,256]{1,0:T(8,128)S(1)}, f32[48,256]{1,0:T(8,128)S(1)}, u32[]{:S(2)}, u32[]{:S(2)}) collective-permute-start(f32[48,256]{1,0:T(8,128)S(1)} %reduce_sum.9), channel_id=1, source_target_pairs={{0,32},{32,0},{1,33},{33,1},{2,34},{34,2},{3,35},{35,3},{4,36},{36... | collective-permute-start | bytes 147464 | tf_op jit(solution)/shard_map/ppermute | solution.py:12
  139.3 0.9 collective-permute-done.2
  140.2 0.1 broadcast_in_dim.55
  140.2 0.0 copy-start.1
  140.2 16.2 %all_to_all.11 = f32[16,48,256]{2,1,0:T(8,128)S(1)} all-to-all(f32[16,48,256]{2,1,0:T(8,128)S(1)} %broadcast_in_dim.55), channel_id=1, replica_groups=mesh['chip'=8,'core'=2,'half'=2,'z'=16] {'chip','half'}, dimensions={0} | all-to-all | bytes 1572864 | tf_op jit(solution)/shard_map/all_to_all | solution.py:43
  156.4 0.0 copy-done.4
  156.4 0.4 convolution_convert_fusion.1
  156.9 0.3 convolution_subtract_fusion
  157.2 0.4 convolution_convert_fusion
  157.6 0.0 copy-done.1
  157.7 0.7 subtract_convert_fusion
  158.4 3.4 %collective-permute-start.3 = (bf16[2048,128]{1,0:T(8,128)(2,1)S(1)}, bf16[2048,128]{1,0:T(8,128)(2,1)S(1)}, u32[]{:S(2)}, u32[]{:S(2)}) collective-permute-start(bf16[2048,128]{1,0:T(8,128)(2,1)S(1)} %subtract_convert_fusion), channel_id=1, source_target_pairs={{0,16},{16,0},{1,17},{17,1},{2,18},{18,2},{3,19},{19,3},{4,20},{20... | collective-permute-start | bytes 1572872 | tf_op jit(solution)/shard_map/ppermute | solution.py:12
  161.8 0.7 fusion.4
  162.5 0.1 pad_maximum_fusion
  162.6 10.6 %collective-permute-done.3 = bf16[2048,128]{1,0:T(8,128)(2,1)S(1)} collective-permute-done((bf16[2048,128]{1,0:T(8,128)(2,1)S(1)}, bf16[2048,128]{1,0:T(8,128)(2,1)S(1)}, u32[]{:S(2)}, u32[]{:S(2)}) %collective-permute-start.3) | collective-permute-done | bytes 524320 | tf_op jit(solution)/shard_map/ppermute | solution.py:12
  173.2 0.1 bitcast_dynamic-update-slice_fusion
  173.3 0.0 copy-start.2
  173.3 1.0 copy-done.2
  (5 shorter events, 0.1 us)
Async XLA Ops:
  0.0 8.3 %copy-start.3 = (bf16[4096,128]{1,0:T(8,128)(2,1)S(1)}, bf16[4096,128]{1,0:T(8,128)(2,1)}, u32[]{:S(2)}) copy-start(bf16[4096,128]{1,0:T(8,128)(2,1)} %param.4) | copy-start | bytes 3145732
  2.7 8.4 %copy-start.5 = (s32[32]{0:T(128)S(1)}, s32[32]{0:T(128)}, u32[]{:S(2)}) copy-start(s32[32]{0:T(128)} %param.7) | copy-start | bytes 388
  2.7 25.3 %collective-permute-start = (bf16[2048,256]{1,0:T(8,128)(2,1)}, bf16[2048,256]{1,0:T(8,128)(2,1)S(1)}, u32[]{:S(2)}, u32[]{:S(2)}) collective-permute-start(bf16[2048,256]{1,0:T(8,128)(2,1)} %get-tuple-element.9), channel_id=1, source_target_pairs={{0,16},{16,0},{1,17},{17,1},{2,18},{18,2},{3,19},{19,3},{4,20},{20... | collective-permute-start | bytes 3145736 | tf_op jit(solution)/shard_map/ppermute | solution.py:12
  9.2 94.6 %collective-permute-start.1 = (bf16[2048,128]{1,0:T(8,128)(2,1)}, bf16[2048,128]{1,0:T(8,128)(2,1)S(1)}, u32[]{:S(2)}, u32[]{:S(2)}) collective-permute-start(bf16[2048,128]{1,0:T(8,128)(2,1)} %get-tuple-element.11), channel_id=1, source_target_pairs={{0,16},{16,0},{1,17},{17,1},{2,18},{18,2},{3,19},{19,3},{4,20},{20... | collective-permute-start | bytes 1572872 | tf_op jit(solution)/shard_map/ppermute | solution.py:12
  103.8 1.1 copy-start
  122.5 34.0 %copy-start.4 = (f32[2,256,256]{2,1,0:T(8,128)S(1)}, f32[2,256,256]{2,1,0:T(8,128)}, u32[]{:S(2)}) copy-start(f32[2,256,256]{2,1,0:T(8,128)} %param.6) | copy-start | bytes 1572868
  122.5 17.7 %collective-permute-start.2 = (f32[48,256]{1,0:T(8,128)S(1)}, f32[48,256]{1,0:T(8,128)S(1)}, u32[]{:S(2)}, u32[]{:S(2)}) collective-permute-start(f32[48,256]{1,0:T(8,128)S(1)} %reduce_sum.9), channel_id=1, source_target_pairs={{0,32},{32,0},{1,33},{33,1},{2,34},{34,2},{3,35},{35,3},{4,36},{36... | collective-permute-start | bytes 147464 | tf_op jit(solution)/shard_map/ppermute | solution.py:12
  140.2 17.4 %copy-start.1 = (bf16[2048,128]{1,0:T(8,128)(2,1)S(1)}, bf16[2048,128]{1,0:T(8,128)(2,1)}, u32[]{:S(2)}) copy-start(bf16[2048,128]{1,0:T(8,128)(2,1)} %copy-done) | copy-start | bytes 1572868
  158.4 14.8 %collective-permute-start.3 = (bf16[2048,128]{1,0:T(8,128)(2,1)S(1)}, bf16[2048,128]{1,0:T(8,128)(2,1)S(1)}, u32[]{:S(2)}, u32[]{:S(2)}) collective-permute-start(bf16[2048,128]{1,0:T(8,128)(2,1)S(1)} %subtract_convert_fusion), channel_id=1, source_target_pairs={{0,16},{16,0},{1,17},{17,1},{2,18},{18,2},{3,19},{19,3},{4,20},{20... | collective-permute-start | bytes 1572872 | tf_op jit(solution)/shard_map/ppermute | solution.py:12
  173.3 1.0 copy-start.2
